TPU v7x, 32 devices: a whole 2x2x4 slice. The times are simulated.
32 devices in a mesh: tm: 8 (over z, x), head: 4 (over y, core).
Axes of the slice: x: 2, y: 2, z: 4, core: 2. Of those that a mesh axis runs over, the one named last changes fastest.
Arguments:
- frames: float32 [2, 4096, 512], P(None, 'tm'), may hold values from -6 to 6
- cotangent: float32 [2, 4096, 512], P(None, 'tm'), may hold values from -6 to 6
- seg_counts: int32 [2, 4], replicated, may hold values from 1 to 225, as said below
- query_weight: float32 [512, 512], P(None, 'head'), may hold values from -0.25 to 0.25
- query_bias: float32 [512], P('head'), may hold values from -3 to 3
- key_weight: float32 [512, 512], P(None, 'head'), may hold values from -0.25 to 0.25
- value_weight: float32 [512, 512], P(None, 'head'), may hold values from -0.25 to 0.25
- value_bias: float32 [512], P('head'), may hold values from -3 to 3
- out_weight: float32 [512, 512], P('head'), may hold values from -0.75 to 0.75
- out_bias: float32 [512], replicated, may hold values from -3 to 3
- first_gain: float32 [512], replicated, may hold values from 0.25 to 1.75
- first_shift: float32 [512], replicated, may hold values from -2 to 2
- second_gain: float32 [512], replicated, may hold values from 0.25 to 1.75
- second_shift: float32 [512], replicated, may hold values from -2 to 2
- inner_weight: float32 [512, 2048], P(None, 'head'), may hold values from -0.25 to 0.25
- inner_bias: float32 [2048], P('head'), may hold values from -3 to 3
- outer_weight: float32 [2048, 512], P('head'), may hold values from -0.1875 to 0.1875
- outer_bias: float32 [512], replicated, may hold values from -3 to 3
Outputs:
- layer_output: float32 [2, 4096, 512], P(None, 'tm')
- frames_grad: float32 [2, 4096, 512], P(None, 'tm')
- query_weight_grad: float32 [512, 512], P(None, 'head')
- query_bias_grad: float32 [512], P('head')
- key_weight_grad: float32 [512, 512], P(None, 'head')
- value_weight_grad: float32 [512, 512], P(None, 'head')
- value_bias_grad: float32 [512], P('head')
- out_weight_grad: float32 [512, 512], P('head')
- out_bias_grad: float32 [512], replicated
- first_gain_grad: float32 [512], replicated
- first_shift_grad: float32 [512], replicated
- second_gain_grad: float32 [512], replicated
- second_shift_grad: float32 [512], replicated
- inner_weight_grad: float32 [512, 2048], P(None, 'head')
- inner_bias_grad: float32 [2048], P('head')
- outer_weight_grad: float32 [2048, 512], P('head')
- outer_bias_grad: float32 [512], replicated
Inputs may be any that keep to these rules, and one draw needn't show every extreme that they name: `seg_counts`: each row sums to 256; in each row exactly one utterance has 225 segments, the others at least one.
All inputs are finite; a program needn't handle non-finite values.
Results may differ from a plain program's by a relative error of at most 0.0003.
Values sent between devices are 32-bit elements; how exact they have to be, the bound alone decides.
No kernel may reach another device: no remote copies, remote signals or barrier semaphores. Data moves between devices by JAX's collectives and lax.ppermute only.
A program may use at most 128 MiB of HBM per device.

v0:
```python
import functools

import jax
import jax.numpy as jnp
from jax import lax
from jax.experimental import pallas as pl
from jax.experimental.pallas import tpu as pltpu
from jax.sharding import PartitionSpec as P

HEAD_DIM = 64
SEG = 16
RC = 4
LC = 30
MEM = 4

EPSILON = 1e-05
MASKED = -1e30
F32 = jnp.float32

BEFORE = MEM * SEG
AHEAD = 8
CACHE = 32
SUMS = 8
BLOCK = 64
WIN = CACHE + BLOCK + AHEAD
SWIN = 16
KEYS = 128
FIRST_GAIN, FIRST_SHIFT, SECOND_GAIN, SECOND_SHIFT, OUT_BIAS, INNER_BIAS, OUTER_BIAS = range(7)
PAIR = 2 * HEAD_DIM
MIB = 1 << 20


def mm(left, right, left_dim=1, right_dim=0):
    return lax.dot_general(
        left,
        right,
        (((left_dim,), (right_dim,)), ((), ())),
        precision=lax.Precision.HIGH,
        preferred_element_type=F32,
    )


def normalise(values):
    centred = values - jnp.mean(values, axis=-1, keepdims=True)
    variance = jnp.mean(centred * centred, axis=-1, keepdims=True)
    rate = lax.rsqrt(variance + EPSILON)
    return centred * rate, rate


def norm_back(grad, gain, xhat, rate):
    scaled = grad * gain
    first = jnp.mean(scaled, axis=-1, keepdims=True)
    second = jnp.mean(scaled * xhat, axis=-1, keepdims=True)
    return rate * (scaled - first - xhat * second)


def column_sums(values):
    return jnp.sum(values, axis=0, keepdims=True)


def seg_means(values):
    rows, width = values.shape
    return jnp.sum(values.reshape(rows // SEG, SEG, width), axis=1) * (1.0 / SEG)


def near_bit():
    return lax.axis_index("head") % 2


def far_bit():
    return lax.axis_index("head") // 2


def my_rows(rows):
    half = rows // 2
    return pl.ds(pl.multiple_of(near_bit() * half, half), half)


def lanes_of(place, width, start=0):
    at = place + near_bit() - 2 * place * near_bit()
    return pl.ds(pl.multiple_of(start + at * width, width), width)


def half_rows(place, half):
    return pl.ds(pl.multiple_of(place * half, half), half)


def full(shape):
    return pl.BlockSpec(shape, lambda *_: (0,) * len(shape))


class Steps:
    def __init__(self):
        self.held = []
        self.us = 0.1

    def call(self, kernel, name, outs, args, specs=None, scratch=(), vmem=32, copies=0, far=(), far_outs=()):
        specs = dict(specs or {})
        given, made, held = len(args), len(outs), tuple(self.held)
        token = bool(far_outs)
        somewhere = pl.BlockSpec(memory_space=pl.ANY)
        in_hbm = pl.BlockSpec(memory_space=pltpu.HBM)

        def body(*refs):
            ins, rest = refs[:given], refs[given + len(held) :]
            if token:
                rest[made][...] = jnp.zeros(rest[made].shape, F32)
            kernel(*ins, *rest[:made], *rest[made + token :])

        args = [pltpu.with_memory_space_constraint(a, pltpu.HBM) if i in far else a for i, a in enumerate(args)]
        out_specs = [in_hbm if i in far_outs else full(shape) for i, shape in enumerate(outs)]
        out_shape = [
            pltpu.HBM(shape, F32) if i in far_outs else jax.ShapeDtypeStruct(shape, F32) for i, shape in enumerate(outs)
        ]
        if token:
            out_specs.append(full((1, 128)))
            out_shape.append(jax.ShapeDtypeStruct((1, 128), F32))
        out = pl.pallas_call(
            body,
            name=name,
            grid=(1,),
            in_specs=[in_hbm if i in far else specs.get(i, full(a.shape)) for i, a in enumerate(args)]
            + [somewhere] * len(held),
            out_specs=out_specs,
            out_shape=out_shape,
            scratch_shapes=[pltpu.VMEM(shape, F32) for shape in scratch]
            + ([pltpu.SemaphoreType.DMA((copies,))] if copies else []),
            compiler_params=pltpu.CompilerParams(vmem_limit_bytes=vmem * MIB),
            cost_estimate=pl.CostEstimate(flops=int(self.us * 5.18e8), bytes_accessed=0, transcendentals=0),
        )(*args, *held)
        self.held = [out[-1]]
        return out[:made]


def copy_all(pairs, sems):
    copies = [pltpu.make_async_copy(a, b, sems.at[i]) for i, (a, b) in enumerate(pairs)]
    for copy in copies:
        copy.start()
    return copies


def pack_kernel(wq, wk, wv, wo, bq, bv, bi, frames, out, edge, sems):
    rows, width = wq.shape
    out[rows:] = jnp.zeros((out.shape[0] - rows, out.shape[1]), F32)
    pairs = [(w, out.at[pl.ds(0, rows), pl.ds(i * width, width)]) for i, w in enumerate((wq, wk, wv))]
    for at in range(0, wo.shape[1], width):
        pairs.append((wo.at[:, pl.ds(at, width)], out.at[pl.ds(at, width), pl.ds(3 * width, width)]))
    pairs += [(b, out.at[pl.ds(rows, 1), pl.ds(i * width, width)]) for i, b in ((0, bq), (2, bv))]
    pairs.append((bi, out.at[pl.ds(rows + 1, 1), pl.ds(0, bi.shape[1])]))
    start = pl.multiple_of((1 - near_bit()) * (frames.shape[1] - BEFORE), BEFORE)
    pairs += [(frames.at[m, pl.ds(start, BEFORE)], edge.at[m]) for m in range(frames.shape[0])]
    for copy in copy_all(pairs, sems):
        copy.wait()


def norm_kernel(
    frames, gain, shift, wi, wu, wo, cotangent,
    x_ref, xhat_ref, rate_ref, normed_ref, wi_ref, wu_ref, wo_ref, g_0, g_1, before, ahead, params, sems,
):
    micros, half, _ = x_ref.shape
    rows = frames.shape[1]
    pairs = [(gain, params.at[pl.ds(0, 1)]), (shift, params.at[pl.ds(8, 1)])]
    pairs += [(frames.at[m, my_rows(rows)], x_ref.at[m]) for m in range(micros)]
    pairs += [(frames.at[m, pl.ds(half - BEFORE, BEFORE)], before.at[m]) for m in range(micros)]
    pairs += [(frames.at[m, pl.ds(half, AHEAD)], ahead.at[m]) for m in range(micros)]
    pairs += [(wo, wo_ref), (wi, wi_ref), (wu, wu_ref)]
    pairs += [(cotangent.at[m, my_rows(rows)], g) for m, g in enumerate((g_0, g_1))]
    copies = copy_all(pairs, sems)
    for copy in copies[:2]:
        copy.wait()
    for micro in range(micros):
        copies[2 + micro].wait()
        xhat, rate = normalise(x_ref[micro])
        xhat_ref[micro] = xhat
        normed_ref[micro] = xhat * params[0:1] + params[8:9]
        rate_ref[micro] = jnp.broadcast_to(rate, (half, rate_ref.shape[2]))
    for copy in copies[2 + micros :]:
        copy.wait()


def project_kernel(normed, own, pair, g1, s1, g2, s2, bo, bi, bu, q_ref, kv_ref, w_ref, bias, rows_ref, sems):
    micros, half, wide = q_ref.shape
    features = normed.shape[2]
    width = own.shape[1] // 4
    copies = copy_all([(v, rows_ref.at[i]) for i, v in enumerate((g1, s1, g2, s2, bo, bi, bu))], sems)
    for number in range(3):
        at = slice(number * width, (number + 1) * width)
        for place, source in enumerate((own, pair)):
            lanes = lanes_of(place, width, 2 * number * width)
            w_ref[:, lanes] = source[:features, at]
            bias[:, lanes] = source[features : features + 1, at]
    for micro in range(micros):
        out = mm(normed[micro], w_ref[...]) + bias[...]
        q_ref[micro] = out[:, :wide]
        kv_ref[micro] = out[:, wide:]
    for copy in copies:
        copy.wait()


def edges_kernel(edge, before, ahead, params, w_ref, bias, xhat_ref, normed_ref, kv_ref):
    near = near_bit()
    wide = w_ref.shape[1] // 3
    for micro in range(edge.shape[0]):
        first = jnp.where(near == 0, edge[micro], before[micro])
        last = jnp.where(near == 0, ahead[micro], edge[micro, :AHEAD])
        xhat, _ = normalise(jnp.concatenate([first, last], axis=0))
        normed = xhat * params[FIRST_GAIN] + params[FIRST_SHIFT]
        xhat_ref[micro] = xhat
        normed_ref[micro] = normed
        kv_ref[micro] = mm(normed, w_ref[:, wide:]) + bias[:, wide:]


def fill_keys(kv, edge, kx, sx):
    length = kv.shape[0]
    kx[BEFORE : BEFORE + length] = kv
    segs = length // SEG
    sx[SUMS : SUMS + segs] = seg_means(kv)
    if edge is not None:
        kx[:BEFORE] = edge[:BEFORE]
        kx[BEFORE + length :] = edge[BEFORE:]
        sx[: SUMS - MEM] = jnp.zeros((SUMS - MEM, kv.shape[1]), F32)
        sx[SUMS - MEM : SUMS] = seg_means(edge[:BEFORE])
        sx[SUMS + segs :] = jnp.zeros((sx.shape[0] - SUMS - segs, kv.shape[1]), F32)


def summary_start(block):
    return (block * (BLOCK // SEG) + SUMS - MEM) // SUMS * SUMS


def frame_rows(block):
    start = BEFORE - CACHE + block * BLOCK
    return slice(start, start + WIN)


def key_window(kx, sx, block, lanes):
    start = summary_start(block)
    rows = [kx[frame_rows(block), lanes], sx[start : start + SWIN, lanes]]
    return jnp.concatenate(rows + [jnp.zeros((KEYS - WIN - SWIN, PAIR), F32)], axis=0)


def by_head(values):
    first = lax.broadcasted_iota(jnp.int32, values.shape, 1) < HEAD_DIM
    return jnp.concatenate([jnp.where(first, values, 0.0), jnp.where(first, 0.0, values)], axis=0)


def side_by_side(values):
    rows = values.shape[0] // 2
    first = lax.broadcasted_iota(jnp.int32, (rows, values.shape[1]), 1) < HEAD_DIM
    return jnp.where(first, values[:rows], values[rows:])


def owner_of(segment, bounds):
    owner = jnp.where(segment < 0, -1, 0)
    for bound in bounds:
        owner = owner + (segment >= bound).astype(jnp.int32)
    return owner


def visible(block, base, bounds):
    row = lax.broadcasted_iota(jnp.int32, (2 * BLOCK, 1), 0) % BLOCK
    column = lax.broadcasted_iota(jnp.int32, (1, KEYS), 1)
    query_seg = block * (BLOCK // SEG) + row // SEG
    frame = block * BLOCK - CACHE + column
    is_frame = column < WIN
    summary = summary_start(block) - SUMS + column - WIN
    key_seg = jnp.where(is_frame, (frame + CACHE) // SEG - CACHE // SEG, summary)
    key_seg = jnp.where(column < WIN + SWIN, key_seg, -(1 << 20))
    inside = (frame >= query_seg * SEG - LC) & (frame < query_seg * SEG + SEG + RC)
    near = (key_seg >= query_seg - MEM) & (key_seg < query_seg)
    seen = (is_frame & inside) | ((column >= WIN) & near)
    return seen & (owner_of(key_seg + base, bounds) == owner_of(query_seg + base, bounds))


def bounds_of(counts, micro):
    bounds, total = [], 0
    for utterance in range(counts.shape[1]):
        total = total + counts[micro, utterance]
        bounds.append(total)
    return bounds


def first_segment(length):
    return (lax.axis_index("tm") * 2 + near_bit()) * (length // SEG)


def block_rows(block):
    return slice(block * BLOCK, (block + 1) * BLOCK)


def attend_block(block, seen, query, kx, sx, keep, put):
    width = query.shape[1]
    for pair in range(width // PAIR):
        lanes = slice(pair * PAIR, (pair + 1) * PAIR)
        value_lanes = slice(width + pair * PAIR, width + (pair + 1) * PAIR)
        scores = mm(by_head(query[:, lanes] * HEAD_DIM ** (-0.5)), key_window(kx, sx, block, lanes), 1, 1)
        scores = jnp.where(seen, scores, MASKED)
        weights = jnp.exp(scores - jnp.max(scores, axis=-1, keepdims=True))
        weights = weights / jnp.sum(weights, axis=-1, keepdims=True)
        keep(pair, weights)
        put(lanes, side_by_side(mm(weights, key_window(kx, sx, block, value_lanes))))


def attend_inner_kernel(counts, q_ref, kv_ref, mix_ref, p_ref, kx, sx):
    micros, length, _ = q_ref.shape
    base = first_segment(length)
    for micro in range(micros):
        fill_keys(kv_ref[micro], None, kx, sx)
        bounds = bounds_of(counts, micro)
        for number, block in enumerate(range(1, length // BLOCK - 1)):
            def keep(pair, weights):
                p_ref[micro, number, pair] = weights

            def put(lanes, values):
                mix_ref[micro, block_rows(number), lanes] = values

            seen = visible(block, base, bounds)
            attend_block(block, seen, q_ref[micro, block_rows(block)], kx, sx, keep, put)


def attend_outer_kernel(micro, counts, q_ref, kv_ref, edge, inner, mix_ref, p_ref, kx, sx):
    _, length, _ = q_ref.shape
    base = first_segment(length)
    fill_keys(kv_ref[micro], edge[micro], kx, sx)
    bounds = bounds_of(counts, micro)
    mix_ref[BLOCK : length - BLOCK] = inner[micro]
    for number, block in enumerate((0, length // BLOCK - 1)):
        def keep(pair, weights):
            p_ref[number, pair] = weights

        def put(lanes, values):
            mix_ref[block_rows(block), lanes] = values

        seen = visible(block, base, bounds)
        attend_block(block, seen, q_ref[micro, block_rows(block)], kx, sx, keep, put)


def back_kernel(
    micro, grad_ref, mid_ref, g_ref, params, wo_here, mix, q_ref, kv_ref, edge, p_inner, p_outer,
    dmid_ref, dq_ref, dkv_ref, dwo_own, dwo_pair, vec_ref,
    kx, sx, dsx, dmix, dwo,
):
    _, length, width = q_ref.shape
    near_width = dwo_own.shape[1]
    grad = grad_ref[...]
    xhat, rate = normalise(mid_ref[...])
    dmid = g_ref[...] + norm_back(grad, params[SECOND_GAIN], xhat, rate)
    dmid_ref[...] = dmid
    vec_ref[0:1] = column_sums(dmid)
    vec_ref[1:2] = column_sums(grad * xhat)
    vec_ref[2:3] = column_sums(grad)
    dmix[...] = mm(dmid, wo_here[...], 1, 1)
    dwo[...] = mm(dmid, mix[...], 0, 0)
    dwo_own[...] = dwo[:, lanes_of(0, near_width)]
    dwo_pair[...] = dwo[:, lanes_of(1, near_width)]
    fill_keys(kv_ref[micro], edge[micro], kx, sx)
    dkv_ref[...] = jnp.zeros_like(dkv_ref)
    dsx[...] = jnp.zeros_like(dsx)
    for block in range(length // BLOCK):
        start = summary_start(block)
        rows, frames, sums = block_rows(block), frame_rows(block), slice(start, start + SWIN)
        for pair in range(width // PAIR):
            lanes = slice(pair * PAIR, (pair + 1) * PAIR)
            value_lanes = slice(width + pair * PAIR, width + (pair + 1) * PAIR)
            inside = 0 < block < length // BLOCK - 1
            weights = p_inner[micro, block - 1, pair] if inside else p_outer[min(block, 1), pair]
            grad = by_head(dmix[rows, lanes])
            dweights = mm(grad, key_window(kx, sx, block, value_lanes), 1, 1)
            dscores = weights * (dweights - jnp.sum(dweights * weights, axis=-1, keepdims=True))
            dquery = side_by_side(mm(dscores, key_window(kx, sx, block, lanes)))
            dq_ref[rows, lanes] = dquery * HEAD_DIM ** (-0.5)
            dkeys = mm(dscores, by_head(q_ref[micro, rows, lanes] * HEAD_DIM ** (-0.5)), 0, 0)
            dvalues = mm(weights, grad, 0, 0)
            dkv_ref[frames, lanes] += dkeys[:WIN]
            dkv_ref[frames, value_lanes] += dvalues[:WIN]
            dsx[sums, lanes] += dkeys[WIN : WIN + SWIN]
            dsx[sums, value_lanes] += dvalues[WIN : WIN + SWIN]
    count = BEFORE + length
    segs = count // SEG
    spread = dsx[SUMS - MEM : SUMS - MEM + segs] * (1.0 / SEG)
    spread = jnp.broadcast_to(spread[:, None, :], (segs, SEG, 2 * width))
    dkv_ref[:count] += spread.reshape(count, 2 * width)


def feed_kernel(
    micro, mix_own, mix_far, wo_here, wo_far, wo_far_pair, x_ref, g_ref, params, pair, wi_own, wi_pair, wu_own, wu_pair,
    n2_ref, h_ref, dpre_ref, mid_ref, part_ref,
    mix, wo,
):
    width = mix_own.shape[1] // 2
    features, hidden = wi_own.shape
    far = far_bit()
    here = pl.multiple_of(far * 2 * width, 2 * width)
    there = pl.multiple_of((1 - far) * 2 * width, 2 * width)
    mix[:, pl.ds(here, 2 * width)] = mix_own[...]
    mix[:, pl.ds(there, 2 * width)] = mix_far[...]
    wo[pl.ds(here, 2 * width)] = wo_here[...]
    wo[lanes_of(0, width, there)] = wo_far[...]
    wo[lanes_of(1, width, there)] = wo_far_pair[...]
    middle = x_ref[micro] + mm(mix[...], wo[...]) + params[OUT_BIAS]
    mid_ref[...] = middle
    xhat, _ = normalise(middle)
    normed = xhat * params[SECOND_GAIN] + params[SECOND_SHIFT]
    n2_ref[...] = normed
    part = None
    for place, (wi, wu, bias) in enumerate(((wi_own, wu_own, params[INNER_BIAS][:, :hidden]), (wi_pair, wu_pair, pair[features + 1 : features + 2, :hidden]))):
        at = slice(place * hidden, (place + 1) * hidden)
        pre = mm(normed, wi[...]) + bias
        phi = 0.5 + 0.5 * lax.erf(pre * (0.5**0.5))
        h_ref[:, at] = pre * phi
        slope = phi + pre * (jnp.exp(-0.5 * pre * pre) * 0.3989422804014327)
        dpre = mm(g_ref[...], wu[...], 1, 1) * slope
        dpre_ref[:, at] = dpre
        step = mm(dpre, wi[...], 1, 1)
        part = step if part is None else part + step
    part_ref[...] = part


def put_rows(value, outs):
    at = 0
    for out in outs:
        count = out.shape[0]
        out[...] = value[at : at + count]
        at += count


def inner_weights_kernel(n2_0, n2_1, d_0, d_1, own_ref, *rest):
    *pair, vec_ref = rest
    hidden = own_ref.shape[1]
    for place, outs in enumerate(((own_ref,), pair)):
        at = slice(place * hidden, (place + 1) * hidden)
        put_rows(mm(n2_0[...], d_0[:, at], 0, 0) + mm(n2_1[...], d_1[:, at], 0, 0), outs)
        vec_ref[place : place + 1] = column_sums(d_0[:, at]) + column_sums(d_1[:, at])


def outer_weights_kernel(h_0, h_1, g_0, g_1, own_ref, *rest):
    *pair, vec_ref = rest
    hidden = own_ref.shape[0]
    for place, outs in enumerate(((own_ref,), pair)):
        at = slice(place * hidden, (place + 1) * hidden)
        put_rows(mm(h_0[:, at], g_0[...], 0, 0) + mm(h_1[:, at], g_1[...], 0, 0), outs)
    vec_ref[...] = column_sums(g_0[...]) + column_sums(g_1[...])


def feed_out_kernel(h_0, h_1, wu_own, wu_pair, out_ref):
    hidden = wu_own.shape[0]
    rows = h_0.shape[0]
    for micro, h_ref in enumerate((h_0, h_1)):
        part = mm(h_ref[:, :hidden], wu_own[...]) + mm(h_ref[:, hidden:], wu_pair[...])
        out_ref[micro * rows : (micro + 1) * rows] = part


def out_half_kernel(mid_0, mid_1, part, far, params, out):
    rows = mid_0.shape[0]
    for micro, mid_ref in enumerate((mid_0, mid_1)):
        at = slice(micro * rows, (micro + 1) * rows)
        out[at] = mid_ref[...] + (part[at] + far[at]) + params[OUTER_BIAS]


def project_back_kernel(
    dq_0, dkv_0, dq_1, dkv_1, xhat, xhat_edge, w_ref, part_ref, pair_ref, beyond_ref, vec_ref, work
):
    near = near_bit()
    length, wide = dq_0.shape
    own = slice(BEFORE, BEFORE + length)
    gain, shift = 0.0, 0.0
    for micro, (dq, dkv) in enumerate(((dq_0, dkv_0), (dq_1, dkv_1))):
        work[...] = mm(dkv[...], w_ref[:, wide:], 1, 1)
        work[own] += mm(dq[...], w_ref[:, :wide], 1, 1)
        part_ref[micro * length : (micro + 1) * length] = work[own]
        before = work[:BEFORE]
        ahead = jnp.concatenate([work[BEFORE + length :], jnp.zeros((BEFORE - AHEAD, work.shape[1]), F32)], axis=0)
        pair_ref[micro] = jnp.where(near == 0, ahead, before)
        beyond_ref[micro] = jnp.where(near == 0, before, ahead)
        gain = gain + column_sums(work[own] * xhat[micro]) + column_sums(work[:BEFORE] * xhat_edge[micro, :BEFORE])
        gain = gain + column_sums(work[BEFORE + length :] * xhat_edge[micro, BEFORE:])
        shift = shift + column_sums(work[...])
    vec_ref[0:1] = gain
    vec_ref[1:2] = shift


def edge_add_kernel(part, pair, beyond, out):
    out[...] = part[...]
    near = near_bit()
    micros = pair.shape[0]
    length = part.shape[0] // micros
    for micro in range(micros):
        end = (micro + 1) * length
        out[end - BEFORE : end] += jnp.where(near == 0, pair[micro], beyond[micro])
        out[end - length : end - length + AHEAD] += jnp.where(near == 0, beyond[micro, :AHEAD], pair[micro, :AHEAD])


def project_weights_kernel(
    normed, normed_edge, dq_0, dq_1, dkv_0, dkv_1, wo_own_0, wo_own_1, wo_pair_0, wo_pair_1, mid_0, mid_1, first, vec_outer, vec_inner,
    own_0, own_1, rows_ref, pair_0, pair_1, message, sums, row,
):
    features = normed.shape[2]
    width = wo_own_0.shape[1]
    hidden = vec_inner.shape[1]
    length, wide = dq_0.shape
    own, after = slice(BEFORE, BEFORE + length), slice(BEFORE + length, None)
    edges = jnp.concatenate([dkv_0[:BEFORE], dkv_0[after], dkv_1[:BEFORE], dkv_1[after]], axis=0)
    normed_edges = jnp.concatenate([normed_edge[0], normed_edge[1]], axis=0)
    queries = mm(normed[0], dq_0[...], 0, 0) + mm(normed[1], dq_1[...], 0, 0)
    keyvals = mm(normed[0], dkv_0[own], 0, 0) + mm(normed[1], dkv_1[own], 0, 0) + mm(normed_edges, edges, 0, 0)
    sums[:, :wide] = queries
    sums[:, wide:] = keyvals
    row[:, :wide] = column_sums(dq_0[...]) + column_sums(dq_1[...])
    row[:, wide:] = column_sums(dkv_0[...]) + column_sums(dkv_1[...])
    rows_ref[0:3] = (mid_0[...] + mid_1[...]) * 0.5
    rows_ref[3:5] = first[...]
    rows_ref[5:6] = vec_outer[...] * 0.5
    rows_ref[6:] = jnp.zeros((2, features), F32)
    half = own_0.shape[0]
    pair_0[half : half + 6] = rows_ref[0:6]
    pair_0[half + 6 :] = jnp.zeros((2, features), F32)
    for place, (out_ref, at) in enumerate(((rows_ref, 6), (pair_0, half + 6))):
        for number in range(3):
            lanes = slice(number * width, (number + 1) * width)
            out_ref[at : at + 1, lanes] = row[:, lanes_of(place, width, 2 * number * width)]
        out_ref[at + 1 : at + 2, :hidden] = vec_inner[place : place + 1]
    for place, (outs, wo_0, wo_1) in enumerate((((own_0, own_1), wo_own_0, wo_own_1), ((pair_0, pair_1), wo_pair_0, wo_pair_1))):
        for number in range(3):
            lanes = slice(number * width, (number + 1) * width)
            message[:, lanes] = sums[:, lanes_of(place, width, 2 * number * width)]
        message[:, 3 * width :] = wo_0[...] + wo_1[...]
        for number, out_ref in enumerate(outs):
            out_ref[:half] = message[number * half : (number + 1) * half]


def frames_back_kernel(a_ref, b_ref, xhat, rate, dmid_0, dmid_1, params, out):
    rows = dmid_0.shape[0]
    for micro, dmid_ref in enumerate((dmid_0, dmid_1)):
        at = slice(micro * rows, (micro + 1) * rows)
        grad = norm_back(a_ref[at] + b_ref[at], params[FIRST_GAIN], xhat[micro], rate[micro, :, :1])
        out[at] = dmid_ref[...] + grad


def place_kernel(own, pair, out, sems):
    micros, half = out.shape[0], out.shape[1] // 2
    near = near_bit()
    pairs = []
    for micro in range(micros):
        rows = pl.ds(micro * half, half)
        pairs.append((own.at[rows], out.at[micro, half_rows(near, half)]))
        pairs.append((pair.at[rows], out.at[micro, half_rows(1 - near, half)]))
    for copy in copy_all(pairs, sems):
        copy.wait()


def place_of(bit):
    return lax.axis_index("tm") // bit % 2


def add_pieces(out, a_ref, pieces, rows_ref=None, new_rows=None):
    count, at = a_ref.shape[0], 0
    if not pieces:
        out[...] = a_ref[...]
        if new_rows is not None:
            new_rows[...] = rows_ref[...]
    for piece in pieces:
        take = min(piece.shape[0], count - at)
        if take:
            out[at : at + take] = a_ref[at : at + take] + piece[:take]
        if take < piece.shape[0]:
            new_rows[...] = rows_ref[...] + piece[take:]
        at += take


def add_split_kernel(bits, counts, rows, *refs):
    total = len(bits)
    values, refs = refs[:total], refs[total:]
    rows_ref, refs = (refs[0], refs[1:]) if rows else (None, refs)
    pieces = []
    for count in counts:
        pieces.append(refs[:count])
        refs = refs[count:]
    kept, sent, refs = refs[:total], refs[total : 2 * total], refs[2 * total :]
    new_rows, work = (refs[0], refs[1]) if rows else (None, refs[0])
    for number, bit in enumerate(bits):
        small = (rows_ref, new_rows) if rows and number == 0 else ()
        half = kept[number].shape[0]
        add_pieces(work, values[number], pieces[number], *small)
        place = place_of(bit)
        kept[number][...] = work[half_rows(place, half)]
        sent[number][:half] = work[half_rows(1 - place, half)]
        if small:
            sent[number][half:] = new_rows[...]


def last_kernel(rows, a_ref, *refs):
    rows_ref, refs = (refs[0], refs[1:]) if rows else (None, refs)
    b_ref, out_ref = refs
    half = a_ref.shape[0]
    out_ref[:half] = a_ref[...] + b_ref[:half]
    if rows:
        out_ref[half:] = rows_ref[...] + b_ref[half:]


def stack_kernel(rows, a_0, a_1, *refs):
    rows_ref, refs = (refs[0], refs[1:]) if rows else (None, refs)
    b_0, b_1, out_ref = refs
    half = a_0.shape[0]
    out_ref[:half] = a_0[...] + b_0[:half]
    out_ref[half : 2 * half] = a_1[...] + b_1[...]
    if rows:
        out_ref[2 * half :] = rows_ref[...] + b_0[half:]


def add_whole_kernel(a_ref, b_ref, *outs):
    at = 0
    for out in outs:
        count = out.shape[0]
        out[...] = a_ref[at : at + count] + b_ref[at : at + count]
        at += count


def join_kernel(bits, *refs):
    total = len(bits)
    for bit, mine, theirs, out in zip(bits, refs[:total], refs[total : 2 * total], refs[2 * total :], strict=True):
        half = mine.shape[0]
        place = place_of(bit)
        out[half_rows(place, half)] = mine[...]
        out[half_rows(1 - place, half)] = theirs[...]


def join_out_kernel(bit, mine, theirs, out, sems):
    half = mine.shape[0]
    place = place_of(bit)
    for copy in copy_all([(mine, out.at[half_rows(place, half)]), (theirs, out.at[half_rows(1 - place, half)])], sems):
        copy.wait()


def join_heads_kernel(bits, *refs):
    *parts, wq, wk, wv, wo = refs
    width = wq.shape[1]
    at = 0
    for number, bit in enumerate(bits):
        mine, theirs = parts[2 * number : 2 * number + 2]
        half = mine.shape[0]
        place = place_of(bit)
        for where, part in ((place, mine), (1 - place, theirs)):
            rows = pl.ds(pl.multiple_of(at + where * half, half), half)
            for heads, out in enumerate((wq, wk, wv)):
                out[rows, :] = part[:, heads * width : (heads + 1) * width]
            wo[:, rows] = part[:, 3 * width :].T
        at += 2 * half


def small_kernel(rows, far, outs):
    width = outs[-3].shape[1]
    for number, out in enumerate(outs[:6]):
        out[...] = rows[number : number + 1] + far[number : number + 1]
    outs[6][...] = rows[6:7, :width]
    outs[7][...] = rows[6:7, 2 * width : 3 * width]
    outs[8][...] = rows[7:8, : outs[8].shape[1]]


def finish_kernel(bits, rows, far, *refs):
    count = 2 * len(bits)
    small_kernel(rows, far, refs[count : count + 9])
    join_heads_kernel(bits, *refs[:count], *refs[count + 9 :])


def swap(value, axis, bit):
    size = lax.axis_size(axis)
    return lax.ppermute(value, axis, [(i, i ^ bit) for i in range(size)])


def swap_near(parts):
    return [swap(part, "head", 1) for part in parts]


def swap_edges(value, back):
    size, group = lax.axis_size("tm"), lax.axis_size("head")
    pairs = []
    for source in range(size):
        for place in range(group):
            target = source + (1 - 2 * (place % 2)) * (-1 if back else 1)
            if 0 <= target < size:
                pairs.append((source * group + place, target * group + (place ^ 1 if back else place)))
    return lax.ppermute(value, ("tm", "head"), pairs)


class SumsOverTm:
    def __init__(self, run, a, b, rows=None):
        bits = [1 << i for i in range(lax.axis_size("tm").bit_length() - 1)]
        self.run, self.values, self.got = run, list(a), [list(v) for v in b]
        self.rows = [] if rows is None else [rows]
        self.apart = [(bits[1], bits[0]), (bits[0], bits[1])]
        self.together, self.last = bits[2:-1], bits[-1]
        self.todo = [("split", pair) for pair in self.apart]
        self.todo.append(("stack",))
        self.todo += [("split", (bit,)) for bit in self.together] + [("last",)] * bool(self.together)
        self.todo.append(("add",))
        self.todo += [("join", (bit,)) for bit in reversed(self.together)] + [("part",)] * bool(self.together)
        self.todo.append(("join", self.apart[1]))
        self.step()

    def step(self):
        run, values = self.run, self.values
        kind, *rest = self.todo.pop(0)
        features = values[0].shape[1]
        count = values[0].shape[0]
        more = sum(v.shape[0] for v in self.rows)
        has_rows = bool(self.rows)
        shape = lambda rows: (rows, features)
        got = [piece for pieces in self.got for piece in pieces]
        if kind == "split":
            (bits,) = rest
            half = count // 2
            extra = [more] + [0] * (len(bits) - 1)
            out = run.call(
                functools.partial(add_split_kernel, bits, [len(v) for v in self.got], has_rows), "add_split",
                [shape(half)] * len(bits) + [shape(half + e) for e in extra] + [v.shape for v in self.rows],
                (*values, *self.rows, *got), scratch=[shape(count)],
            )
            self.values, messages, self.rows = out[: len(bits)], out[len(bits) : 2 * len(bits)], out[2 * len(bits) :]
            self.got = [[swap(v, "tm", bit)] for v, bit in zip(messages, bits, strict=True)]
            return
        if kind in ("stack", "last"):
            if kind == "stack":
                (value,) = run.call(
                    functools.partial(stack_kernel, has_rows), "stack", [shape(2 * count + more)], (*values, *self.rows, *got)
                )
                count = 2 * count
            else:
                (value,) = run.call(
                    functools.partial(last_kernel, has_rows), "stack", [shape(count + more)], (*values, *self.rows, *got)
                )
            if kind == "stack" and self.together:
                self.values, self.rows = [value[:count]], [value[count:]] * has_rows
                self.values, self.got = self.values, [[]]
                return self.step()
            self.values, self.count = [value], count
            self.got = [[swap(value, "tm", self.last)]]
            return
        if kind == "add":
            parts = [self.count] if self.together else [self.count // 2] * 2
            out = run.call(
                add_whole_kernel, "add", [shape(n) for n in parts] + [v.shape for v in self.rows], (*values, *got)
            )
            self.values, self.rows = out[: len(parts)], out[len(parts) :]
        elif kind == "join":
            (bits,) = rest
            self.values = run.call(
                functools.partial(join_kernel, bits), "join", [shape(2 * count)] * len(bits), (*values, *got)
            )
        elif kind == "part":
            self.values = [values[0][: count // 2], values[0][count // 2 :]]
        following = self.todo[0] if self.todo else ("join", self.apart[0])
        if following[0] == "part":
            return self.step()
        self.got = [[swap(v, "tm", bit)] for v, bit in zip(self.values, following[1], strict=True)]

    @property
    def joined(self):
        return not self.todo

    def halves(self, number):
        return self.apart[0][number], (self.values[number], *self.got[number])


ORDER = (
    ("pack", 8), ("norm", 4.8), ("project", 2.2), ("attend_inner", 11), ("edges", 1), ("hand_on", 0.5),
    ("attend_outer0", 24), ("attend_outer1", 1), ("feed0", 18), ("feed1", 14), ("outer_weights", 6),
    ("inner_weights", 11), ("feed_out", 0.6), ("grad_sum0", 18), ("ffn", 11), ("back0", 6), ("grad_sum1", 18),
    ("back1", 0.5), ("ffn", 0.1), ("project_back", 1.8), ("project_weights", 2), ("ffn", 0.1), ("edge_add", 5),
    ("out_half", 5), ("out_send", 6), ("heads", 20), ("place_out", 1.3), ("heads", 0.1), ("ffn", 0.1), ("heads", 3),
    ("frames_back", 0.6), ("ffn", 20), ("place_frames", 0.1), ("heads", 0.1), ("heads", 0.1), ("join_outer", 0.1),
    ("join_inner", 0.1), ("finish", 1.3),
)
PIECES = 1


def copy_kernel(source, target):
    target[...] = source[...]


def hand_on_kernel(own, pair, far, here, far_copy):
    far_copy[...] = far[...]
    width = far.shape[0]
    for near, source in enumerate((own, pair)):
        for at in range(0, far.shape[1], width):
            lanes = slice(3 * width, 4 * width)
            here[lanes_of(near, width), at : at + width] = source[at : at + width, lanes]


class Layer:
    def __init__(
        self, frames, cotangent, seg_counts, query_weight, query_bias, key_weight, value_weight, value_bias,
        out_weight, out_bias, first_gain, first_shift, second_gain, second_shift,
        inner_weight, inner_bias, outer_weight, outer_bias,
    ):
        self.frames, self.cotangent, self.counts = frames, cotangent, seg_counts
        self.projections = (query_weight, key_weight, value_weight)
        self.weights = (inner_weight, outer_weight, out_weight)
        row = lambda v: v.reshape(1, v.shape[0])
        self.bq, self.bv, self.bo, self.bi, self.bu = map(row, (query_bias, value_bias, out_bias, inner_bias, outer_bias))
        self.g1, self.s1, self.g2, self.s2 = map(row, (first_gain, first_shift, second_gain, second_shift))
        micros, shard, features = frames.shape
        self.micros, self.features = micros, features
        self.width, self.hidden = query_weight.shape[1], inner_weight.shape[1]
        self.length = shard // 2
        self.segs, self.blocks, self.pairs = self.length // SEG, self.length // BLOCK, 2 * self.width // PAIR
        self.big = (self.length, features)
        self.each = (micros, self.length)
        self.quarter = (self.length // 2, features)
        self.square = (2 * BLOCK, KEYS)
        self.around = BEFORE + self.length + AHEAD
        self.key_scratch = [(self.around, 4 * self.width), (SUMS + self.segs + SUMS, 4 * self.width)]
        self.run = Steps()
        self.smem = pl.BlockSpec(memory_space=pltpu.SMEM)
        pairs = [None] * micros
        self.mix, self.mix_far, self.p_outer, self.fed, self.dn2 = (list(pairs) for _ in range(5))
        self.back_of = list(pairs)
        self.sums = {}

    def pack(self):
        args = (*self.projections, self.weights[2], self.bq, self.bv, self.bi, self.frames)
        self.own, edge = self.run.call(
            pack_kernel, "pack", [(self.features + 8, 4 * self.width), (self.micros, BEFORE, self.features)], args,
            copies=6 + self.features // self.width + self.micros, far=range(8),
        )
        self.pair = swap(self.own, "head", 1)
        self.edge = swap_edges(edge, False)

    def norm(self):
        each, features, micros = self.each, self.features, self.micros
        wi, wu, wo = self.weights
        (self.x, self.xhat, self.rate, self.normed, self.wi, self.wu, self.wo, *self.g, self.before, self.ahead) = self.run.call(
            norm_kernel, "norm",
            [each + (features,)] * 2 + [each + (128,), each + (features,), wi.shape, wu.shape, wo.shape, self.big, self.big,
             (micros, BEFORE, features), (micros, AHEAD, features)],
            (self.frames, self.g1, self.s1, wi, wu, wo, self.cotangent),
            scratch=[(16, features)], copies=4 * micros + 5, far=range(7),
        )
        self.wo_far = swap(self.wo, "head", 2)
        self.wi_pair, self.wu_pair = (swap(v, "head", 1) for v in (self.wi, self.wu))

    def project(self):
        each, features, width = self.each, self.features, self.width
        args = (self.normed, self.own, self.pair, self.g1, self.s1, self.g2, self.s2, self.bo, self.bi, self.bu)
        self.q, self.kv, self.w_all, self.bias, self.params = self.run.call(
            project_kernel, "project",
            [each + (2 * width,), each + (4 * width,), (features, 6 * width), (1, 6 * width), (7, 1, features)],
            args, copies=7, far=range(3, 10),
        )

    def edges(self):
        shape = (self.micros, BEFORE + AHEAD)
        self.xhat_edge, self.normed_edge, self.kv_edge = self.run.call(
            edges_kernel, "edges", [shape + (self.features,)] * 2 + [shape + (4 * self.width,)],
            (self.edge, self.before, self.ahead, self.params, self.w_all, self.bias),
        )

    def attend_inner(self):
        self.mix_inner, self.p_inner = self.run.call(
            attend_inner_kernel, "attend_inner",
            [(self.micros, self.length - 2 * BLOCK, 2 * self.width),
             (self.micros, self.blocks - 2, self.pairs) + self.square],
            (self.counts, self.q, self.kv), {0: self.smem}, self.key_scratch,
        )

    def attend_outer(self, m):
        self.mix[m], self.p_outer[m] = self.run.call(
            functools.partial(attend_outer_kernel, m), "attend_outer",
            [(self.length, 2 * self.width), (2, self.pairs) + self.square],
            (self.counts, self.q, self.kv, self.kv_edge, self.mix_inner),
            {0: self.smem}, self.key_scratch,
        )
        self.mix_far[m] = swap(self.mix[m], "head", 2)

    def hand_on(self):
        shape = self.wo_far.shape
        self.wo_here, far = self.run.call(
            hand_on_kernel, "hand_on", [(2 * shape[0], shape[1]), shape], (self.own, self.pair, self.wo_far)
        )
        self.wo_far_pair = swap(far, "head", 1)

    def feed(self, m):
        big, features, hidden = self.big, self.features, self.hidden
        *self.fed[m], part = self.run.call(
            functools.partial(feed_kernel, m), "feed", [big, (self.length, 2 * hidden), (self.length, 2 * hidden), big, big],
            (self.mix[m], self.mix_far[m], self.wo_here, self.wo_far, self.wo_far_pair, self.x, self.g[m], self.params,
             self.pair, self.wi, self.wi_pair, self.wu, self.wu_pair),
            scratch=[big, (features, features)],
        )
        self.dn2[m] = (part, swap(part, "head", 2))

    def inner_weights(self):
        features, hidden = self.features, self.hidden
        self.inner_own, *pair, self.vec_inner = self.run.call(
            inner_weights_kernel, "inner_weights",
            [(features, hidden)] + [(features // PIECES, hidden)] * PIECES + [(2, hidden)],
            (self.fed[0][0], self.fed[1][0], self.fed[0][2], self.fed[1][2]),
        )
        self.inner_pair = swap_near(pair)

    def outer_weights(self):
        features, hidden = self.features, self.hidden
        self.outer_own, *pair, self.vec_outer = self.run.call(
            outer_weights_kernel, "outer_weights",
            [(hidden, features)] + [(hidden // PIECES, features)] * PIECES + [(1, features)],
            (self.fed[0][1], self.fed[1][1], *self.g),
        )
        self.outer_pair = swap_near(pair)

    def feed_out(self):
        (part,) = self.run.call(
            feed_out_kernel, "feed_out", [(self.micros * self.length, self.features)],
            (self.fed[0][1], self.fed[1][1], self.wu, self.wu_pair),
        )
        self.part = (part, swap(part, "head", 2))

    def out_half(self):
        (half,) = self.run.call(
            out_half_kernel, "out_half", [(self.micros * self.length, self.features)],
            (self.fed[0][3], self.fed[1][3], *self.part, self.params),
        )
        self.out = half

    def out_send(self):
        (half,) = self.run.call(copy_kernel, "out_send", [self.out.shape], (self.out,))
        self.out = (half, swap(half, "head", 1))

    def grad_sum(self, m):
        (self.dn2[m],) = self.run.call(add_whole_kernel, "grad_sum", [self.big], self.dn2[m])

    def back(self, m):
        length, width, features = self.length, self.width, self.features
        self.back_of[m] = self.run.call(
            functools.partial(back_kernel, m), "back",
            [self.big, (length, 2 * width), (self.around, 4 * width), (features, width), (features, width), (3, features)],
            (self.dn2[m], self.fed[m][3], self.g[m], self.params, self.wo_here, self.mix[m], self.q, self.kv,
             self.kv_edge, self.p_inner, self.p_outer[m]),
            scratch=self.key_scratch + self.key_scratch[1:] + [(length, 2 * width), (features, 2 * width)],
        )

    def pick(self, number):
        return [v[number] for v in self.back_of]

    def project_back(self):
        features, micros = self.features, self.micros
        (dq_0, dq_1), (dkv_0, dkv_1) = self.pick(1), self.pick(2)
        part, pair, beyond, self.vec_first = self.run.call(
            project_back_kernel, "project_back",
            [(micros * self.length, features)] + [(micros, BEFORE, features)] * 2 + [(2, features)],
            (dq_0, dkv_0, dq_1, dkv_1, self.xhat, self.xhat_edge, self.w_all), scratch=[(self.around, features)],
        )
        self.edges_back = (part, swap(pair, "head", 1), swap_edges(beyond, True))

    def edge_add(self):
        part = self.edges_back[0]
        (part,) = self.run.call(edge_add_kernel, "edge_add", [part.shape], self.edges_back)
        self.dn1 = (part, swap(part, "head", 2))

    def project_weights(self):
        features, width = self.features, self.width
        *self.heads_own, self.rows, a, b = self.run.call(
            project_weights_kernel, "project_weights",
            [(features // 2, 4 * width)] * 2 + [(8, features), (features // 2 + 8, 4 * width), (features // 2, 4 * width)],
            (self.normed, self.normed_edge, *self.pick(1), *self.pick(2), *self.pick(3), *self.pick(4), *self.pick(5),
             self.vec_first, self.vec_outer, self.vec_inner),
            scratch=[(features, 4 * width), (features, 6 * width), (1, 6 * width)],
        )
        self.heads_pair = swap_near((a, b))

    def begin(self, name):
        if name == "heads":
            a, b = self.heads_pair
            return SumsOverTm(self.run, self.heads_own, ((a,), (b,)), self.rows)
        return SumsOverTm(self.run, (self.outer_own, self.inner_own), (self.outer_pair, self.inner_pair))

    def sum(self, name):
        if name not in self.sums:
            self.sums[name] = self.begin(name)
        elif not self.sums[name].joined:
            self.sums[name].step()

    def ffn(self):
        self.sum("ffn")

    def heads(self):
        self.sum("heads")

    def frames_back(self):
        (half,) = self.run.call(
            frames_back_kernel, "frames_back", [(self.micros * self.length, self.features)],
            (*self.dn1, self.xhat, self.rate, *self.pick(0), self.params),
        )
        self.grad = (half, swap(half, "head", 1))

    def place(self, name, halves):
        (out,) = self.run.call(
            place_kernel, name, [(self.micros, 2 * self.length, self.features)], halves, copies=2 * self.micros, far_outs=[0]
        )
        return out

    def place_out(self):
        self.layer_output = self.place("place_out", self.out)

    def place_frames(self):
        self.frames_grad = self.place("place_frames", self.grad)

    def join(self, name, number, shape):
        bit, parts = self.sums["ffn"].halves(number)
        (out,) = self.run.call(
            functools.partial(join_out_kernel, bit), name, [shape], parts, copies=2, far_outs=[0]
        )
        return out

    def settle(self, *names):
        while not all(self.sums[name].joined for name in names):
            for name in names:
                self.sum(name)

    def join_outer(self):
        self.settle("ffn", "heads")
        self.outer_grad = self.join("join_outer", 0, self.weights[1].shape)

    def join_inner(self):
        self.inner_grad = self.join("join_inner", 1, self.weights[0].shape)

    def finish(self):
        features, width, hidden = self.features, self.width, self.hidden
        sums = self.sums["heads"]
        rows = sums.rows[0]
        bits, parts = zip(*(sums.halves(i) for i in range(2)), strict=True)
        out = self.run.call(
            functools.partial(finish_kernel, list(bits)), "finish",
            [(1, features)] * 6 + [(1, width)] * 2 + [(1, hidden)] + [(features, width)] * 3 + [(width, features)],
            (rows, swap(rows, "head", 2), *parts[0], *parts[1]),
        )
        bo, g2, s2, g1, s1, bu, bq, bv, bi = (v.reshape(v.shape[1]) for v in out[:9])
        wq, wk, wv, wo = out[9:]
        return (
            self.layer_output, self.frames_grad, wq, bq, wk, wv, bv, wo, bo, g1, s1, g2, s2, self.inner_grad, bi,
            self.outer_grad, bu,
        )


def per_device(*args):
    layer = Layer(*args)
    for step, us in ORDER:
        layer.run.us = us
        name = step.rstrip("0123456789")
        result = getattr(layer, name)(*(int(digit) for digit in step[len(name) :]))
    return result


def solution(mesh):
    in_specs = (
        P(None, "tm", None),
        P(None, "tm", None),
        P(),
        P(None, "head"),
        P("head"),
        P(None, "head"),
        P(None, "head"),
        P("head"),
        P("head", None),
        P(),
        P(),
        P(),
        P(),
        P(),
        P(None, "head"),
        P("head"),
        P("head", None),
        P(),
    )
    out_specs = (
        P(None, "tm", None),
        P(None, "tm", None),
        P(None, "head"),
        P("head"),
        P(None, "head"),
        P(None, "head"),
        P("head"),
        P("head", None),
        P(),
        P(),
        P(),
        P(),
        P(),
        P(None, "head"),
        P("head"),
        P("head", None),
        P(),
    )
    return jax.shard_map(
        per_device, mesh=mesh, in_specs=in_specs, out_specs=out_specs, check_vma=False
    )
```

profile of v0, /device:TPU:0, one launch (start us, length us, event | category | flops | bytes accessed | tf_op | source)
XLA Modules:
  0.0 138.9 jit_solution(12462195586088404168)
XLA Ops:
  2.6 4.4 %collective-permute-start.1 = (f32[2,64,512]{2,1,0:T(8,128)S(1)}, f32[2,64,512]{2,1,0:T(8,128)S(1)}, u32[]{:S(2)}, u32[]{:S(2)}) collective-permute-start(f32[2,64,512]{2,1,0:T(8,128)S(1)} %get-tuple-element.131.refs_7_), channel_id=1, source_target_pairs={{0,4},{2,6},{4,8},{5,1},{6,10},{7,3},{8,12},{9,5},{10,14},{11,7},{... | collective-permute-start | bytes 786440 | tf_op jit(solution)/shard_map/ppermute | solution.py:681
  7.0 2.5 %norm.1 = (f32[2,256,512]{2,1,0:T(8,128)S(1)}, f32[2,256,512]{2,1,0:T(8,128)S(1)}, f32[2,256,128]{2,1,0:T(8,128)S(1)}, f32[2,256,512]{2,1,0:T(8,128)S(1)}, f32[5...) custom-call(f32[2,512,512]{2,1,0:T(8,128)} %refs_0_.6, ...), custom_call_target="tpu_custom_call" | custom-call | flops 2486400000 | tf_op jit(solution)/shard_map/norm/pallas_call | solution.py:118
  13.5 3.7 %attend_inner.1 = (f32[2,128,256]{2,1,0:T(8,128)S(1)}, f32[2,2,2,128,128]{4,3,2,1,0:T(8,128)S(1)}) custom-call(s32[2,4]{1,0:T(2,128)S(1)} %copy-done, f32[2,256,256]{2,1,0:T(8,128)S(1)} %get-tuple-element.135.refs_1_.refs_6_, f32[2,256,512]{2,1,0:T(8,128)S(1)} %get-tuple-element.136.refs_2_.refs_7_, ...), custom_call_target="tpu_custom_call" | custom-call | flops 5697999872 | tf_op jit(solution)/shard_map/attend_inner/pallas_call | solution.py:118
  18.3 2.1 %attend_outer.2 = (f32[256,256]{1,0:T(8,128)S(1)}, f32[2,2,128,128]{3,2,1,0:T(8,128)S(1)}) custom-call(s32[2,4]{1,0:T(2,128)S(1)} %copy-done, f32[2,256,256]{2,1,0:T(8,128)S(1)} %get-tuple-element.135.refs_1_.refs_6_, f32[2,256,512]{2,1,0:T(8,128)S(1)} %get-tuple-element.136.refs_2_.refs_7_, f32[2,72,512]{2,1,0:T(8,128)S(1)} %get-tuple-element.142.refs_3_.refs_8_, ...), custom_call_target="tpu_custom_call" | custom-call | flops 12432000000 | tf_op jit(solution)/shard_map/attend_outer/pallas_call | solution.py:118
  24.6 5.0 %collective-permute-done.3.refs_1_ = f32[256,256]{1,0:T(8,128)S(1)} collective-permute-done((f32[256,256]{1,0:T(8,128)S(1)}, f32[256,256]{1,0:T(8,128)S(1)}, u32[]{:S(2)}, u32[]{:S(2)}) %collective-permute-start.3) | collective-permute-done | bytes 262176 | tf_op jit(solution)/shard_map/ppermute | solution.py:666
  29.6 3.8 %feed.2 = (f32[256,512]{1,0:T(8,128)S(1)}, f32[256,1024]{1,0:T(8,128)S(1)}, f32[256,1024]{1,0:T(8,128)S(1)}, f32[256,512]{1,0:T(8,128)S(1)}, f32[256,512]{1,0:T(8,128)S(1)}) custom-call(f32[256,256]{1,0:T(8,128)S(1)} %get-tuple-element.146.refs_0_.refs_5_, f32[256,256]{1,0:T(8,128)S(1)} %collective-permute-done.3.refs_1_, ...), custom_call_target="tpu_custom_call" | custom-call | flops 9324000256 | tf_op jit(solution)/shard_map/feed/pallas_call | solution.py:118
  34.3 4.0 %feed.3 = (f32[256,512]{1,0:T(8,128)S(1)}, f32[256,1024]{1,0:T(8,128)S(1)}, f32[256,1024]{1,0:T(8,128)S(1)}, f32[256,512]{1,0:T(8,128)S(1)}, f32[256,512]{1,0:T(8,128)S(1)}) custom-call(f32[256,256]{1,0:T(8,128)S(1)} %get-tuple-element.155.refs_0_.refs_5_, f32[256,256]{1,0:T(8,128)S(1)} %collective-permute-done.7.refs_1_, ...), custom_call_target="tpu_custom_call" | custom-call | flops 7251999744 | tf_op jit(solution)/shard_map/feed/pallas_call | solution.py:118
  50.5 4.5 %back.2 = (f32[256,512]{1,0:T(8,128)S(1)}, f32[256,256]{1,0:T(8,128)S(1)}, f32[328,512]{1,0:T(8,128)S(1)}, f32[512,128]{1,0:T(8,128)S(1)}, f32[512,128]{1,0:T(8,128)S(1)}, /*index=5*/f32[3,512]{1,0:T(4,128)S(1)}) custom-call(f32[256,512]{1,0:T(8,128)S(1)} %grad_sum.2.refs_4_.refs_0_, f32[256,512]{1,0:T(8,128)S(1)} %get-tuple-element.154.refs_1_.refs_0_, ...), custom_call_target="tpu_custom_call" | custom-call | flops 3108000000 | tf_op jit(solution)/shard_map/back/pallas_call | solution.py:118
  55.0 2.5 %collective-permute-done.12.refs_1_ = f32[256,512]{1,0:T(8,128)S(1)} collective-permute-done((f32[256,512]{1,0:T(8,128)S(1)}, f32[256,512]{1,0:T(8,128)S(1)}, u32[]{:S(2)}, u32[]{:S(2)}) %collective-permute-start.12) | collective-permute-done | bytes 524320 | tf_op jit(solution)/shard_map/ppermute | solution.py:666
  57.6 4.3 %back.3 = (f32[256,512]{1,0:T(8,128)S(1)}, f32[256,256]{1,0:T(8,128)S(1)}, f32[328,512]{1,0:T(8,128)S(1)}, f32[512,128]{1,0:T(8,128)S(1)}, f32[512,128]{1,0:T(8,128)S(1)}, /*index=5*/f32[3,512]{1,0:T(4,128)S(1)}) custom-call(f32[256,512]{1,0:T(8,128)S(1)} %grad_sum.3.refs_0_.refs_11_, f32[256,512]{1,0:T(8,128)S(1)} %get-tuple-element.158.refs_1_, ...), custom_call_target="tpu_custom_call" | custom-call | flops 259000000 | tf_op jit(solution)/shard_map/back/pallas_call | solution.py:118
  67.9 2.6 %project_weights.1 = (f32[256,512]{1,0:T(8,128)S(1)}, f32[256,512]{1,0:T(8,128)S(1)}, f32[8,512]{1,0:T(8,128)S(1)}, f32[264,512]{1,0:T(8,128)S(1)}, f32[256,512]{1,0:T(8,128)S(1)}) custom-call(f32[2,256,512]{2,1,0:T(8,128)S(1)} %get-tuple-element.132.refs_0_, f32[2,72,512]{2,1,0:T(8,128)S(1)} %get-tuple-element.191.refs_1_, ...), custom_call_target="tpu_custom_call" | custom-call | flops 1036000000 | tf_op jit(solution)/shard_map/project_weights/pallas_call | solution.py:118
  70.5 2.1 %collective-permute-start.20 = (f32[264,512]{1,0:T(8,128)S(1)}, f32[264,512]{1,0:T(8,128)S(1)}, u32[]{:S(2)}, u32[]{:S(2)}) collective-permute-start(f32[264,512]{1,0:T(8,128)S(1)} %get-tuple-element.201), channel_id=1, source_target_pairs={{0,1},{1,0},{2,3},{3,2},{4,5},{5,4},{6,7},{7,6},{8,9},{9,8},{10,11... | collective-permute-start | bytes 1622024 | tf_op jit(solution)/shard_map/ppermute | solution.py:666
  72.7 2.7 %collective-permute-start.27 = (f32[256,512]{1,0:T(8,128)S(1)}, f32[256,512]{1,0:T(8,128)S(1)}, u32[]{:S(2)}, u32[]{:S(2)}) collective-permute-start(f32[256,512]{1,0:T(8,128)S(1)} %stack.2.refs_3_.refs_0_), channel_id=1, source_target_pairs={{0,16},{4,20},{8,24},{12,28},{16,0},{20,4},{24,8},{28,12},{1,17},{... | collective-permute-start | bytes 1572872 | tf_op jit(solution)/shard_map/ppermute | solution.py:666
  76.6 3.1 %collective-permute-done.8.refs_3_ = f32[512,512]{1,0:T(8,128)S(1)} collective-permute-done((f32[512,512]{1,0:T(8,128)S(1)}, f32[512,512]{1,0:T(8,128)S(1)}, u32[]{:S(2)}, u32[]{:S(2)}) %collective-permute-start.8) | collective-permute-done | bytes 1048608 | tf_op jit(solution)/shard_map/ppermute | solution.py:666
  81.5 2.2 %collective-permute-start.24 = (f32[128,512]{1,0:T(8,128)S(1)}, f32[128,512]{1,0:T(8,128)S(1)}, u32[]{:S(2)}, u32[]{:S(2)}) collective-permute-start(f32[128,512]{1,0:T(8,128)S(1)} %get-tuple-element.210), channel_id=1, source_target_pairs={{0,4},{4,0},{8,12},{12,8},{16,20},{20,16},{24,28},{28,24},{1,5},{5... | collective-permute-start | bytes 786440 | tf_op jit(solution)/shard_map/ppermute | solution.py:666
  85.1 5.3 %collective-permute-done.24.refs_4_ = f32[128,512]{1,0:T(8,128)S(1)} collective-permute-done((f32[128,512]{1,0:T(8,128)S(1)}, f32[128,512]{1,0:T(8,128)S(1)}, u32[]{:S(2)}, u32[]{:S(2)}) %collective-permute-start.24) | collective-permute-done | bytes 262176 | tf_op jit(solution)/shard_map/ppermute | solution.py:666
  90.4 9.3 %collective-permute-done.23.refs_3_ = f32[136,512]{1,0:T(8,128)S(1)} collective-permute-done((f32[136,512]{1,0:T(8,128)S(1)}, f32[136,512]{1,0:T(8,128)S(1)}, u32[]{:S(2)}, u32[]{:S(2)}) %collective-permute-start.23) | collective-permute-done | bytes 278560 | tf_op jit(solution)/shard_map/ppermute | solution.py:666
  104.0 2.5 %collective-permute-done.26.refs_4_ = f32[64,512]{1,0:T(8,128)S(1)} collective-permute-done((f32[64,512]{1,0:T(8,128)S(1)}, f32[64,512]{1,0:T(8,128)S(1)}, u32[]{:S(2)}, u32[]{:S(2)}) %collective-permute-start.26) | collective-permute-done | bytes 131104 | tf_op jit(solution)/shard_map/ppermute | solution.py:666
  106.5 2.8 %collective-permute-start.31 = (f32[136,512]{1,0:T(8,128)S(1)}, f32[136,512]{1,0:T(8,128)S(1)}, u32[]{:S(2)}, u32[]{:S(2)}) collective-permute-start(f32[136,512]{1,0:T(8,128)S(1)} %stack.3.refs_7_.refs_0_), channel_id=1, source_target_pairs={{0,16},{4,20},{8,24},{12,28},{16,0},{20,4},{24,8},{28,12},{1,17},{... | collective-permute-start | bytes 835592 | tf_op jit(solution)/shard_map/ppermute | solution.py:666
  110.0 3.8 %collective-permute-done.30.refs_3_ = f32[128,512]{1,0:T(8,128)S(1)} collective-permute-done((f32[128,512]{1,0:T(8,128)S(1)}, f32[128,512]{1,0:T(8,128)S(1)}, u32[]{:S(2)}, u32[]{:S(2)}) %collective-permute-start.30) | collective-permute-done | bytes 262176 | tf_op jit(solution)/shard_map/ppermute | solution.py:666
  116.8 2.1 %collective-permute-done.31.refs_1_ = f32[136,512]{1,0:T(8,128)S(1)} collective-permute-done((f32[136,512]{1,0:T(8,128)S(1)}, f32[136,512]{1,0:T(8,128)S(1)}, u32[]{:S(2)}, u32[]{:S(2)}) %collective-permute-start.31) | collective-permute-done | bytes 278560 | tf_op jit(solution)/shard_map/ppermute | solution.py:666
  120.5 2.3 %collective-permute-start.34 = (f32[64,512]{1,0:T(8,128)S(1)}, f32[64,512]{1,0:T(8,128)S(1)}, u32[]{:S(2)}, u32[]{:S(2)}) collective-permute-start(f32[64,512]{1,0:T(8,128)S(1)} %get-tuple-element.224.refs_1_), channel_id=1, source_target_pairs={{0,8},{4,12},{8,0},{12,4},{16,24},{20,28},{24,16},{28,20},{1,9},{5... | collective-permute-start | bytes 393224 | tf_op jit(solution)/shard_map/ppermute | solution.py:666
  122.8 6.7 %collective-permute-done.33.refs_2_ = f32[64,512]{1,0:T(8,128)S(1)} collective-permute-done((f32[64,512]{1,0:T(8,128)S(1)}, f32[64,512]{1,0:T(8,128)S(1)}, u32[]{:S(2)}, u32[]{:S(2)}) %collective-permute-start.33) | collective-permute-done | bytes 131104 | tf_op jit(solution)/shard_map/ppermute | solution.py:666
  131.9 3.8 %collective-permute-start.32 = (f32[8,512]{1,0:T(8,128)S(1)}, f32[8,512]{1,0:T(8,128)S(1)}, u32[]{:S(2)}, u32[]{:S(2)}) collective-permute-start(f32[8,512]{1,0:T(8,128)S(1)} %get-tuple-element.222.refs_4_.refs_0_), channel_id=1, source_target_pairs={{0,2},{1,3},{2,0},{3,1},{4,6},{5,7},{6,4},{7,5},{8,10},{9,11},{10,... | collective-permute-start | bytes 49160 | tf_op jit(solution)/shard_map/ppermute | solution.py:666
  (94 shorter events, 49.6 us)
Async XLA Ops:
  2.1 9.5 %collective-permute-start = (f32[520,512]{1,0:T(8,128)S(1)}, f32[520,512]{1,0:T(8,128)S(1)}, u32[]{:S(2)}, u32[]{:S(2)}) collective-permute-start(f32[520,512]{1,0:T(8,128)S(1)} %get-tuple-element.133.refs_1_.refs_0_), channel_id=1, source_target_pairs={{0,1},{1,0},{2,3},{3,2},{4,5},{5,4},{6,7},{7,6},{8,9},{9,8},{10,11... | collective-permute-start | bytes 3194888 | tf_op jit(solution)/shard_map/ppermute | solution.py:666
  2.6 14.7 %collective-permute-start.1 = (f32[2,64,512]{2,1,0:T(8,128)S(1)}, f32[2,64,512]{2,1,0:T(8,128)S(1)}, u32[]{:S(2)}, u32[]{:S(2)}) collective-permute-start(f32[2,64,512]{2,1,0:T(8,128)S(1)} %get-tuple-element.131.refs_7_), channel_id=1, source_target_pairs={{0,4},{2,6},{4,8},{5,1},{6,10},{7,3},{8,12},{9,5},{10,14},{11,7},{... | collective-permute-start | bytes 786440 | tf_op jit(solution)/shard_map/ppermute | solution.py:681
  11.1 13.5 %collective-permute-start.6 = (f32[512,512]{1,0:T(8,128)S(1)}, f32[512,512]{1,0:T(8,128)S(1)}, u32[]{:S(2)}, u32[]{:S(2)}) collective-permute-start(f32[512,512]{1,0:T(8,128)S(1)} %get-tuple-element.151.refs_11_.refs_2_), channel_id=1, source_target_pairs={{0,1},{1,0},{2,3},{3,2},{4,5},{5,4},{6,7},{7,6},{8,9},{9,8},{10,11... | collective-permute-start | bytes 3145736 | tf_op jit(solution)/shard_map/ppermute | solution.py:666
  11.1 13.5 %collective-permute-start.5 = (f32[512,512]{1,0:T(8,128)S(1)}, f32[512,512]{1,0:T(8,128)S(1)}, u32[]{:S(2)}, u32[]{:S(2)}) collective-permute-start(f32[512,512]{1,0:T(8,128)S(1)} %get-tuple-element.150.refs_9_), channel_id=1, source_target_pairs={{0,1},{1,0},{2,3},{3,2},{4,5},{5,4},{6,7},{7,6},{8,9},{9,8},{10,11... | collective-permute-start | bytes 3145736 | tf_op jit(solution)/shard_map/ppermute | solution.py:666
  20.4 9.2 %collective-permute-start.3 = (f32[256,256]{1,0:T(8,128)S(1)}, f32[256,256]{1,0:T(8,128)S(1)}, u32[]{:S(2)}, u32[]{:S(2)}) collective-permute-start(f32[256,256]{1,0:T(8,128)S(1)} %get-tuple-element.146.refs_0_.refs_5_), channel_id=1, source_target_pairs={{0,2},{1,3},{2,0},{3,1},{4,6},{5,7},{6,4},{7,5},{8,10},{9,11},{10,... | collective-permute-start | bytes 786440 | tf_op jit(solution)/shard_map/ppermute | solution.py:666
  23.0 11.3 %collective-permute-start.7 = (f32[256,256]{1,0:T(8,128)S(1)}, f32[256,256]{1,0:T(8,128)S(1)}, u32[]{:S(2)}, u32[]{:S(2)}) collective-permute-start(f32[256,256]{1,0:T(8,128)S(1)} %get-tuple-element.155.refs_0_.refs_5_), channel_id=1, source_target_pairs={{0,2},{1,3},{2,0},{3,1},{4,6},{5,7},{6,4},{7,5},{8,10},{9,11},{10,... | collective-permute-start | bytes 786440 | tf_op jit(solution)/shard_map/ppermute | solution.py:666
  33.5 13.4 %collective-permute-start.9 = (f32[256,512]{1,0:T(8,128)S(1)}, f32[256,512]{1,0:T(8,128)S(1)}, u32[]{:S(2)}, u32[]{:S(2)}) collective-permute-start(f32[256,512]{1,0:T(8,128)S(1)} %get-tuple-element.157.refs_13_.refs_0_), channel_id=1, source_target_pairs={{0,2},{1,3},{2,0},{3,1},{4,6},{5,7},{6,4},{7,5},{8,10},{9,11},{10,... | collective-permute-start | bytes 1572872 | tf_op jit(solution)/shard_map/ppermute | solution.py:666
  42.7 14.8 %collective-permute-start.12 = (f32[256,512]{1,0:T(8,128)S(1)}, f32[256,512]{1,0:T(8,128)S(1)}, u32[]{:S(2)}, u32[]{:S(2)}) collective-permute-start(f32[256,512]{1,0:T(8,128)S(1)} %get-tuple-element.165.refs_4_.refs_0_), channel_id=1, source_target_pairs={{0,2},{1,3},{2,0},{3,1},{4,6},{5,7},{6,4},{7,5},{8,10},{9,11},{10,... | collective-permute-start | bytes 1572872 | tf_op jit(solution)/shard_map/ppermute | solution.py:666
  46.1 33.7 %collective-permute-start.8 = (f32[512,512]{1,0:T(8,128)S(1)}, f32[512,512]{1,0:T(8,128)S(1)}, u32[]{:S(2)}, u32[]{:S(2)}) collective-permute-start(f32[512,512]{1,0:T(8,128)S(1)} %feed_out.1.refs_2_), channel_id=1, source_target_pairs={{0,2},{1,3},{2,0},{3,1},{4,6},{5,7},{6,4},{7,5},{8,10},{9,11},{10,... | collective-permute-start | bytes 3145736 | tf_op jit(solution)/shard_map/ppermute | solution.py:666
  47.3 14.6 %collective-permute-start.13 = (f32[256,512]{1,0:T(8,128)S(1)}, f32[256,512]{1,0:T(8,128)S(1)}, u32[]{:S(2)}, u32[]{:S(2)}) collective-permute-start(f32[256,512]{1,0:T(8,128)S(1)} %get-tuple-element.182), channel_id=1, source_target_pairs={{0,8},{4,12},{8,0},{12,4},{16,24},{20,28},{24,16},{28,20},{1,9},{5... | collective-permute-start | bytes 1572872 | tf_op jit(solution)/shard_map/ppermute | solution.py:666
  49.2 13.1 %collective-permute-start.14 = (f32[256,512]{1,0:T(8,128)S(1)}, f32[256,512]{1,0:T(8,128)S(1)}, u32[]{:S(2)}, u32[]{:S(2)}) collective-permute-start(f32[256,512]{1,0:T(8,128)S(1)} %get-tuple-element.172.refs_11_), channel_id=1, source_target_pairs={{0,4},{4,0},{8,12},{12,8},{16,20},{20,16},{24,28},{28,24},{1,5},{5... | collective-permute-start | bytes 1572872 | tf_op jit(solution)/shard_map/ppermute | solution.py:666
  63.8 8.7 %collective-permute-start.18 = (f32[128,512]{1,0:T(8,128)S(1)}, f32[128,512]{1,0:T(8,128)S(1)}, u32[]{:S(2)}, u32[]{:S(2)}) collective-permute-start(f32[128,512]{1,0:T(8,128)S(1)} %get-tuple-element.184.refs_7_), channel_id=1, source_target_pairs={{0,8},{4,12},{8,0},{12,4},{16,24},{20,28},{24,16},{28,20},{1,9},{5... | collective-permute-start | bytes 786440 | tf_op jit(solution)/shard_map/ppermute | solution.py:666
  70.5 9.7 %collective-permute-start.20 = (f32[264,512]{1,0:T(8,128)S(1)}, f32[264,512]{1,0:T(8,128)S(1)}, u32[]{:S(2)}, u32[]{:S(2)}) collective-permute-start(f32[264,512]{1,0:T(8,128)S(1)} %get-tuple-element.201), channel_id=1, source_target_pairs={{0,1},{1,0},{2,3},{3,2},{4,5},{5,4},{6,7},{7,6},{8,9},{9,8},{10,11... | collective-permute-start | bytes 1622024 | tf_op jit(solution)/shard_map/ppermute | solution.py:666
  72.7 28.4 %collective-permute-start.27 = (f32[256,512]{1,0:T(8,128)S(1)}, f32[256,512]{1,0:T(8,128)S(1)}, u32[]{:S(2)}, u32[]{:S(2)}) collective-permute-start(f32[256,512]{1,0:T(8,128)S(1)} %stack.2.refs_3_.refs_0_), channel_id=1, source_target_pairs={{0,16},{4,20},{8,24},{12,28},{16,0},{20,4},{24,8},{28,12},{1,17},{... | collective-permute-start | bytes 1572872 | tf_op jit(solution)/shard_map/ppermute | solution.py:666
  75.5 33.9 %collective-permute-start.22 = (f32[512,512]{1,0:T(8,128)S(1)}, f32[512,512]{1,0:T(8,128)S(1)}, u32[]{:S(2)}, u32[]{:S(2)}) collective-permute-start(f32[512,512]{1,0:T(8,128)S(1)} %edge_add.1.refs_5_.refs_0_), channel_id=1, source_target_pairs={{0,2},{1,3},{2,0},{3,1},{4,6},{5,7},{6,4},{7,5},{8,10},{9,11},{10,... | collective-permute-start | bytes 3145736 | tf_op jit(solution)/shard_map/ppermute | solution.py:666
  80.3 19.4 %collective-permute-start.23 = (f32[136,512]{1,0:T(8,128)S(1)}, f32[136,512]{1,0:T(8,128)S(1)}, u32[]{:S(2)}, u32[]{:S(2)}) collective-permute-start(f32[136,512]{1,0:T(8,128)S(1)} %get-tuple-element.209), channel_id=1, source_target_pairs={{0,8},{4,12},{8,0},{12,4},{16,24},{20,28},{24,16},{28,20},{1,9},{5... | collective-permute-start | bytes 835592 | tf_op jit(solution)/shard_map/ppermute | solution.py:666
  81.5 8.9 %collective-permute-start.24 = (f32[128,512]{1,0:T(8,128)S(1)}, f32[128,512]{1,0:T(8,128)S(1)}, u32[]{:S(2)}, u32[]{:S(2)}) collective-permute-start(f32[128,512]{1,0:T(8,128)S(1)} %get-tuple-element.210), channel_id=1, source_target_pairs={{0,4},{4,0},{8,12},{12,8},{16,20},{20,16},{24,28},{28,24},{1,5},{5... | collective-permute-start | bytes 786440 | tf_op jit(solution)/shard_map/ppermute | solution.py:666
  101.2 8.8 %collective-permute-start.29 = (f32[128,512]{1,0:T(8,128)S(1)}, f32[128,512]{1,0:T(8,128)S(1)}, u32[]{:S(2)}, u32[]{:S(2)}) collective-permute-start(f32[128,512]{1,0:T(8,128)S(1)} %get-tuple-element.218.refs_0_), channel_id=1, source_target_pairs={{0,4},{4,0},{8,12},{12,8},{16,20},{20,16},{24,28},{28,24},{1,5},{5... | collective-permute-start | bytes 786440 | tf_op jit(solution)/shard_map/ppermute | solution.py:666
  102.0 11.9 %collective-permute-start.30 = (f32[128,512]{1,0:T(8,128)S(1)}, f32[128,512]{1,0:T(8,128)S(1)}, u32[]{:S(2)}, u32[]{:S(2)}) collective-permute-start(f32[128,512]{1,0:T(8,128)S(1)} %get-tuple-element.217.refs_5_.refs_1_), channel_id=1, source_target_pairs={{0,8},{4,12},{8,0},{12,4},{16,24},{20,28},{24,16},{28,20},{1,9},{5... | collective-permute-start | bytes 786440 | tf_op jit(solution)/shard_map/ppermute | solution.py:666
  106.5 12.3 %collective-permute-start.31 = (f32[136,512]{1,0:T(8,128)S(1)}, f32[136,512]{1,0:T(8,128)S(1)}, u32[]{:S(2)}, u32[]{:S(2)}) collective-permute-start(f32[136,512]{1,0:T(8,128)S(1)} %stack.3.refs_7_.refs_0_), channel_id=1, source_target_pairs={{0,16},{4,20},{8,24},{12,28},{16,0},{20,4},{24,8},{28,12},{1,17},{... | collective-permute-start | bytes 835592 | tf_op jit(solution)/shard_map/ppermute | solution.py:666
  113.9 21.8 %collective-permute-start.38 = (f32[256,512]{1,0:T(8,128)S(1)}, f32[256,512]{1,0:T(8,128)S(1)}, u32[]{:S(2)}, u32[]{:S(2)}) collective-permute-start(f32[256,512]{1,0:T(8,128)S(1)} %get-tuple-element.227.refs_0_), channel_id=1, source_target_pairs={{0,8},{4,12},{8,0},{12,4},{16,24},{20,28},{24,16},{28,20},{1,9},{5... | collective-permute-start | bytes 1572872 | tf_op jit(solution)/shard_map/ppermute | solution.py:666
  114.0 22.7 %collective-permute-start.37 = (f32[256,512]{1,0:T(8,128)S(1)}, f32[256,512]{1,0:T(8,128)S(1)}, u32[]{:S(2)}, u32[]{:S(2)}) collective-permute-start(f32[256,512]{1,0:T(8,128)S(1)} %get-tuple-element.219.refs_2_.refs_0_), channel_id=1, source_target_pairs={{0,4},{4,0},{8,12},{12,8},{16,20},{20,16},{24,28},{28,24},{1,5},{5... | collective-permute-start | bytes 1572872 | tf_op jit(solution)/shard_map/ppermute | solution.py:666
  118.9 10.6 %collective-permute-start.33 = (f32[64,512]{1,0:T(8,128)S(1)}, f32[64,512]{1,0:T(8,128)S(1)}, u32[]{:S(2)}, u32[]{:S(2)}) collective-permute-start(f32[64,512]{1,0:T(8,128)S(1)} %get-tuple-element.223.refs_0_), channel_id=1, source_target_pairs={{0,4},{4,0},{8,12},{12,8},{16,20},{20,16},{24,28},{28,24},{1,5},{5... | collective-permute-start | bytes 393224 | tf_op jit(solution)/shard_map/ppermute | solution.py:666
  120.5 9.0 %collective-permute-start.34 = (f32[64,512]{1,0:T(8,128)S(1)}, f32[64,512]{1,0:T(8,128)S(1)}, u32[]{:S(2)}, u32[]{:S(2)}) collective-permute-start(f32[64,512]{1,0:T(8,128)S(1)} %get-tuple-element.224.refs_1_), channel_id=1, source_target_pairs={{0,8},{4,12},{8,0},{12,4},{16,24},{20,28},{24,16},{28,20},{1,9},{5... | collective-permute-start | bytes 393224 | tf_op jit(solution)/shard_map/ppermute | solution.py:666
  (16 other events, 100.7 us)
where the time goes:
time: 141 us; the launch traced here: 139 us
  Pallas kernels  49.6 us (35%)
  starting transfers between devices  47.3 us (34%)
  waiting for transfers between devices  40.9 us (29%)
    pallas_call x38, Pallas kernels, call(): pl.pallas_call(body, name=name, grid=(1,), in_specs=[in_hbm if i in far e...  49.6 us
    ppermute x37, starting transfers between devices, swap(): return lax.ppermute(value, axis, [(i, i ^ bit) for i in range(size)])  42.2 us
    ppermute x37, waiting for transfers between devices, swap(): return lax.ppermute(value, axis, [(i, i ^ bit) for i in range(size)])  40.9 us
    ppermute x2, starting transfers between devices, swap_edges(): return lax.ppermute(value, ('tm', 'head'), pairs)  5.1 us
  transfers between devices with their start and end apart: 39, of which 11 were waited for; matrix products, arithmetic and copies ran while one was open for 0% of the time, Pallas kernels for 34%

commit v1 on v0

--- a/solution.py
+++ b/solution.py
@@ -300,10 +300,10 @@
         put(lanes, side_by_side(mm(weights, key_window(kx, sx, block, value_lanes))))
 
 
-def attend_inner_kernel(counts, q_ref, kv_ref, mix_ref, p_ref, kx, sx):
-    micros, length, _ = q_ref.shape
+def attend_inner_kernel(counts, q_ref, kv_ref, mix_0, mix_1, p_ref, kx, sx):
+    _, length, _ = q_ref.shape
     base = first_segment(length)
-    for micro in range(micros):
+    for micro, mix_ref in enumerate((mix_0, mix_1)):
         fill_keys(kv_ref[micro], None, kx, sx)
         bounds = bounds_of(counts, micro)
         for number, block in enumerate(range(1, length // BLOCK - 1)):
@@ -311,33 +311,39 @@
                 p_ref[micro, number, pair] = weights
 
             def put(lanes, values):
-                mix_ref[micro, block_rows(number), lanes] = values
+                mix_ref[block_rows(number), lanes] = values
 
             seen = visible(block, base, bounds)
             attend_block(block, seen, q_ref[micro, block_rows(block)], kx, sx, keep, put)
 
 
-def attend_outer_kernel(micro, counts, q_ref, kv_ref, edge, inner, mix_ref, p_ref, kx, sx):
+def attend_outer_kernel(micro, counts, q_ref, kv_ref, edge, mix_ref, p_ref, kx, sx):
     _, length, _ = q_ref.shape
     base = first_segment(length)
     fill_keys(kv_ref[micro], edge[micro], kx, sx)
     bounds = bounds_of(counts, micro)
-    mix_ref[BLOCK : length - BLOCK] = inner[micro]
     for number, block in enumerate((0, length // BLOCK - 1)):
         def keep(pair, weights):
             p_ref[number, pair] = weights
 
         def put(lanes, values):
-            mix_ref[block_rows(block), lanes] = values
+            mix_ref[block_rows(number), lanes] = values
 
         seen = visible(block, base, bounds)
         attend_block(block, seen, q_ref[micro, block_rows(block)], kx, sx, keep, put)
 
 
+def fill_rows(target, lanes, inner, outer):
+    length = inner.shape[0] + outer.shape[0]
+    target[:BLOCK, lanes] = outer[:BLOCK]
+    target[BLOCK : length - BLOCK, lanes] = inner[...]
+    target[length - BLOCK : length, lanes] = outer[BLOCK:]
+
+
 def back_kernel(
-    micro, grad_ref, mid_ref, g_ref, params, wo_here, mix, q_ref, kv_ref, edge, p_inner, p_outer,
+    micro, grad_ref, mid_ref, g_ref, params, wo_here, mix_inner, mix_outer, q_ref, kv_ref, edge, p_inner, p_outer,
     dmid_ref, dq_ref, dkv_ref, dwo_own, dwo_pair, vec_ref,
-    kx, sx, dsx, dmix, dwo,
+    kx, sx, dsx, dmix, mix, dwo,
 ):
     _, length, width = q_ref.shape
     near_width = dwo_own.shape[1]
@@ -349,6 +355,7 @@
     vec_ref[1:2] = column_sums(grad * xhat)
     vec_ref[2:3] = column_sums(grad)
     dmix[...] = mm(dmid, wo_here[...], 1, 1)
+    fill_rows(mix, slice(None), mix_inner, mix_outer)
     dwo[...] = mm(dmid, mix[...], 0, 0)
     dwo_own[...] = dwo[:, lanes_of(0, near_width)]
     dwo_pair[...] = dwo[:, lanes_of(1, near_width)]
@@ -382,17 +389,17 @@
 
 
 def feed_kernel(
-    micro, mix_own, mix_far, wo_here, wo_far, wo_far_pair, x_ref, g_ref, params, pair, wi_own, wi_pair, wu_own, wu_pair,
+    micro, own_inner, own_outer, far_inner, far_outer, wo_here, wo_far, wo_far_pair, x_ref, g_ref, params, pair, wi_own, wi_pair, wu_own, wu_pair,
     n2_ref, h_ref, dpre_ref, mid_ref, part_ref,
     mix, wo,
 ):
-    width = mix_own.shape[1] // 2
+    width = own_inner.shape[1] // 2
     features, hidden = wi_own.shape
     far = far_bit()
     here = pl.multiple_of(far * 2 * width, 2 * width)
     there = pl.multiple_of((1 - far) * 2 * width, 2 * width)
-    mix[:, pl.ds(here, 2 * width)] = mix_own[...]
-    mix[:, pl.ds(there, 2 * width)] = mix_far[...]
+    fill_rows(mix, pl.ds(here, 2 * width), own_inner, own_outer)
+    fill_rows(mix, pl.ds(there, 2 * width), far_inner, far_outer)
     wo[pl.ds(here, 2 * width)] = wo_here[...]
     wo[lanes_of(0, width, there)] = wo_far[...]
     wo[lanes_of(1, width, there)] = wo_far_pair[...]
@@ -811,7 +818,7 @@
         self.run = Steps()
         self.smem = pl.BlockSpec(memory_space=pltpu.SMEM)
         pairs = [None] * micros
-        self.mix, self.mix_far, self.p_outer, self.fed, self.dn2 = (list(pairs) for _ in range(5))
+        self.mix_outer, self.far_outer, self.p_outer, self.fed, self.dn2 = (list(pairs) for _ in range(5))
         self.back_of = list(pairs)
         self.sums = {}
 
@@ -854,21 +861,23 @@
         )
 
     def attend_inner(self):
-        self.mix_inner, self.p_inner = self.run.call(
+        *self.mix_inner, self.p_inner = self.run.call(
             attend_inner_kernel, "attend_inner",
-            [(self.micros, self.length - 2 * BLOCK, 2 * self.width),
-             (self.micros, self.blocks - 2, self.pairs) + self.square],
+            [(self.length - 2 * BLOCK, 2 * self.width)] * 2 + [(self.micros, self.blocks - 2, self.pairs) + self.square],
             (self.counts, self.q, self.kv), {0: self.smem}, self.key_scratch,
         )
+        self.far_inner = [swap(v, "head", 2) for v in self.mix_inner]
 
     def attend_outer(self, m):
-        self.mix[m], self.p_outer[m] = self.run.call(
+        if m:
+            self.run.held.append(self.far_inner[0])
+        self.mix_outer[m], self.p_outer[m] = self.run.call(
             functools.partial(attend_outer_kernel, m), "attend_outer",
-            [(self.length, 2 * self.width), (2, self.pairs) + self.square],
-            (self.counts, self.q, self.kv, self.kv_edge, self.mix_inner),
+            [(2 * BLOCK, 2 * self.width), (2, self.pairs) + self.square],
+            (self.counts, self.q, self.kv, self.kv_edge),
             {0: self.smem}, self.key_scratch,
         )
-        self.mix_far[m] = swap(self.mix[m], "head", 2)
+        self.far_outer[m] = swap(self.mix_outer[m], "head", 2)
 
     def hand_on(self):
         shape = self.wo_far.shape
@@ -881,7 +890,7 @@
         big, features, hidden = self.big, self.features, self.hidden
         *self.fed[m], part = self.run.call(
             functools.partial(feed_kernel, m), "feed", [big, (self.length, 2 * hidden), (self.length, 2 * hidden), big, big],
-            (self.mix[m], self.mix_far[m], self.wo_here, self.wo_far, self.wo_far_pair, self.x, self.g[m], self.params,
+            (self.mix_inner[m], self.mix_outer[m], self.far_inner[m], self.far_outer[m], self.wo_here, self.wo_far, self.wo_far_pair, self.x, self.g[m], self.params,
              self.pair, self.wi, self.wi_pair, self.wu, self.wu_pair),
             scratch=[big, (features, features)],
         )
@@ -931,9 +940,9 @@
         self.back_of[m] = self.run.call(
             functools.partial(back_kernel, m), "back",
             [self.big, (length, 2 * width), (self.around, 4 * width), (features, width), (features, width), (3, features)],
-            (self.dn2[m], self.fed[m][3], self.g[m], self.params, self.wo_here, self.mix[m], self.q, self.kv,
+            (self.dn2[m], self.fed[m][3], self.g[m], self.params, self.wo_here, self.mix_inner[m], self.mix_outer[m], self.q, self.kv,
              self.kv_edge, self.p_inner, self.p_outer[m]),
-            scratch=self.key_scratch + self.key_scratch[1:] + [(length, 2 * width), (features, 2 * width)],
+            scratch=self.key_scratch + self.key_scratch[1:] + [(length, 2 * width)] * 2 + [(features, 2 * width)],
         )
 
     def pick(self, number):

time: 141 us -> 140 us (level)
  starting transfers between devices: 47.3 us -> 44.9 us
  waiting for transfers between devices: 40.9 us -> 43.3 us
    ppermute x37 -> x39, waiting for transfers between devices: 40.9 us -> 43.3 us  [swap(): return lax.ppermute(value, axis, [(i, i ^ bit) for i in range(size)])]
    ppermute x37 -> x39, starting transfers between devices: 42.2 us -> 39.8 us  [swap(): return lax.ppermute(value, axis, [(i, i ^ bit) for i in range(size)])]
  transfers between devices with their start and end apart: 39 -> 41, of which waited for: 11 -> 15; matrix products, arithmetic and copies ran while one was open for 0% -> 0% of each run, Pallas kernels for 34% -> 34%
where the time goes in v1:
time: 140 us; the launch traced here: 139 us
  Pallas kernels  49.6 us (35%)
  starting transfers between devices  44.9 us (32%)
  waiting for transfers between devices  43.3 us (31%)
    pallas_call x38, Pallas kernels, call(): pl.pallas_call(body, name=name, grid=(1,), in_specs=[in_hbm if i in far e...  49.6 us
    ppermute x39, waiting for transfers between devices, swap(): return lax.ppermute(value, axis, [(i, i ^ bit) for i in range(size)])  43.3 us
    ppermute x39, starting transfers between devices, swap(): return lax.ppermute(value, axis, [(i, i ^ bit) for i in range(size)])  39.8 us
    ppermute x2, starting transfers between devices, swap_edges(): return lax.ppermute(value, ('tm', 'head'), pairs)  5.1 us
  transfers between devices with their start and end apart: 41, of which 15 were waited for; matrix products, arithmetic and copies ran while one was open for 0% of the time, Pallas kernels for 34%

profile of v1, /device:TPU:0, one launch (start us, length us, event | category | flops | bytes accessed | tf_op | source)
XLA Modules:
  0.0 138.9 jit_solution(12735443692942868687)
XLA Ops:
  2.6 4.4 %collective-permute-start.1 = (f32[2,64,512]{2,1,0:T(8,128)S(1)}, f32[2,64,512]{2,1,0:T(8,128)S(1)}, u32[]{:S(2)}, u32[]{:S(2)}) collective-permute-start(f32[2,64,512]{2,1,0:T(8,128)S(1)} %get-tuple-element.132.refs_7_), channel_id=1, source_target_pairs={{0,4},{2,6},{4,8},{5,1},{6,10},{7,3},{8,12},{9,5},{10,14},{11,7},{... | collective-permute-start | bytes 786440 | tf_op jit(solution)/shard_map/ppermute | solution.py:688
  7.0 2.5 %norm.1 = (f32[2,256,512]{2,1,0:T(8,128)S(1)}, f32[2,256,512]{2,1,0:T(8,128)S(1)}, f32[2,256,128]{2,1,0:T(8,128)S(1)}, f32[2,256,512]{2,1,0:T(8,128)S(1)}, f32[5...) custom-call(f32[2,512,512]{2,1,0:T(8,128)} %refs_0_.6, ...), custom_call_target="tpu_custom_call" | custom-call | flops 2486400000 | tf_op jit(solution)/shard_map/norm/pallas_call | solution.py:118
  11.6 1.9 %project.1 = (f32[2,256,256]{2,1,0:T(8,128)S(1)}, f32[2,256,512]{2,1,0:T(8,128)S(1)}, f32[512,768]{1,0:T(8,128)S(1)}, f32[1,768]{1,0:T(1,128)S(1)}, f32[7,1,512]{2,1,0:T(1,128)S(1)}) custom-call(f32[2,256,512]{2,1,0:T(8,128)S(1)} %get-tuple-element.133.refs_0_, f32[520,512]{1,0:T(8,128)S(1)} %get-tuple-element.134.refs_1_.refs_0_, ...), custom_call_target="tpu_custom_call" | custom-call | flops 1139600000 | tf_op jit(solution)/shard_map/project/pallas_call | solution.py:118
  13.5 3.7 %attend_inner.1 = (f32[128,256]{1,0:T(8,128)S(1)}, f32[128,256]{1,0:T(8,128)S(1)}, f32[2,2,2,128,128]{4,3,2,1,0:T(8,128)S(1)}) custom-call(s32[2,4]{1,0:T(2,128)S(1)} %copy-done, f32[2,256,256]{2,1,0:T(8,128)S(1)} %get-tuple-element.136.refs_1_.refs_7_, f32[2,256,512]{2,1,0:T(8,128)S(1)} %get-tuple-element.137.refs_2_.refs_8_, ...), custom_call_target="tpu_custom_call" | custom-call | flops 5697999872 | tf_op jit(solution)/shard_map/attend_inner/pallas_call | solution.py:118
  19.0 2.1 %attend_outer.2 = (f32[128,256]{1,0:T(8,128)S(1)}, f32[2,2,128,128]{3,2,1,0:T(8,128)S(1)}) custom-call(s32[2,4]{1,0:T(2,128)S(1)} %copy-done, f32[2,256,256]{2,1,0:T(8,128)S(1)} %get-tuple-element.136.refs_1_.refs_7_, f32[2,256,512]{2,1,0:T(8,128)S(1)} %get-tuple-element.137.refs_2_.refs_8_, f32[2,72,512]{2,1,0:T(8,128)S(1)} %get-tuple-element.144.refs_3_.refs_9_, ...), custom_call_target="tpu_custom_call" | custom-call | flops 12432000000 | tf_op jit(solution)/shard_map/attend_outer/pallas_call | solution.py:118
  23.2 2.1 %attend_outer.3 = (f32[128,256]{1,0:T(8,128)S(1)}, f32[2,2,128,128]{3,2,1,0:T(8,128)S(1)}) custom-call(s32[2,4]{1,0:T(2,128)S(1)} %copy-done, f32[2,256,256]{2,1,0:T(8,128)S(1)} %get-tuple-element.136.refs_1_.refs_7_, f32[2,256,512]{2,1,0:T(8,128)S(1)} %get-tuple-element.137.refs_2_.refs_8_, f32[2,72,512]{2,1,0:T(8,128)S(1)} %get-tuple-element.144.refs_3_.refs_9_, ...), custom_call_target="tpu_custom_call" | custom-call | flops 518000000 | tf_op jit(solution)/shard_map/attend_outer/pallas_call | solution.py:118
  27.4 3.9 %feed.2 = (f32[256,512]{1,0:T(8,128)S(1)}, f32[256,1024]{1,0:T(8,128)S(1)}, f32[256,1024]{1,0:T(8,128)S(1)}, f32[256,512]{1,0:T(8,128)S(1)}, f32[256,512]{1,0:T(8,128)S(1)}) custom-call(f32[128,256]{1,0:T(8,128)S(1)} %get-tuple-element.139.refs_0_.refs_5_, f32[128,256]{1,0:T(8,128)S(1)} %get-tuple-element.147.refs_1_.refs_6_, ...), custom_call_target="tpu_custom_call" | custom-call | flops 9324000256 | tf_op jit(solution)/shard_map/feed/pallas_call | solution.py:118
  32.8 4.1 %feed.3 = (f32[256,512]{1,0:T(8,128)S(1)}, f32[256,1024]{1,0:T(8,128)S(1)}, f32[256,1024]{1,0:T(8,128)S(1)}, f32[256,512]{1,0:T(8,128)S(1)}, f32[256,512]{1,0:T(8,128)S(1)}) custom-call(f32[128,256]{1,0:T(8,128)S(1)} %get-tuple-element.156.refs_0_.refs_5_, f32[128,256]{1,0:T(8,128)S(1)} %get-tuple-element.157.refs_1_.refs_6_, ...), custom_call_target="tpu_custom_call" | custom-call | flops 7251999744 | tf_op jit(solution)/shard_map/feed/pallas_call | solution.py:118
  38.8 1.9 %inner_weights.1 = (f32[512,512]{1,0:T(8,128)S(1)}, f32[512,512]{1,0:T(8,128)S(1)}, f32[2,512]{1,0:T(2,128)S(1)}) custom-call(f32[256,512]{1,0:T(8,128)S(1)} %get-tuple-element.163.refs_0_, f32[256,512]{1,0:T(8,128)S(1)} %get-tuple-element.164.refs_1_, f32[256,1024]{1,0:T(8,128)S(1)} %get-tuple-element.165.refs_2_, ...), custom_call_target="tpu_custom_call" | custom-call | flops 5697999872 | tf_op jit(solution)/shard_map/inner_weights/pallas_call | solution.py:118
  42.6 2.0 %feed_out.1.refs_2_ = f32[512,512]{1,0:T(8,128)S(1)} custom-call(f32[256,1024]{1,0:T(8,128)S(1)} %get-tuple-element.161.refs_0_, f32[256,1024]{1,0:T(8,128)S(1)} %get-tuple-element.162.refs_1_, f32[512,512]{1,0:T(8,128)S(1)} %get-tuple-element.152.refs_13_.refs_2_, f32[512,512]{1,0:T(8,128)S(1)} %collective-permute-done.7.refs_14_.refs_3_, ...), custom_call_target="tpu_custom_call" | custom-call | flops 310800000 | tf_op jit(solution)/shard_map/feed_out/pallas_call | solution.py:118
  49.1 4.5 %back.2 = (f32[256,512]{1,0:T(8,128)S(1)}, f32[256,256]{1,0:T(8,128)S(1)}, f32[328,512]{1,0:T(8,128)S(1)}, f32[512,128]{1,0:T(8,128)S(1)}, f32[512,128]{1,0:T(8,128)S(1)}, /*index=5*/f32[3,512]{1,0:T(4,128)S(1)}) custom-call(f32[256,512]{1,0:T(8,128)S(1)} %grad_sum.2.refs_4_.refs_0_, f32[256,512]{1,0:T(8,128)S(1)} %get-tuple-element.155.refs_1_.refs_0_, ...), custom_call_target="tpu_custom_call" | custom-call | flops 3108000000 | tf_op jit(solution)/shard_map/back/pallas_call | solution.py:118
  53.6 2.5 %collective-permute-done.14.refs_1_ = f32[256,512]{1,0:T(8,128)S(1)} collective-permute-done((f32[256,512]{1,0:T(8,128)S(1)}, f32[256,512]{1,0:T(8,128)S(1)}, u32[]{:S(2)}, u32[]{:S(2)}) %collective-permute-start.14) | collective-permute-done | bytes 524320 | tf_op jit(solution)/shard_map/ppermute | solution.py:673
  56.2 4.3 %back.3 = (f32[256,512]{1,0:T(8,128)S(1)}, f32[256,256]{1,0:T(8,128)S(1)}, f32[328,512]{1,0:T(8,128)S(1)}, f32[512,128]{1,0:T(8,128)S(1)}, f32[512,128]{1,0:T(8,128)S(1)}, /*index=5*/f32[3,512]{1,0:T(4,128)S(1)}) custom-call(f32[256,512]{1,0:T(8,128)S(1)} %grad_sum.3.refs_0_.refs_12_, f32[256,512]{1,0:T(8,128)S(1)} %get-tuple-element.160.refs_1_, ...), custom_call_target="tpu_custom_call" | custom-call | flops 259000000 | tf_op jit(solution)/shard_map/back/pallas_call | solution.py:118
  66.5 2.6 %project_weights.1 = (f32[256,512]{1,0:T(8,128)S(1)}, f32[256,512]{1,0:T(8,128)S(1)}, f32[8,512]{1,0:T(8,128)S(1)}, f32[264,512]{1,0:T(8,128)S(1)}, f32[256,512]{1,0:T(8,128)S(1)}) custom-call(f32[2,256,512]{2,1,0:T(8,128)S(1)} %get-tuple-element.133.refs_0_, f32[2,72,512]{2,1,0:T(8,128)S(1)} %get-tuple-element.193.refs_1_, ...), custom_call_target="tpu_custom_call" | custom-call | flops 1036000000 | tf_op jit(solution)/shard_map/project_weights/pallas_call | solution.py:118
  69.1 1.9 %collective-permute-start.22 = (f32[264,512]{1,0:T(8,128)S(1)}, f32[264,512]{1,0:T(8,128)S(1)}, u32[]{:S(2)}, u32[]{:S(2)}) collective-permute-start(f32[264,512]{1,0:T(8,128)S(1)} %get-tuple-element.203), channel_id=1, source_target_pairs={{0,1},{1,0},{2,3},{3,2},{4,5},{5,4},{6,7},{7,6},{8,9},{9,8},{10,11... | collective-permute-start | bytes 1622024 | tf_op jit(solution)/shard_map/ppermute | solution.py:673
  71.1 2.6 %collective-permute-start.29 = (f32[256,512]{1,0:T(8,128)S(1)}, f32[256,512]{1,0:T(8,128)S(1)}, u32[]{:S(2)}, u32[]{:S(2)}) collective-permute-start(f32[256,512]{1,0:T(8,128)S(1)} %stack.2.refs_3_.refs_0_), channel_id=1, source_target_pairs={{0,16},{4,20},{8,24},{12,28},{16,0},{20,4},{24,8},{28,12},{1,17},{... | collective-permute-start | bytes 1572872 | tf_op jit(solution)/shard_map/ppermute | solution.py:673
  75.7 2.9 %collective-permute-done.10.refs_3_ = f32[512,512]{1,0:T(8,128)S(1)} collective-permute-done((f32[512,512]{1,0:T(8,128)S(1)}, f32[512,512]{1,0:T(8,128)S(1)}, u32[]{:S(2)}, u32[]{:S(2)}) %collective-permute-start.10) | collective-permute-done | bytes 1048608 | tf_op jit(solution)/shard_map/ppermute | solution.py:673
  80.4 2.0 %collective-permute-start.26 = (f32[128,512]{1,0:T(8,128)S(1)}, f32[128,512]{1,0:T(8,128)S(1)}, u32[]{:S(2)}, u32[]{:S(2)}) collective-permute-start(f32[128,512]{1,0:T(8,128)S(1)} %get-tuple-element.212), channel_id=1, source_target_pairs={{0,4},{4,0},{8,12},{12,8},{16,20},{20,16},{24,28},{28,24},{1,5},{5... | collective-permute-start | bytes 786440 | tf_op jit(solution)/shard_map/ppermute | solution.py:673
  83.7 5.3 %collective-permute-done.26.refs_4_ = f32[128,512]{1,0:T(8,128)S(1)} collective-permute-done((f32[128,512]{1,0:T(8,128)S(1)}, f32[128,512]{1,0:T(8,128)S(1)}, u32[]{:S(2)}, u32[]{:S(2)}) %collective-permute-start.26) | collective-permute-done | bytes 262176 | tf_op jit(solution)/shard_map/ppermute | solution.py:673
  89.0 9.4 %collective-permute-done.25.refs_3_ = f32[136,512]{1,0:T(8,128)S(1)} collective-permute-done((f32[136,512]{1,0:T(8,128)S(1)}, f32[136,512]{1,0:T(8,128)S(1)}, u32[]{:S(2)}, u32[]{:S(2)}) %collective-permute-start.25) | collective-permute-done | bytes 278560 | tf_op jit(solution)/shard_map/ppermute | solution.py:673
  100.7 2.0 %collective-permute-start.32 = (f32[128,512]{1,0:T(8,128)S(1)}, f32[128,512]{1,0:T(8,128)S(1)}, u32[]{:S(2)}, u32[]{:S(2)}) collective-permute-start(f32[128,512]{1,0:T(8,128)S(1)} %get-tuple-element.219.refs_5_.refs_1_), channel_id=1, source_target_pairs={{0,8},{4,12},{8,0},{12,4},{16,24},{20,28},{24,16},{28,20},{1,9},{5... | collective-permute-start | bytes 786440 | tf_op jit(solution)/shard_map/ppermute | solution.py:673
  102.7 3.8 %collective-permute-done.28.refs_4_ = f32[64,512]{1,0:T(8,128)S(1)} collective-permute-done((f32[64,512]{1,0:T(8,128)S(1)}, f32[64,512]{1,0:T(8,128)S(1)}, u32[]{:S(2)}, u32[]{:S(2)}) %collective-permute-start.28) | collective-permute-done | bytes 131104 | tf_op jit(solution)/shard_map/ppermute | solution.py:673
  109.6 5.6 %collective-permute-done.32.refs_3_ = f32[128,512]{1,0:T(8,128)S(1)} collective-permute-done((f32[128,512]{1,0:T(8,128)S(1)}, f32[128,512]{1,0:T(8,128)S(1)}, u32[]{:S(2)}, u32[]{:S(2)}) %collective-permute-start.32) | collective-permute-done | bytes 262176 | tf_op jit(solution)/shard_map/ppermute | solution.py:673
  121.3 8.4 %collective-permute-done.35.refs_2_ = f32[64,512]{1,0:T(8,128)S(1)} collective-permute-done((f32[64,512]{1,0:T(8,128)S(1)}, f32[64,512]{1,0:T(8,128)S(1)}, u32[]{:S(2)}, u32[]{:S(2)}) %collective-permute-start.35) | collective-permute-done | bytes 131104 | tf_op jit(solution)/shard_map/ppermute | solution.py:673
  (98 shorter events, 51.5 us)
Async XLA Ops:
  2.1 9.5 %collective-permute-start = (f32[520,512]{1,0:T(8,128)S(1)}, f32[520,512]{1,0:T(8,128)S(1)}, u32[]{:S(2)}, u32[]{:S(2)}) collective-permute-start(f32[520,512]{1,0:T(8,128)S(1)} %get-tuple-element.134.refs_1_.refs_0_), channel_id=1, source_target_pairs={{0,1},{1,0},{2,3},{3,2},{4,5},{5,4},{6,7},{7,6},{8,9},{9,8},{10,11... | collective-permute-start | bytes 3194888 | tf_op jit(solution)/shard_map/ppermute | solution.py:673
  2.6 15.2 %collective-permute-start.1 = (f32[2,64,512]{2,1,0:T(8,128)S(1)}, f32[2,64,512]{2,1,0:T(8,128)S(1)}, u32[]{:S(2)}, u32[]{:S(2)}) collective-permute-start(f32[2,64,512]{2,1,0:T(8,128)S(1)} %get-tuple-element.132.refs_7_), channel_id=1, source_target_pairs={{0,4},{2,6},{4,8},{5,1},{6,10},{7,3},{8,12},{9,5},{10,14},{11,7},{... | collective-permute-start | bytes 786440 | tf_op jit(solution)/shard_map/ppermute | solution.py:688
  9.5 9.3 %collective-permute-start.2 = (f32[128,512]{1,0:T(8,128)S(1)}, f32[128,512]{1,0:T(8,128)S(1)}, u32[]{:S(2)}, u32[]{:S(2)}) collective-permute-start(f32[128,512]{1,0:T(8,128)S(1)} %get-tuple-element.145), channel_id=1, source_target_pairs={{0,2},{1,3},{2,0},{3,1},{4,6},{5,7},{6,4},{7,5},{8,10},{9,11},{10,... | collective-permute-start | bytes 786440 | tf_op jit(solution)/shard_map/ppermute | solution.py:673
  11.1 14.2 %collective-permute-start.7 = (f32[512,512]{1,0:T(8,128)S(1)}, f32[512,512]{1,0:T(8,128)S(1)}, u32[]{:S(2)}, u32[]{:S(2)}) collective-permute-start(f32[512,512]{1,0:T(8,128)S(1)} %get-tuple-element.152.refs_13_.refs_2_), channel_id=1, source_target_pairs={{0,1},{1,0},{2,3},{3,2},{4,5},{5,4},{6,7},{7,6},{8,9},{9,8},{10,11... | collective-permute-start | bytes 3145736 | tf_op jit(solution)/shard_map/ppermute | solution.py:673
  11.1 15.8 %collective-permute-start.6 = (f32[512,512]{1,0:T(8,128)S(1)}, f32[512,512]{1,0:T(8,128)S(1)}, u32[]{:S(2)}, u32[]{:S(2)}) collective-permute-start(f32[512,512]{1,0:T(8,128)S(1)} %get-tuple-element.151.refs_11_), channel_id=1, source_target_pairs={{0,1},{1,0},{2,3},{3,2},{4,5},{5,4},{6,7},{7,6},{8,9},{9,8},{10,11... | collective-permute-start | bytes 3145736 | tf_op jit(solution)/shard_map/ppermute | solution.py:673
  18.9 8.5 %collective-permute-start.5 = (f32[128,512]{1,0:T(8,128)S(1)}, f32[128,512]{1,0:T(8,128)S(1)}, u32[]{:S(2)}, u32[]{:S(2)}) collective-permute-start(f32[128,512]{1,0:T(8,128)S(1)} %get-tuple-element.146.refs_4_), channel_id=1, source_target_pairs={{0,1},{1,0},{2,3},{3,2},{4,5},{5,4},{6,7},{7,6},{8,9},{9,8},{10,11... | collective-permute-start | bytes 786440 | tf_op jit(solution)/shard_map/ppermute | solution.py:673
  22.7 10.1 %collective-permute-start.8 = (f32[128,256]{1,0:T(8,128)S(1)}, f32[128,256]{1,0:T(8,128)S(1)}, u32[]{:S(2)}, u32[]{:S(2)}) collective-permute-start(f32[128,256]{1,0:T(8,128)S(1)} %get-tuple-element.156.refs_0_.refs_5_), channel_id=1, source_target_pairs={{0,2},{1,3},{2,0},{3,1},{4,6},{5,7},{6,4},{7,5},{8,10},{9,11},{10,... | collective-permute-start | bytes 393224 | tf_op jit(solution)/shard_map/ppermute | solution.py:673
  31.2 14.2 %collective-permute-start.11 = (f32[256,512]{1,0:T(8,128)S(1)}, f32[256,512]{1,0:T(8,128)S(1)}, u32[]{:S(2)}, u32[]{:S(2)}) collective-permute-start(f32[256,512]{1,0:T(8,128)S(1)} %get-tuple-element.159.refs_15_.refs_0_), channel_id=1, source_target_pairs={{0,2},{1,3},{2,0},{3,1},{4,6},{5,7},{6,4},{7,5},{8,10},{9,11},{10,... | collective-permute-start | bytes 1572872 | tf_op jit(solution)/shard_map/ppermute | solution.py:673
  41.3 14.8 %collective-permute-start.14 = (f32[256,512]{1,0:T(8,128)S(1)}, f32[256,512]{1,0:T(8,128)S(1)}, u32[]{:S(2)}, u32[]{:S(2)}) collective-permute-start(f32[256,512]{1,0:T(8,128)S(1)} %get-tuple-element.167.refs_4_.refs_0_), channel_id=1, source_target_pairs={{0,2},{1,3},{2,0},{3,1},{4,6},{5,7},{6,4},{7,5},{8,10},{9,11},{10,... | collective-permute-start | bytes 1572872 | tf_op jit(solution)/shard_map/ppermute | solution.py:673
  44.7 33.9 %collective-permute-start.10 = (f32[512,512]{1,0:T(8,128)S(1)}, f32[512,512]{1,0:T(8,128)S(1)}, u32[]{:S(2)}, u32[]{:S(2)}) collective-permute-start(f32[512,512]{1,0:T(8,128)S(1)} %feed_out.1.refs_2_), channel_id=1, source_target_pairs={{0,2},{1,3},{2,0},{3,1},{4,6},{5,7},{6,4},{7,5},{8,10},{9,11},{10,... | collective-permute-start | bytes 3145736 | tf_op jit(solution)/shard_map/ppermute | solution.py:673
  45.9 14.6 %collective-permute-start.15 = (f32[256,512]{1,0:T(8,128)S(1)}, f32[256,512]{1,0:T(8,128)S(1)}, u32[]{:S(2)}, u32[]{:S(2)}) collective-permute-start(f32[256,512]{1,0:T(8,128)S(1)} %get-tuple-element.184), channel_id=1, source_target_pairs={{0,8},{4,12},{8,0},{12,4},{16,24},{20,28},{24,16},{28,20},{1,9},{5... | collective-permute-start | bytes 1572872 | tf_op jit(solution)/shard_map/ppermute | solution.py:673
  47.5 13.1 %collective-permute-start.16 = (f32[256,512]{1,0:T(8,128)S(1)}, f32[256,512]{1,0:T(8,128)S(1)}, u32[]{:S(2)}, u32[]{:S(2)}) collective-permute-start(f32[256,512]{1,0:T(8,128)S(1)} %get-tuple-element.174.refs_12_), channel_id=1, source_target_pairs={{0,4},{4,0},{8,12},{12,8},{16,20},{20,16},{24,28},{28,24},{1,5},{5... | collective-permute-start | bytes 1572872 | tf_op jit(solution)/shard_map/ppermute | solution.py:673
  69.1 9.9 %collective-permute-start.22 = (f32[264,512]{1,0:T(8,128)S(1)}, f32[264,512]{1,0:T(8,128)S(1)}, u32[]{:S(2)}, u32[]{:S(2)}) collective-permute-start(f32[264,512]{1,0:T(8,128)S(1)} %get-tuple-element.203), channel_id=1, source_target_pairs={{0,1},{1,0},{2,3},{3,2},{4,5},{5,4},{6,7},{7,6},{8,9},{9,8},{10,11... | collective-permute-start | bytes 1622024 | tf_op jit(solution)/shard_map/ppermute | solution.py:673
  71.1 29.0 %collective-permute-start.29 = (f32[256,512]{1,0:T(8,128)S(1)}, f32[256,512]{1,0:T(8,128)S(1)}, u32[]{:S(2)}, u32[]{:S(2)}) collective-permute-start(f32[256,512]{1,0:T(8,128)S(1)} %stack.2.refs_3_.refs_0_), channel_id=1, source_target_pairs={{0,16},{4,20},{8,24},{12,28},{16,0},{20,4},{24,8},{28,12},{1,17},{... | collective-permute-start | bytes 1572872 | tf_op jit(solution)/shard_map/ppermute | solution.py:673
  73.9 33.5 %collective-permute-start.24 = (f32[512,512]{1,0:T(8,128)S(1)}, f32[512,512]{1,0:T(8,128)S(1)}, u32[]{:S(2)}, u32[]{:S(2)}) collective-permute-start(f32[512,512]{1,0:T(8,128)S(1)} %edge_add.1.refs_5_.refs_0_), channel_id=1, source_target_pairs={{0,2},{1,3},{2,0},{3,1},{4,6},{5,7},{6,4},{7,5},{8,10},{9,11},{10,... | collective-permute-start | bytes 3145736 | tf_op jit(solution)/shard_map/ppermute | solution.py:673
  79.2 19.2 %collective-permute-start.25 = (f32[136,512]{1,0:T(8,128)S(1)}, f32[136,512]{1,0:T(8,128)S(1)}, u32[]{:S(2)}, u32[]{:S(2)}) collective-permute-start(f32[136,512]{1,0:T(8,128)S(1)} %get-tuple-element.211), channel_id=1, source_target_pairs={{0,8},{4,12},{8,0},{12,4},{16,24},{20,28},{24,16},{28,20},{1,9},{5... | collective-permute-start | bytes 835592 | tf_op jit(solution)/shard_map/ppermute | solution.py:673
  80.4 8.6 %collective-permute-start.26 = (f32[128,512]{1,0:T(8,128)S(1)}, f32[128,512]{1,0:T(8,128)S(1)}, u32[]{:S(2)}, u32[]{:S(2)}) collective-permute-start(f32[128,512]{1,0:T(8,128)S(1)} %get-tuple-element.212), channel_id=1, source_target_pairs={{0,4},{4,0},{8,12},{12,8},{16,20},{20,16},{24,28},{28,24},{1,5},{5... | collective-permute-start | bytes 786440 | tf_op jit(solution)/shard_map/ppermute | solution.py:673
  100.2 9.4 %collective-permute-start.31 = (f32[128,512]{1,0:T(8,128)S(1)}, f32[128,512]{1,0:T(8,128)S(1)}, u32[]{:S(2)}, u32[]{:S(2)}) collective-permute-start(f32[128,512]{1,0:T(8,128)S(1)} %get-tuple-element.220.refs_0_), channel_id=1, source_target_pairs={{0,4},{4,0},{8,12},{12,8},{16,20},{20,16},{24,28},{28,24},{1,5},{5... | collective-permute-start | bytes 786440 | tf_op jit(solution)/shard_map/ppermute | solution.py:673
  100.7 14.5 %collective-permute-start.32 = (f32[128,512]{1,0:T(8,128)S(1)}, f32[128,512]{1,0:T(8,128)S(1)}, u32[]{:S(2)}, u32[]{:S(2)}) collective-permute-start(f32[128,512]{1,0:T(8,128)S(1)} %get-tuple-element.219.refs_5_.refs_1_), channel_id=1, source_target_pairs={{0,8},{4,12},{8,0},{12,4},{16,24},{20,28},{24,16},{28,20},{1,9},{5... | collective-permute-start | bytes 786440 | tf_op jit(solution)/shard_map/ppermute | solution.py:673
  106.6 12.0 %collective-permute-start.33 = (f32[136,512]{1,0:T(8,128)S(1)}, f32[136,512]{1,0:T(8,128)S(1)}, u32[]{:S(2)}, u32[]{:S(2)}) collective-permute-start(f32[136,512]{1,0:T(8,128)S(1)} %stack.3.refs_7_.refs_0_), channel_id=1, source_target_pairs={{0,16},{4,20},{8,24},{12,28},{16,0},{20,4},{24,8},{28,12},{1,17},{... | collective-permute-start | bytes 835592 | tf_op jit(solution)/shard_map/ppermute | solution.py:673
  115.2 19.7 %collective-permute-start.40 = (f32[256,512]{1,0:T(8,128)S(1)}, f32[256,512]{1,0:T(8,128)S(1)}, u32[]{:S(2)}, u32[]{:S(2)}) collective-permute-start(f32[256,512]{1,0:T(8,128)S(1)} %get-tuple-element.229.refs_0_), channel_id=1, source_target_pairs={{0,8},{4,12},{8,0},{12,4},{16,24},{20,28},{24,16},{28,20},{1,9},{5... | collective-permute-start | bytes 1572872 | tf_op jit(solution)/shard_map/ppermute | solution.py:673
  115.3 20.6 %collective-permute-start.39 = (f32[256,512]{1,0:T(8,128)S(1)}, f32[256,512]{1,0:T(8,128)S(1)}, u32[]{:S(2)}, u32[]{:S(2)}) collective-permute-start(f32[256,512]{1,0:T(8,128)S(1)} %get-tuple-element.221.refs_2_.refs_0_), channel_id=1, source_target_pairs={{0,4},{4,0},{8,12},{12,8},{16,20},{20,16},{24,28},{28,24},{1,5},{5... | collective-permute-start | bytes 1572872 | tf_op jit(solution)/shard_map/ppermute | solution.py:673
  118.7 11.0 %collective-permute-start.35 = (f32[64,512]{1,0:T(8,128)S(1)}, f32[64,512]{1,0:T(8,128)S(1)}, u32[]{:S(2)}, u32[]{:S(2)}) collective-permute-start(f32[64,512]{1,0:T(8,128)S(1)} %get-tuple-element.225.refs_0_), channel_id=1, source_target_pairs={{0,4},{4,0},{8,12},{12,8},{16,20},{20,16},{24,28},{28,24},{1,5},{5... | collective-permute-start | bytes 393224 | tf_op jit(solution)/shard_map/ppermute | solution.py:673
  120.4 10.6 %collective-permute-start.36 = (f32[64,512]{1,0:T(8,128)S(1)}, f32[64,512]{1,0:T(8,128)S(1)}, u32[]{:S(2)}, u32[]{:S(2)}) collective-permute-start(f32[64,512]{1,0:T(8,128)S(1)} %get-tuple-element.226.refs_1_), channel_id=1, source_target_pairs={{0,8},{4,12},{8,0},{12,4},{16,24},{20,28},{24,16},{28,20},{1,9},{5... | collective-permute-start | bytes 393224 | tf_op jit(solution)/shard_map/ppermute | solution.py:673
  (18 other events, 111.9 us)

commit v2 on v1

--- a/solution.py
+++ b/solution.py
@@ -691,7 +691,7 @@
 class SumsOverTm:
     def __init__(self, run, a, b, rows=None):
         bits = [1 << i for i in range(lax.axis_size("tm").bit_length() - 1)]
-        self.run, self.values, self.got = run, list(a), [list(v) for v in b]
+        self.run, self.values, self.got, self.ones = run, list(a), [list(v) for v in b], []
         self.rows = [] if rows is None else [rows]
         self.apart = [(bits[1], bits[0]), (bits[0], bits[1])]
         self.together, self.last = bits[2:-1], bits[-1]
@@ -759,6 +759,22 @@
             return self.step()
         self.got = [[swap(v, "tm", bit)] for v, bit in zip(self.values, following[1], strict=True)]
 
+    def join_one(self, number):
+        if len(self.todo) != 1:
+            return
+        bits = self.todo[0][1]
+        value = self.values[number]
+        values, got = list(self.values), list(self.got)
+        (values[number],) = self.run.call(
+            functools.partial(join_kernel, bits[number : number + 1]), "join", [(2 * value.shape[0], value.shape[1])],
+            (value, *got[number]),
+        )
+        got[number] = [swap(values[number], "tm", self.apart[0][number])]
+        self.values, self.got = values, got
+        self.ones.append(number)
+        if len(self.ones) == 2:
+            self.todo.pop()
+
     @property
     def joined(self):
         return not self.todo
@@ -773,8 +789,8 @@
     ("inner_weights", 11), ("feed_out", 0.6), ("grad_sum0", 18), ("ffn", 11), ("back0", 6), ("grad_sum1", 18),
     ("back1", 0.5), ("ffn", 0.1), ("project_back", 1.8), ("project_weights", 2), ("ffn", 0.1), ("edge_add", 5),
     ("out_half", 5), ("out_send", 6), ("heads", 20), ("place_out", 1.3), ("heads", 0.1), ("ffn", 0.1), ("heads", 3),
-    ("frames_back", 0.6), ("ffn", 20), ("place_frames", 0.1), ("heads", 0.1), ("heads", 0.1), ("join_outer", 0.1),
-    ("join_inner", 0.1), ("finish", 1.3),
+    ("frames_back", 0.6), ("ffn_last0", 0.1), ("ffn_last1", 20), ("place_frames", 0.1), ("heads", 0.1),
+    ("heads", 0.1), ("join_outer", 0.1), ("join_inner", 0.1), ("finish", 1.3),
 )
 PIECES = 1
 
@@ -992,6 +1008,12 @@
     def heads(self):
         self.sum("heads")
 
+    def ffn_last(self, number):
+        self.sums["ffn"].join_one(number)
+
+    def heads_last(self, number):
+        self.sums["heads"].join_one(number)
+
     def frames_back(self):
         (half,) = self.run.call(
             frames_back_kernel, "frames_back", [(self.micros * self.length, self.features)],

time: 140 us -> 139 us (level)
    pallas_call x38 -> x39, Pallas kernels: 49.6 us -> 49.7 us  [call(): pl.pallas_call(body, name=name, grid=(1,), in_specs=[in_hbm if i in far e...]
  transfers between devices with their start and end apart: 41 -> 41, of which waited for: 15 -> 14; matrix products, arithmetic and copies ran while one was open for 0% -> 0% of each run, Pallas kernels for 34% -> 34%
where the time goes in v2:
time: 139 us
  Pallas kernels  49.7 us (36%)
  waiting for transfers between devices  44.4 us (32%)
  starting transfers between devices  43.8 us (32%)
    pallas_call x39, Pallas kernels, call(): pl.pallas_call(body, name=name, grid=(1,), in_specs=[in_hbm if i in far e...  49.7 us
    ppermute x39, waiting for transfers between devices, swap(): return lax.ppermute(value, axis, [(i, i ^ bit) for i in range(size)])  44.4 us
    ppermute x39, starting transfers between devices, swap(): return lax.ppermute(value, axis, [(i, i ^ bit) for i in range(size)])  38.7 us
    ppermute x2, starting transfers between devices, swap_edges(): return lax.ppermute(value, ('tm', 'head'), pairs)  5.1 us
  transfers between devices with their start and end apart: 41, of which 14 were waited for; matrix products, arithmetic and copies ran while one was open for 0% of the time, Pallas kernels for 34%

profile of v2, /device:TPU:0, one launch (start us, length us, event | category | flops | bytes accessed | tf_op | source)
XLA Modules:
  0.0 139.0 jit_solution(13712753850046890371)
XLA Ops:
  2.6 4.4 %collective-permute-start.1 = (f32[2,64,512]{2,1,0:T(8,128)S(1)}, f32[2,64,512]{2,1,0:T(8,128)S(1)}, u32[]{:S(2)}, u32[]{:S(2)}) collective-permute-start(f32[2,64,512]{2,1,0:T(8,128)S(1)} %get-tuple-element.130.refs_7_), channel_id=1, source_target_pairs={{0,4},{2,6},{4,8},{5,1},{6,10},{7,3},{8,12},{9,5},{10,14},{11,7},{... | collective-permute-start | bytes 786440 | tf_op jit(solution)/shard_map/ppermute | solution.py:688
  7.0 2.5 %norm.1 = (f32[2,256,512]{2,1,0:T(8,128)S(1)}, f32[2,256,512]{2,1,0:T(8,128)S(1)}, f32[2,256,128]{2,1,0:T(8,128)S(1)}, f32[2,256,512]{2,1,0:T(8,128)S(1)}, f32[5...) custom-call(f32[2,512,512]{2,1,0:T(8,128)} %refs_0_.6, ...), custom_call_target="tpu_custom_call" | custom-call | flops 2486400000 | tf_op jit(solution)/shard_map/norm/pallas_call | solution.py:118
  13.5 3.7 %attend_inner.1 = (f32[128,256]{1,0:T(8,128)S(1)}, f32[128,256]{1,0:T(8,128)S(1)}, f32[2,2,2,128,128]{4,3,2,1,0:T(8,128)S(1)}) custom-call(s32[2,4]{1,0:T(2,128)S(1)} %copy-done, f32[2,256,256]{2,1,0:T(8,128)S(1)} %get-tuple-element.134.refs_1_.refs_7_, f32[2,256,512]{2,1,0:T(8,128)S(1)} %get-tuple-element.135.refs_2_.refs_8_, ...), custom_call_target="tpu_custom_call" | custom-call | flops 5697999872 | tf_op jit(solution)/shard_map/attend_inner/pallas_call | solution.py:118
  19.0 2.1 %attend_outer.2 = (f32[128,256]{1,0:T(8,128)S(1)}, f32[2,2,128,128]{3,2,1,0:T(8,128)S(1)}) custom-call(s32[2,4]{1,0:T(2,128)S(1)} %copy-done, f32[2,256,256]{2,1,0:T(8,128)S(1)} %get-tuple-element.134.refs_1_.refs_7_, f32[2,256,512]{2,1,0:T(8,128)S(1)} %get-tuple-element.135.refs_2_.refs_8_, f32[2,72,512]{2,1,0:T(8,128)S(1)} %get-tuple-element.142.refs_3_.refs_9_, ...), custom_call_target="tpu_custom_call" | custom-call | flops 12432000000 | tf_op jit(solution)/shard_map/attend_outer/pallas_call | solution.py:118
  23.2 2.1 %attend_outer.3 = (f32[128,256]{1,0:T(8,128)S(1)}, f32[2,2,128,128]{3,2,1,0:T(8,128)S(1)}) custom-call(s32[2,4]{1,0:T(2,128)S(1)} %copy-done, f32[2,256,256]{2,1,0:T(8,128)S(1)} %get-tuple-element.134.refs_1_.refs_7_, f32[2,256,512]{2,1,0:T(8,128)S(1)} %get-tuple-element.135.refs_2_.refs_8_, f32[2,72,512]{2,1,0:T(8,128)S(1)} %get-tuple-element.142.refs_3_.refs_9_, ...), custom_call_target="tpu_custom_call" | custom-call | flops 518000000 | tf_op jit(solution)/shard_map/attend_outer/pallas_call | solution.py:118
  27.4 3.9 %feed.2 = (f32[256,512]{1,0:T(8,128)S(1)}, f32[256,1024]{1,0:T(8,128)S(1)}, f32[256,1024]{1,0:T(8,128)S(1)}, f32[256,512]{1,0:T(8,128)S(1)}, f32[256,512]{1,0:T(8,128)S(1)}) custom-call(f32[128,256]{1,0:T(8,128)S(1)} %get-tuple-element.137.refs_0_.refs_5_, f32[128,256]{1,0:T(8,128)S(1)} %get-tuple-element.145.refs_1_.refs_6_, ...), custom_call_target="tpu_custom_call" | custom-call | flops 9324000256 | tf_op jit(solution)/shard_map/feed/pallas_call | solution.py:118
  32.8 4.1 %feed.3 = (f32[256,512]{1,0:T(8,128)S(1)}, f32[256,1024]{1,0:T(8,128)S(1)}, f32[256,1024]{1,0:T(8,128)S(1)}, f32[256,512]{1,0:T(8,128)S(1)}, f32[256,512]{1,0:T(8,128)S(1)}) custom-call(f32[128,256]{1,0:T(8,128)S(1)} %get-tuple-element.154.refs_0_.refs_5_, f32[128,256]{1,0:T(8,128)S(1)} %get-tuple-element.155.refs_1_.refs_6_, ...), custom_call_target="tpu_custom_call" | custom-call | flops 7251999744 | tf_op jit(solution)/shard_map/feed/pallas_call | solution.py:118
  38.8 1.9 %inner_weights.1 = (f32[512,512]{1,0:T(8,128)S(1)}, f32[512,512]{1,0:T(8,128)S(1)}, f32[2,512]{1,0:T(2,128)S(1)}) custom-call(f32[256,512]{1,0:T(8,128)S(1)} %get-tuple-element.161.refs_0_, f32[256,512]{1,0:T(8,128)S(1)} %get-tuple-element.162.refs_1_, f32[256,1024]{1,0:T(8,128)S(1)} %get-tuple-element.163.refs_2_, ...), custom_call_target="tpu_custom_call" | custom-call | flops 5697999872 | tf_op jit(solution)/shard_map/inner_weights/pallas_call | solution.py:118
  42.6 2.0 %feed_out.1.refs_2_ = f32[512,512]{1,0:T(8,128)S(1)} custom-call(f32[256,1024]{1,0:T(8,128)S(1)} %get-tuple-element.159.refs_0_, f32[256,1024]{1,0:T(8,128)S(1)} %get-tuple-element.160.refs_1_, f32[512,512]{1,0:T(8,128)S(1)} %get-tuple-element.150.refs_13_.refs_2_, f32[512,512]{1,0:T(8,128)S(1)} %collective-permute-done.7.refs_14_.refs_3_, ...), custom_call_target="tpu_custom_call" | custom-call | flops 310800000 | tf_op jit(solution)/shard_map/feed_out/pallas_call | solution.py:118
  49.1 4.5 %back.2 = (f32[256,512]{1,0:T(8,128)S(1)}, f32[256,256]{1,0:T(8,128)S(1)}, f32[328,512]{1,0:T(8,128)S(1)}, f32[512,128]{1,0:T(8,128)S(1)}, f32[512,128]{1,0:T(8,128)S(1)}, /*index=5*/f32[3,512]{1,0:T(4,128)S(1)}) custom-call(f32[256,512]{1,0:T(8,128)S(1)} %grad_sum.2.refs_4_.refs_0_, f32[256,512]{1,0:T(8,128)S(1)} %get-tuple-element.153.refs_1_.refs_0_, ...), custom_call_target="tpu_custom_call" | custom-call | flops 3108000000 | tf_op jit(solution)/shard_map/back/pallas_call | solution.py:118
  53.6 2.5 %collective-permute-done.14.refs_1_ = f32[256,512]{1,0:T(8,128)S(1)} collective-permute-done((f32[256,512]{1,0:T(8,128)S(1)}, f32[256,512]{1,0:T(8,128)S(1)}, u32[]{:S(2)}, u32[]{:S(2)}) %collective-permute-start.14) | collective-permute-done | bytes 524320 | tf_op jit(solution)/shard_map/ppermute | solution.py:673
  56.2 4.3 %back.3 = (f32[256,512]{1,0:T(8,128)S(1)}, f32[256,256]{1,0:T(8,128)S(1)}, f32[328,512]{1,0:T(8,128)S(1)}, f32[512,128]{1,0:T(8,128)S(1)}, f32[512,128]{1,0:T(8,128)S(1)}, /*index=5*/f32[3,512]{1,0:T(4,128)S(1)}) custom-call(f32[256,512]{1,0:T(8,128)S(1)} %grad_sum.3.refs_0_.refs_12_, f32[256,512]{1,0:T(8,128)S(1)} %get-tuple-element.158.refs_1_, ...), custom_call_target="tpu_custom_call" | custom-call | flops 259000000 | tf_op jit(solution)/shard_map/back/pallas_call | solution.py:118
  66.5 2.6 %project_weights.1 = (f32[256,512]{1,0:T(8,128)S(1)}, f32[256,512]{1,0:T(8,128)S(1)}, f32[8,512]{1,0:T(8,128)S(1)}, f32[264,512]{1,0:T(8,128)S(1)}, f32[256,512]{1,0:T(8,128)S(1)}) custom-call(f32[2,256,512]{2,1,0:T(8,128)S(1)} %get-tuple-element.131.refs_0_, f32[2,72,512]{2,1,0:T(8,128)S(1)} %get-tuple-element.191.refs_1_, ...), custom_call_target="tpu_custom_call" | custom-call | flops 1036000000 | tf_op jit(solution)/shard_map/project_weights/pallas_call | solution.py:118
  71.1 2.6 %collective-permute-start.29 = (f32[256,512]{1,0:T(8,128)S(1)}, f32[256,512]{1,0:T(8,128)S(1)}, u32[]{:S(2)}, u32[]{:S(2)}) collective-permute-start(f32[256,512]{1,0:T(8,128)S(1)} %stack.2.refs_3_.refs_0_), channel_id=1, source_target_pairs={{0,16},{4,20},{8,24},{12,28},{16,0},{20,4},{24,8},{28,12},{1,17},{... | collective-permute-start | bytes 1572872 | tf_op jit(solution)/shard_map/ppermute | solution.py:673
  75.7 2.9 %collective-permute-done.10.refs_3_ = f32[512,512]{1,0:T(8,128)S(1)} collective-permute-done((f32[512,512]{1,0:T(8,128)S(1)}, f32[512,512]{1,0:T(8,128)S(1)}, u32[]{:S(2)}, u32[]{:S(2)}) %collective-permute-start.10) | collective-permute-done | bytes 1048608 | tf_op jit(solution)/shard_map/ppermute | solution.py:673
  80.4 2.0 %collective-permute-start.26 = (f32[128,512]{1,0:T(8,128)S(1)}, f32[128,512]{1,0:T(8,128)S(1)}, u32[]{:S(2)}, u32[]{:S(2)}) collective-permute-start(f32[128,512]{1,0:T(8,128)S(1)} %get-tuple-element.210), channel_id=1, source_target_pairs={{0,4},{4,0},{8,12},{12,8},{16,20},{20,16},{24,28},{28,24},{1,5},{5... | collective-permute-start | bytes 786440 | tf_op jit(solution)/shard_map/ppermute | solution.py:673
  83.7 5.3 %collective-permute-done.26.refs_4_ = f32[128,512]{1,0:T(8,128)S(1)} collective-permute-done((f32[128,512]{1,0:T(8,128)S(1)}, f32[128,512]{1,0:T(8,128)S(1)}, u32[]{:S(2)}, u32[]{:S(2)}) %collective-permute-start.26) | collective-permute-done | bytes 262176 | tf_op jit(solution)/shard_map/ppermute | solution.py:673
  89.0 9.4 %collective-permute-done.25.refs_3_ = f32[136,512]{1,0:T(8,128)S(1)} collective-permute-done((f32[136,512]{1,0:T(8,128)S(1)}, f32[136,512]{1,0:T(8,128)S(1)}, u32[]{:S(2)}, u32[]{:S(2)}) %collective-permute-start.25) | collective-permute-done | bytes 278560 | tf_op jit(solution)/shard_map/ppermute | solution.py:673
  100.7 2.0 %collective-permute-start.31 = (f32[128,512]{1,0:T(8,128)S(1)}, f32[128,512]{1,0:T(8,128)S(1)}, u32[]{:S(2)}, u32[]{:S(2)}) collective-permute-start(f32[128,512]{1,0:T(8,128)S(1)} %get-tuple-element.217.refs_5_.refs_0_), channel_id=1, source_target_pairs={{0,8},{4,12},{8,0},{12,4},{16,24},{20,28},{24,16},{28,20},{1,9},{5... | collective-permute-start | bytes 786440 | tf_op jit(solution)/shard_map/ppermute | solution.py:673
  102.7 3.8 %collective-permute-done.28.refs_4_ = f32[64,512]{1,0:T(8,128)S(1)} collective-permute-done((f32[64,512]{1,0:T(8,128)S(1)}, f32[64,512]{1,0:T(8,128)S(1)}, u32[]{:S(2)}, u32[]{:S(2)}) %collective-permute-start.28) | collective-permute-done | bytes 131104 | tf_op jit(solution)/shard_map/ppermute | solution.py:673
  110.9 6.7 %collective-permute-done.31.refs_1_ = f32[128,512]{1,0:T(8,128)S(1)} collective-permute-done((f32[128,512]{1,0:T(8,128)S(1)}, f32[128,512]{1,0:T(8,128)S(1)}, u32[]{:S(2)}, u32[]{:S(2)}) %collective-permute-start.31) | collective-permute-done | bytes 262176 | tf_op jit(solution)/shard_map/ppermute | solution.py:673
  119.2 2.1 %collective-permute-start.35 = (f32[64,512]{1,0:T(8,128)S(1)}, f32[64,512]{1,0:T(8,128)S(1)}, u32[]{:S(2)}, u32[]{:S(2)}) collective-permute-start(f32[64,512]{1,0:T(8,128)S(1)} %get-tuple-element.222.refs_0_), channel_id=1, source_target_pairs={{0,4},{4,0},{8,12},{12,8},{16,20},{20,16},{24,28},{28,24},{1,5},{5... | collective-permute-start | bytes 393224 | tf_op jit(solution)/shard_map/ppermute | solution.py:673
  121.3 8.3 %collective-permute-done.35.refs_2_ = f32[64,512]{1,0:T(8,128)S(1)} collective-permute-done((f32[64,512]{1,0:T(8,128)S(1)}, f32[64,512]{1,0:T(8,128)S(1)}, u32[]{:S(2)}, u32[]{:S(2)}) %collective-permute-start.35) | collective-permute-done | bytes 131104 | tf_op jit(solution)/shard_map/ppermute | solution.py:673
  131.5 2.2 %collective-permute-start.34 = (f32[8,512]{1,0:T(8,128)S(1)}, f32[8,512]{1,0:T(8,128)S(1)}, u32[]{:S(2)}, u32[]{:S(2)}) collective-permute-start(f32[8,512]{1,0:T(8,128)S(1)} %get-tuple-element.221.refs_4_.refs_0_), channel_id=1, source_target_pairs={{0,2},{1,3},{2,0},{3,1},{4,6},{5,7},{6,4},{7,5},{8,10},{9,11},{10,... | collective-permute-start | bytes 49160 | tf_op jit(solution)/shard_map/ppermute | solution.py:673
  (99 shorter events, 50.0 us)
Async XLA Ops:
  2.1 9.5 %collective-permute-start = (f32[520,512]{1,0:T(8,128)S(1)}, f32[520,512]{1,0:T(8,128)S(1)}, u32[]{:S(2)}, u32[]{:S(2)}) collective-permute-start(f32[520,512]{1,0:T(8,128)S(1)} %get-tuple-element.132.refs_1_.refs_0_), channel_id=1, source_target_pairs={{0,1},{1,0},{2,3},{3,2},{4,5},{5,4},{6,7},{7,6},{8,9},{9,8},{10,11... | collective-permute-start | bytes 3194888 | tf_op jit(solution)/shard_map/ppermute | solution.py:673
  2.6 15.2 %collective-permute-start.1 = (f32[2,64,512]{2,1,0:T(8,128)S(1)}, f32[2,64,512]{2,1,0:T(8,128)S(1)}, u32[]{:S(2)}, u32[]{:S(2)}) collective-permute-start(f32[2,64,512]{2,1,0:T(8,128)S(1)} %get-tuple-element.130.refs_7_), channel_id=1, source_target_pairs={{0,4},{2,6},{4,8},{5,1},{6,10},{7,3},{8,12},{9,5},{10,14},{11,7},{... | collective-permute-start | bytes 786440 | tf_op jit(solution)/shard_map/ppermute | solution.py:688
  9.5 9.3 %collective-permute-start.2 = (f32[128,512]{1,0:T(8,128)S(1)}, f32[128,512]{1,0:T(8,128)S(1)}, u32[]{:S(2)}, u32[]{:S(2)}) collective-permute-start(f32[128,512]{1,0:T(8,128)S(1)} %get-tuple-element.143), channel_id=1, source_target_pairs={{0,2},{1,3},{2,0},{3,1},{4,6},{5,7},{6,4},{7,5},{8,10},{9,11},{10,... | collective-permute-start | bytes 786440 | tf_op jit(solution)/shard_map/ppermute | solution.py:673
  11.1 14.2 %collective-permute-start.7 = (f32[512,512]{1,0:T(8,128)S(1)}, f32[512,512]{1,0:T(8,128)S(1)}, u32[]{:S(2)}, u32[]{:S(2)}) collective-permute-start(f32[512,512]{1,0:T(8,128)S(1)} %get-tuple-element.150.refs_13_.refs_2_), channel_id=1, source_target_pairs={{0,1},{1,0},{2,3},{3,2},{4,5},{5,4},{6,7},{7,6},{8,9},{9,8},{10,11... | collective-permute-start | bytes 3145736 | tf_op jit(solution)/shard_map/ppermute | solution.py:673
  11.1 15.8 %collective-permute-start.6 = (f32[512,512]{1,0:T(8,128)S(1)}, f32[512,512]{1,0:T(8,128)S(1)}, u32[]{:S(2)}, u32[]{:S(2)}) collective-permute-start(f32[512,512]{1,0:T(8,128)S(1)} %get-tuple-element.149.refs_11_), channel_id=1, source_target_pairs={{0,1},{1,0},{2,3},{3,2},{4,5},{5,4},{6,7},{7,6},{8,9},{9,8},{10,11... | collective-permute-start | bytes 3145736 | tf_op jit(solution)/shard_map/ppermute | solution.py:673
  22.7 10.1 %collective-permute-start.8 = (f32[128,256]{1,0:T(8,128)S(1)}, f32[128,256]{1,0:T(8,128)S(1)}, u32[]{:S(2)}, u32[]{:S(2)}) collective-permute-start(f32[128,256]{1,0:T(8,128)S(1)} %get-tuple-element.154.refs_0_.refs_5_), channel_id=1, source_target_pairs={{0,2},{1,3},{2,0},{3,1},{4,6},{5,7},{6,4},{7,5},{8,10},{9,11},{10,... | collective-permute-start | bytes 393224 | tf_op jit(solution)/shard_map/ppermute | solution.py:673
  31.2 14.2 %collective-permute-start.11 = (f32[256,512]{1,0:T(8,128)S(1)}, f32[256,512]{1,0:T(8,128)S(1)}, u32[]{:S(2)}, u32[]{:S(2)}) collective-permute-start(f32[256,512]{1,0:T(8,128)S(1)} %get-tuple-element.157.refs_15_.refs_0_), channel_id=1, source_target_pairs={{0,2},{1,3},{2,0},{3,1},{4,6},{5,7},{6,4},{7,5},{8,10},{9,11},{10,... | collective-permute-start | bytes 1572872 | tf_op jit(solution)/shard_map/ppermute | solution.py:673
  41.3 14.8 %collective-permute-start.14 = (f32[256,512]{1,0:T(8,128)S(1)}, f32[256,512]{1,0:T(8,128)S(1)}, u32[]{:S(2)}, u32[]{:S(2)}) collective-permute-start(f32[256,512]{1,0:T(8,128)S(1)} %get-tuple-element.165.refs_4_.refs_0_), channel_id=1, source_target_pairs={{0,2},{1,3},{2,0},{3,1},{4,6},{5,7},{6,4},{7,5},{8,10},{9,11},{10,... | collective-permute-start | bytes 1572872 | tf_op jit(solution)/shard_map/ppermute | solution.py:673
  44.7 33.9 %collective-permute-start.10 = (f32[512,512]{1,0:T(8,128)S(1)}, f32[512,512]{1,0:T(8,128)S(1)}, u32[]{:S(2)}, u32[]{:S(2)}) collective-permute-start(f32[512,512]{1,0:T(8,128)S(1)} %feed_out.1.refs_2_), channel_id=1, source_target_pairs={{0,2},{1,3},{2,0},{3,1},{4,6},{5,7},{6,4},{7,5},{8,10},{9,11},{10,... | collective-permute-start | bytes 3145736 | tf_op jit(solution)/shard_map/ppermute | solution.py:673
  45.9 14.6 %collective-permute-start.15 = (f32[256,512]{1,0:T(8,128)S(1)}, f32[256,512]{1,0:T(8,128)S(1)}, u32[]{:S(2)}, u32[]{:S(2)}) collective-permute-start(f32[256,512]{1,0:T(8,128)S(1)} %get-tuple-element.182), channel_id=1, source_target_pairs={{0,8},{4,12},{8,0},{12,4},{16,24},{20,28},{24,16},{28,20},{1,9},{5... | collective-permute-start | bytes 1572872 | tf_op jit(solution)/shard_map/ppermute | solution.py:673
  47.5 13.1 %collective-permute-start.16 = (f32[256,512]{1,0:T(8,128)S(1)}, f32[256,512]{1,0:T(8,128)S(1)}, u32[]{:S(2)}, u32[]{:S(2)}) collective-permute-start(f32[256,512]{1,0:T(8,128)S(1)} %get-tuple-element.172.refs_12_), channel_id=1, source_target_pairs={{0,4},{4,0},{8,12},{12,8},{16,20},{20,16},{24,28},{28,24},{1,5},{5... | collective-permute-start | bytes 1572872 | tf_op jit(solution)/shard_map/ppermute | solution.py:673
  69.1 9.9 %collective-permute-start.22 = (f32[264,512]{1,0:T(8,128)S(1)}, f32[264,512]{1,0:T(8,128)S(1)}, u32[]{:S(2)}, u32[]{:S(2)}) collective-permute-start(f32[264,512]{1,0:T(8,128)S(1)} %get-tuple-element.201), channel_id=1, source_target_pairs={{0,1},{1,0},{2,3},{3,2},{4,5},{5,4},{6,7},{7,6},{8,9},{9,8},{10,11... | collective-permute-start | bytes 1622024 | tf_op jit(solution)/shard_map/ppermute | solution.py:673
  71.1 29.0 %collective-permute-start.29 = (f32[256,512]{1,0:T(8,128)S(1)}, f32[256,512]{1,0:T(8,128)S(1)}, u32[]{:S(2)}, u32[]{:S(2)}) collective-permute-start(f32[256,512]{1,0:T(8,128)S(1)} %stack.2.refs_3_.refs_0_), channel_id=1, source_target_pairs={{0,16},{4,20},{8,24},{12,28},{16,0},{20,4},{24,8},{28,12},{1,17},{... | collective-permute-start | bytes 1572872 | tf_op jit(solution)/shard_map/ppermute | solution.py:673
  73.9 33.5 %collective-permute-start.24 = (f32[512,512]{1,0:T(8,128)S(1)}, f32[512,512]{1,0:T(8,128)S(1)}, u32[]{:S(2)}, u32[]{:S(2)}) collective-permute-start(f32[512,512]{1,0:T(8,128)S(1)} %edge_add.1.refs_5_.refs_0_), channel_id=1, source_target_pairs={{0,2},{1,3},{2,0},{3,1},{4,6},{5,7},{6,4},{7,5},{8,10},{9,11},{10,... | collective-permute-start | bytes 3145736 | tf_op jit(solution)/shard_map/ppermute | solution.py:673
  79.2 19.2 %collective-permute-start.25 = (f32[136,512]{1,0:T(8,128)S(1)}, f32[136,512]{1,0:T(8,128)S(1)}, u32[]{:S(2)}, u32[]{:S(2)}) collective-permute-start(f32[136,512]{1,0:T(8,128)S(1)} %get-tuple-element.209), channel_id=1, source_target_pairs={{0,8},{4,12},{8,0},{12,4},{16,24},{20,28},{24,16},{28,20},{1,9},{5... | collective-permute-start | bytes 835592 | tf_op jit(solution)/shard_map/ppermute | solution.py:673
  80.4 8.6 %collective-permute-start.26 = (f32[128,512]{1,0:T(8,128)S(1)}, f32[128,512]{1,0:T(8,128)S(1)}, u32[]{:S(2)}, u32[]{:S(2)}) collective-permute-start(f32[128,512]{1,0:T(8,128)S(1)} %get-tuple-element.210), channel_id=1, source_target_pairs={{0,4},{4,0},{8,12},{12,8},{16,20},{20,16},{24,28},{28,24},{1,5},{5... | collective-permute-start | bytes 786440 | tf_op jit(solution)/shard_map/ppermute | solution.py:673
  100.2 9.4 %collective-permute-start.32 = (f32[128,512]{1,0:T(8,128)S(1)}, f32[128,512]{1,0:T(8,128)S(1)}, u32[]{:S(2)}, u32[]{:S(2)}) collective-permute-start(f32[128,512]{1,0:T(8,128)S(1)} %get-tuple-element.218.refs_0_), channel_id=1, source_target_pairs={{0,4},{4,0},{8,12},{12,8},{16,20},{20,16},{24,28},{28,24},{1,5},{5... | collective-permute-start | bytes 786440 | tf_op jit(solution)/shard_map/ppermute | solution.py:673
  100.7 16.9 %collective-permute-start.31 = (f32[128,512]{1,0:T(8,128)S(1)}, f32[128,512]{1,0:T(8,128)S(1)}, u32[]{:S(2)}, u32[]{:S(2)}) collective-permute-start(f32[128,512]{1,0:T(8,128)S(1)} %get-tuple-element.217.refs_5_.refs_0_), channel_id=1, source_target_pairs={{0,8},{4,12},{8,0},{12,4},{16,24},{20,28},{24,16},{28,20},{1,9},{5... | collective-permute-start | bytes 786440 | tf_op jit(solution)/shard_map/ppermute | solution.py:673
  106.6 12.6 %collective-permute-start.33 = (f32[136,512]{1,0:T(8,128)S(1)}, f32[136,512]{1,0:T(8,128)S(1)}, u32[]{:S(2)}, u32[]{:S(2)}) collective-permute-start(f32[136,512]{1,0:T(8,128)S(1)} %stack.3.refs_7_.refs_0_), channel_id=1, source_target_pairs={{0,16},{4,20},{8,24},{12,28},{16,0},{20,4},{24,8},{28,12},{1,17},{... | collective-permute-start | bytes 835592 | tf_op jit(solution)/shard_map/ppermute | solution.py:673
  107.9 9.8 %collective-permute-start.30 = (f32[512,512]{1,0:T(8,128)S(1)}, f32[512,512]{1,0:T(8,128)S(1)}, u32[]{:S(2)}, u32[]{:S(2)}) collective-permute-start(f32[512,512]{1,0:T(8,128)S(1)} %frames_back.1.refs_2_.refs_0_), channel_id=1, source_target_pairs={{0,1},{1,0},{2,3},{3,2},{4,5},{5,4},{6,7},{7,6},{8,9},{9,8},{10,11... | collective-permute-start | bytes 3145736 | tf_op jit(solution)/shard_map/ppermute | solution.py:673
  109.7 24.1 %collective-permute-start.40 = (f32[256,512]{1,0:T(8,128)S(1)}, f32[256,512]{1,0:T(8,128)S(1)}, u32[]{:S(2)}, u32[]{:S(2)}) collective-permute-start(f32[256,512]{1,0:T(8,128)S(1)} %join.3.refs_2_.refs_0_), channel_id=1, source_target_pairs={{0,8},{4,12},{8,0},{12,4},{16,24},{20,28},{24,16},{28,20},{1,9},{5... | collective-permute-start | bytes 1572872 | tf_op jit(solution)/shard_map/ppermute | solution.py:673
  117.7 17.0 %collective-permute-start.39 = (f32[256,512]{1,0:T(8,128)S(1)}, f32[256,512]{1,0:T(8,128)S(1)}, u32[]{:S(2)}, u32[]{:S(2)}) collective-permute-start(f32[256,512]{1,0:T(8,128)S(1)} %join.4.refs_2_.refs_0_), channel_id=1, source_target_pairs={{0,4},{4,0},{8,12},{12,8},{16,20},{20,16},{24,28},{28,24},{1,5},{5... | collective-permute-start | bytes 1572872 | tf_op jit(solution)/shard_map/ppermute | solution.py:673
  119.2 10.4 %collective-permute-start.35 = (f32[64,512]{1,0:T(8,128)S(1)}, f32[64,512]{1,0:T(8,128)S(1)}, u32[]{:S(2)}, u32[]{:S(2)}) collective-permute-start(f32[64,512]{1,0:T(8,128)S(1)} %get-tuple-element.222.refs_0_), channel_id=1, source_target_pairs={{0,4},{4,0},{8,12},{12,8},{16,20},{20,16},{24,28},{28,24},{1,5},{5... | collective-permute-start | bytes 393224 | tf_op jit(solution)/shard_map/ppermute | solution.py:673
  121.3 9.3 %collective-permute-start.36 = (f32[64,512]{1,0:T(8,128)S(1)}, f32[64,512]{1,0:T(8,128)S(1)}, u32[]{:S(2)}, u32[]{:S(2)}) collective-permute-start(f32[64,512]{1,0:T(8,128)S(1)} %get-tuple-element.223.refs_1_), channel_id=1, source_target_pairs={{0,8},{4,12},{8,0},{12,4},{16,24},{20,28},{24,16},{28,20},{1,9},{5... | collective-permute-start | bytes 393224 | tf_op jit(solution)/shard_map/ppermute | solution.py:673
  (18 other events, 113.2 us)

commit v3 on v2

--- a/solution.py
+++ b/solution.py
@@ -444,7 +444,11 @@
     hidden = own_ref.shape[0]
     for place, outs in enumerate(((own_ref,), pair)):
         at = slice(place * hidden, (place + 1) * hidden)
-        put_rows(mm(h_0[:, at], g_0[...], 0, 0) + mm(h_1[:, at], g_1[...], 0, 0), outs)
+        value = mm(h_0[:, at], g_0[...], 0, 0) + mm(h_1[:, at], g_1[...], 0, 0)
+        for out_ref in outs:
+            out_ref[:hidden] = value
+            if out_ref.shape[0] > hidden:
+                out_ref[hidden:] = jnp.zeros((out_ref.shape[0] - hidden, value.shape[1]), F32)
     vec_ref[...] = column_sums(g_0[...]) + column_sums(g_1[...])
 
 
@@ -498,7 +502,7 @@
 
 def project_weights_kernel(
     normed, normed_edge, dq_0, dq_1, dkv_0, dkv_1, wo_own_0, wo_own_1, wo_pair_0, wo_pair_1, mid_0, mid_1, first, vec_outer, vec_inner,
-    own_0, own_1, rows_ref, pair_0, pair_1, message, sums, row,
+    own_ref, rows_ref, pair_0, pair_1, sums, row,
 ):
     features = normed.shape[2]
     width = wo_own_0.shape[1]
@@ -517,21 +521,22 @@
     rows_ref[3:5] = first[...]
     rows_ref[5:6] = vec_outer[...] * 0.5
     rows_ref[6:] = jnp.zeros((2, features), F32)
-    half = own_0.shape[0]
-    pair_0[half : half + 6] = rows_ref[0:6]
-    pair_0[half + 6 :] = jnp.zeros((2, features), F32)
-    for place, (out_ref, at) in enumerate(((rows_ref, 6), (pair_0, half + 6))):
+    half = pair_0.shape[0]
+    pair_1[half : half + 6] = rows_ref[0:6]
+    pair_1[half + 6 :] = jnp.zeros((2, features), F32)
+    for place, (out_ref, at) in enumerate(((rows_ref, 6), (pair_1, half + 6))):
         for number in range(3):
             lanes = slice(number * width, (number + 1) * width)
             out_ref[at : at + 1, lanes] = row[:, lanes_of(place, width, 2 * number * width)]
         out_ref[at + 1 : at + 2, :hidden] = vec_inner[place : place + 1]
-    for place, (outs, wo_0, wo_1) in enumerate((((own_0, own_1), wo_own_0, wo_own_1), ((pair_0, pair_1), wo_pair_0, wo_pair_1))):
-        for number in range(3):
-            lanes = slice(number * width, (number + 1) * width)
-            message[:, lanes] = sums[:, lanes_of(place, width, 2 * number * width)]
-        message[:, 3 * width :] = wo_0[...] + wo_1[...]
-        for number, out_ref in enumerate(outs):
-            out_ref[:half] = message[number * half : (number + 1) * half]
+    shares = (((own_ref, slice(None)),), ((pair_0, slice(half)), (pair_1, slice(half, features))))
+    for place, (share, wo_0, wo_1) in enumerate(((shares[0], wo_own_0, wo_own_1), (shares[1], wo_pair_0, wo_pair_1))):
+        for out_ref, rows in share:
+            count = half if place else features
+            for number in range(3):
+                lanes = slice(number * width, (number + 1) * width)
+                out_ref[:count, lanes] = sums[rows, lanes_of(place, width, 2 * number * width)]
+            out_ref[:count, 3 * width :] = wo_0[rows] + wo_1[rows]
 
 
 def frames_back_kernel(a_ref, b_ref, xhat, rate, dmid_0, dmid_1, params, out):
@@ -568,7 +573,7 @@
         take = min(piece.shape[0], count - at)
         if take:
             out[at : at + take] = a_ref[at : at + take] + piece[:take]
-        if take < piece.shape[0]:
+        if take < piece.shape[0] and new_rows is not None:
             new_rows[...] = rows_ref[...] + piece[take:]
         at += take
 
@@ -603,6 +608,18 @@
         out_ref[half:] = rows_ref[...] + b_ref[half:]
 
 
+def add_cut_kernel(bit, a_ref, rows_ref, *refs):
+    *pieces, kept, sent_0, sent_1, new_rows, work = refs
+    half, cut = kept.shape[0], sent_0.shape[0]
+    add_pieces(work, a_ref, pieces, rows_ref, new_rows)
+    place = place_of(bit)
+    kept[...] = work[half_rows(place, half)]
+    sent = work[half_rows(1 - place, half)]
+    sent_0[...] = sent[:cut]
+    sent_1[: half - cut] = sent[cut:]
+    sent_1[half - cut :] = new_rows[...]
+
+
 def stack_kernel(rows, a_0, a_1, *refs):
     rows_ref, refs = (refs[0], refs[1:]) if rows else (None, refs)
     b_0, b_1, out_ref = refs
@@ -638,19 +655,20 @@
 
 
 def join_heads_kernel(bits, *refs):
-    *parts, wq, wk, wv, wo = refs
+    *parts, wq, wk, wv, wo, work = refs
     width = wq.shape[1]
-    at = 0
-    for number, bit in enumerate(bits):
-        mine, theirs = parts[2 * number : 2 * number + 2]
-        half = mine.shape[0]
-        place = place_of(bit)
-        for where, part in ((place, mine), (1 - place, theirs)):
-            rows = pl.ds(pl.multiple_of(at + where * half, half), half)
-            for heads, out in enumerate((wq, wk, wv)):
-                out[rows, :] = part[:, heads * width : (heads + 1) * width]
-            wo[:, rows] = part[:, 3 * width :].T
-        at += 2 * half
+    count = parts[0].shape[0] // 2
+    first, second = (place_of(bit) for bit in bits)
+    for number in range(2):
+        place = first if number else second
+        for where, part in ((place, parts[2 * number]), (1 - place, parts[2 * number + 1])):
+            for joined in range(2):
+                start = where * 4 * count + joined * 2 * count + count if number else joined * 4 * count + where * 2 * count
+                rows = pl.ds(pl.multiple_of(start, count), count)
+                here = slice(joined * count, (joined + 1) * count)
+                for heads, out in enumerate((wq, wk, wv, work)):
+                    out[rows, :] = part[here, heads * width : (heads + 1) * width]
+    wo[...] = work[...].T
 
 
 def small_kernel(rows, far, outs):
@@ -695,9 +713,12 @@
         self.rows = [] if rows is None else [rows]
         self.apart = [(bits[1], bits[0]), (bits[0], bits[1])]
         self.together, self.last = bits[2:-1], bits[-1]
-        self.todo = [("split", pair) for pair in self.apart]
-        self.todo.append(("stack",))
-        self.todo += [("split", (bit,)) for bit in self.together] + [("last",)] * bool(self.together)
+        if len(a) == 1:
+            self.todo = [("cut", bits[0])] + [("split", (bit,)) for bit in bits[1:-1]] + [("last",)]
+        else:
+            self.todo = [("split", pair) for pair in self.apart]
+            self.todo.append(("stack",))
+            self.todo += [("split", (bit,)) for bit in self.together] + [("last",)] * bool(self.together)
         self.todo.append(("add",))
         self.todo += [("join", (bit,)) for bit in reversed(self.together)] + [("part",)] * bool(self.together)
         self.todo.append(("join", self.apart[1]))
@@ -712,6 +733,15 @@
         has_rows = bool(self.rows)
         shape = lambda rows: (rows, features)
         got = [piece for pieces in self.got for piece in pieces]
+        if kind == "cut":
+            half = count // 2
+            (value, *sent, rows) = run.call(
+                functools.partial(add_cut_kernel, rest[0]), "add_cut",
+                [shape(half), shape(half // 2), shape(half // 2 + more), self.rows[0].shape], (*values, *self.rows, *got),
+                scratch=[shape(count)],
+            )
+            self.values, self.rows, self.got = [value], [rows], [[swap(v, "tm", rest[0]) for v in sent]]
+            return
         if kind == "split":
             (bits,) = rest
             half = count // 2
@@ -925,7 +955,7 @@
         features, hidden = self.features, self.hidden
         self.outer_own, *pair, self.vec_outer = self.run.call(
             outer_weights_kernel, "outer_weights",
-            [(hidden, features)] + [(hidden // PIECES, features)] * PIECES + [(1, features)],
+            [(hidden, features), (hidden + 8, features), (1, features)],
             (self.fed[0][1], self.fed[1][1], *self.g),
         )
         self.outer_pair = swap_near(pair)
@@ -981,19 +1011,18 @@
 
     def project_weights(self):
         features, width = self.features, self.width
-        *self.heads_own, self.rows, a, b = self.run.call(
+        self.heads_own, self.rows, *pair = self.run.call(
             project_weights_kernel, "project_weights",
-            [(features // 2, 4 * width)] * 2 + [(8, features), (features // 2 + 8, 4 * width), (features // 2, 4 * width)],
+            [(features, 4 * width), (8, features), (features // 2, 4 * width), (features // 2 + 8, 4 * width)],
             (self.normed, self.normed_edge, *self.pick(1), *self.pick(2), *self.pick(3), *self.pick(4), *self.pick(5),
              self.vec_first, self.vec_outer, self.vec_inner),
-            scratch=[(features, 4 * width), (features, 6 * width), (1, 6 * width)],
-        )
-        self.heads_pair = swap_near((a, b))
+            scratch=[(features, 6 * width), (1, 6 * width)],
+        )
+        self.heads_pair = tuple(swap(v, "head", 1) for v in pair)
 
     def begin(self, name):
         if name == "heads":
-            a, b = self.heads_pair
-            return SumsOverTm(self.run, self.heads_own, ((a,), (b,)), self.rows)
+            return SumsOverTm(self.run, (self.heads_own,), (self.heads_pair,), self.rows)
         return SumsOverTm(self.run, (self.outer_own, self.inner_own), (self.outer_pair, self.inner_pair))
 
     def sum(self, name):
@@ -1056,11 +1085,11 @@
         features, width, hidden = self.features, self.width, self.hidden
         sums = self.sums["heads"]
         rows = sums.rows[0]
-        bits, parts = zip(*(sums.halves(i) for i in range(2)), strict=True)
+        bits, parts = sums.apart[1], [sums.halves(i)[1] for i in range(2)]
         out = self.run.call(
-            functools.partial(finish_kernel, list(bits)), "finish",
+            functools.partial(finish_kernel, bits), "finish",
             [(1, features)] * 6 + [(1, width)] * 2 + [(1, hidden)] + [(features, width)] * 3 + [(width, features)],
-            (rows, swap(rows, "head", 2), *parts[0], *parts[1]),
+            (rows, swap(rows, "head", 2), *parts[0], *parts[1]), scratch=[(features, width)],
         )
         bo, g2, s2, g1, s1, bu, bq, bv, bi = (v.reshape(v.shape[1]) for v in out[:9])
         wq, wk, wv, wo = out[9:]

time: 139 us -> 139 us (level)
  waiting for transfers between devices: 44.4 us -> 42.3 us
  starting transfers between devices: 43.8 us -> 45.7 us
    ppermute x39 -> x38, waiting for transfers between devices: 44.4 us -> 42.2 us  [swap(): return lax.ppermute(value, axis, [(i, i ^ bit) for i in range(size)])]
    ppermute x39 -> x38, starting transfers between devices: 38.7 us -> 40.6 us  [swap(): return lax.ppermute(value, axis, [(i, i ^ bit) for i in range(size)])]
  transfers between devices with their start and end apart: 41 -> 40, of which waited for: 14 -> 15; matrix products, arithmetic and copies ran while one was open for 0% -> 0% of each run, Pallas kernels for 34% -> 34%
where the time goes in v3:
time: 139 us
  Pallas kernels  49.7 us (36%)
  starting transfers between devices  45.7 us (33%)
  waiting for transfers between devices  42.3 us (30%)
    pallas_call x39, Pallas kernels, call(): pl.pallas_call(body, name=name, grid=(1,), in_specs=[in_hbm if i in far e...  49.7 us
    ppermute x38, waiting for transfers between devices, swap(): return lax.ppermute(value, axis, [(i, i ^ bit) for i in range(size)])  42.2 us
    ppermute x38, starting transfers between devices, swap(): return lax.ppermute(value, axis, [(i, i ^ bit) for i in range(size)])  40.6 us
    ppermute x2, starting transfers between devices, swap_edges(): return lax.ppermute(value, ('tm', 'head'), pairs)  5.1 us
  transfers between devices with their start and end apart: 40, of which 15 were waited for; matrix products, arithmetic and copies ran while one was open for 0% of the time, Pallas kernels for 34%

profile of v3, /device:TPU:0, one launch (start us, length us, event | category | flops | bytes accessed | tf_op | source)
XLA Modules:
  0.0 138.7 jit_solution(13100440070022251274)
XLA Ops:
  2.6 4.4 %collective-permute-start.1 = (f32[2,64,512]{2,1,0:T(8,128)S(1)}, f32[2,64,512]{2,1,0:T(8,128)S(1)}, u32[]{:S(2)}, u32[]{:S(2)}) collective-permute-start(f32[2,64,512]{2,1,0:T(8,128)S(1)} %get-tuple-element.126.refs_7_), channel_id=1, source_target_pairs={{0,4},{2,6},{4,8},{5,1},{6,10},{7,3},{8,12},{9,5},{10,14},{11,7},{... | collective-permute-start | bytes 786440 | tf_op jit(solution)/shard_map/ppermute | solution.py:706
  7.0 2.5 %norm.1 = (f32[2,256,512]{2,1,0:T(8,128)S(1)}, f32[2,256,512]{2,1,0:T(8,128)S(1)}, f32[2,256,128]{2,1,0:T(8,128)S(1)}, f32[2,256,512]{2,1,0:T(8,128)S(1)}, f32[5...) custom-call(f32[2,512,512]{2,1,0:T(8,128)} %refs_0_.6, ...), custom_call_target="tpu_custom_call" | custom-call | flops 2486400000 | tf_op jit(solution)/shard_map/norm/pallas_call | solution.py:118
  11.6 1.9 %project.1 = (f32[2,256,256]{2,1,0:T(8,128)S(1)}, f32[2,256,512]{2,1,0:T(8,128)S(1)}, f32[512,768]{1,0:T(8,128)S(1)}, f32[1,768]{1,0:T(1,128)S(1)}, f32[7,1,512]{2,1,0:T(1,128)S(1)}) custom-call(f32[2,256,512]{2,1,0:T(8,128)S(1)} %get-tuple-element.127.refs_0_, f32[520,512]{1,0:T(8,128)S(1)} %get-tuple-element.128.refs_1_.refs_0_, ...), custom_call_target="tpu_custom_call" | custom-call | flops 1139600000 | tf_op jit(solution)/shard_map/project/pallas_call | solution.py:118
  13.5 3.7 %attend_inner.1 = (f32[128,256]{1,0:T(8,128)S(1)}, f32[128,256]{1,0:T(8,128)S(1)}, f32[2,2,2,128,128]{4,3,2,1,0:T(8,128)S(1)}) custom-call(s32[2,4]{1,0:T(2,128)S(1)} %copy-done, f32[2,256,256]{2,1,0:T(8,128)S(1)} %get-tuple-element.130.refs_1_.refs_7_, f32[2,256,512]{2,1,0:T(8,128)S(1)} %get-tuple-element.131.refs_2_.refs_8_, ...), custom_call_target="tpu_custom_call" | custom-call | flops 5697999872 | tf_op jit(solution)/shard_map/attend_inner/pallas_call | solution.py:118
  19.0 2.1 %attend_outer.2 = (f32[128,256]{1,0:T(8,128)S(1)}, f32[2,2,128,128]{3,2,1,0:T(8,128)S(1)}) custom-call(s32[2,4]{1,0:T(2,128)S(1)} %copy-done, f32[2,256,256]{2,1,0:T(8,128)S(1)} %get-tuple-element.130.refs_1_.refs_7_, f32[2,256,512]{2,1,0:T(8,128)S(1)} %get-tuple-element.131.refs_2_.refs_8_, f32[2,72,512]{2,1,0:T(8,128)S(1)} %get-tuple-element.138.refs_3_.refs_9_, ...), custom_call_target="tpu_custom_call" | custom-call | flops 12432000000 | tf_op jit(solution)/shard_map/attend_outer/pallas_call | solution.py:118
  23.2 2.1 %attend_outer.3 = (f32[128,256]{1,0:T(8,128)S(1)}, f32[2,2,128,128]{3,2,1,0:T(8,128)S(1)}) custom-call(s32[2,4]{1,0:T(2,128)S(1)} %copy-done, f32[2,256,256]{2,1,0:T(8,128)S(1)} %get-tuple-element.130.refs_1_.refs_7_, f32[2,256,512]{2,1,0:T(8,128)S(1)} %get-tuple-element.131.refs_2_.refs_8_, f32[2,72,512]{2,1,0:T(8,128)S(1)} %get-tuple-element.138.refs_3_.refs_9_, ...), custom_call_target="tpu_custom_call" | custom-call | flops 518000000 | tf_op jit(solution)/shard_map/attend_outer/pallas_call | solution.py:118
  27.4 3.9 %feed.2 = (f32[256,512]{1,0:T(8,128)S(1)}, f32[256,1024]{1,0:T(8,128)S(1)}, f32[256,1024]{1,0:T(8,128)S(1)}, f32[256,512]{1,0:T(8,128)S(1)}, f32[256,512]{1,0:T(8,128)S(1)}) custom-call(f32[128,256]{1,0:T(8,128)S(1)} %get-tuple-element.133.refs_0_.refs_5_, f32[128,256]{1,0:T(8,128)S(1)} %get-tuple-element.141.refs_1_.refs_6_, ...), custom_call_target="tpu_custom_call" | custom-call | flops 9324000256 | tf_op jit(solution)/shard_map/feed/pallas_call | solution.py:118
  32.8 4.1 %feed.3 = (f32[256,512]{1,0:T(8,128)S(1)}, f32[256,1024]{1,0:T(8,128)S(1)}, f32[256,1024]{1,0:T(8,128)S(1)}, f32[256,512]{1,0:T(8,128)S(1)}, f32[256,512]{1,0:T(8,128)S(1)}) custom-call(f32[128,256]{1,0:T(8,128)S(1)} %get-tuple-element.150.refs_0_.refs_5_, f32[128,256]{1,0:T(8,128)S(1)} %get-tuple-element.151.refs_1_.refs_6_, ...), custom_call_target="tpu_custom_call" | custom-call | flops 7251999744 | tf_op jit(solution)/shard_map/feed/pallas_call | solution.py:118
  38.9 1.9 %inner_weights.1 = (f32[512,512]{1,0:T(8,128)S(1)}, f32[512,512]{1,0:T(8,128)S(1)}, f32[2,512]{1,0:T(2,128)S(1)}) custom-call(f32[256,512]{1,0:T(8,128)S(1)} %get-tuple-element.157.refs_0_, f32[256,512]{1,0:T(8,128)S(1)} %get-tuple-element.158.refs_1_, f32[256,1024]{1,0:T(8,128)S(1)} %get-tuple-element.159.refs_2_, ...), custom_call_target="tpu_custom_call" | custom-call | flops 5697999872 | tf_op jit(solution)/shard_map/inner_weights/pallas_call | solution.py:118
  42.6 2.1 %feed_out.1.refs_2_ = f32[512,512]{1,0:T(8,128)S(1)} custom-call(f32[256,1024]{1,0:T(8,128)S(1)} %get-tuple-element.155.refs_0_, f32[256,1024]{1,0:T(8,128)S(1)} %get-tuple-element.156.refs_1_, f32[512,512]{1,0:T(8,128)S(1)} %get-tuple-element.146.refs_13_.refs_2_, f32[512,512]{1,0:T(8,128)S(1)} %collective-permute-done.7.refs_14_.refs_3_, ...), custom_call_target="tpu_custom_call" | custom-call | flops 310800000 | tf_op jit(solution)/shard_map/feed_out/pallas_call | solution.py:118
  49.1 4.5 %back.2 = (f32[256,512]{1,0:T(8,128)S(1)}, f32[256,256]{1,0:T(8,128)S(1)}, f32[328,512]{1,0:T(8,128)S(1)}, f32[512,128]{1,0:T(8,128)S(1)}, f32[512,128]{1,0:T(8,128)S(1)}, /*index=5*/f32[3,512]{1,0:T(4,128)S(1)}) custom-call(f32[256,512]{1,0:T(8,128)S(1)} %grad_sum.2.refs_4_.refs_0_, f32[256,512]{1,0:T(8,128)S(1)} %get-tuple-element.149.refs_1_.refs_0_, ...), custom_call_target="tpu_custom_call" | custom-call | flops 3108000000 | tf_op jit(solution)/shard_map/back/pallas_call | solution.py:118
  53.7 2.5 %collective-permute-done.14.refs_1_ = f32[256,512]{1,0:T(8,128)S(1)} collective-permute-done((f32[256,512]{1,0:T(8,128)S(1)}, f32[256,512]{1,0:T(8,128)S(1)}, u32[]{:S(2)}, u32[]{:S(2)}) %collective-permute-start.14) | collective-permute-done | bytes 524320 | tf_op jit(solution)/shard_map/ppermute | solution.py:691
  56.2 4.3 %back.3 = (f32[256,512]{1,0:T(8,128)S(1)}, f32[256,256]{1,0:T(8,128)S(1)}, f32[328,512]{1,0:T(8,128)S(1)}, f32[512,128]{1,0:T(8,128)S(1)}, f32[512,128]{1,0:T(8,128)S(1)}, /*index=5*/f32[3,512]{1,0:T(4,128)S(1)}) custom-call(f32[256,512]{1,0:T(8,128)S(1)} %grad_sum.3.refs_0_.refs_12_, f32[256,512]{1,0:T(8,128)S(1)} %get-tuple-element.154.refs_1_, ...), custom_call_target="tpu_custom_call" | custom-call | flops 259000000 | tf_op jit(solution)/shard_map/back/pallas_call | solution.py:118
  66.5 2.6 %project_weights.1 = (f32[512,512]{1,0:T(8,128)S(1)}, f32[8,512]{1,0:T(8,128)S(1)}, f32[256,512]{1,0:T(8,128)S(1)}, f32[264,512]{1,0:T(8,128)S(1)}) custom-call(f32[2,256,512]{2,1,0:T(8,128)S(1)} %get-tuple-element.127.refs_0_, f32[2,72,512]{2,1,0:T(8,128)S(1)} %get-tuple-element.187.refs_1_, f32[256,256]{1,0:T(8,128)S(1)} %get-tuple-element.169.refs_0_.refs_2_, ...), custom_call_target="tpu_custom_call" | custom-call | flops 1036000000 | tf_op jit(solution)/shard_map/project_weights/pallas_call | solution.py:118
  71.1 2.7 %collective-permute-start.28 = (f32[256,512]{1,0:T(8,128)S(1)}, f32[256,512]{1,0:T(8,128)S(1)}, u32[]{:S(2)}, u32[]{:S(2)}) collective-permute-start(f32[256,512]{1,0:T(8,128)S(1)} %stack.2.refs_3_.refs_0_), channel_id=1, source_target_pairs={{0,16},{4,20},{8,24},{12,28},{16,0},{20,4},{24,8},{28,12},{1,17},{... | collective-permute-start | bytes 1572872 | tf_op jit(solution)/shard_map/ppermute | solution.py:691
  75.7 2.9 %collective-permute-done.10.refs_3_ = f32[512,512]{1,0:T(8,128)S(1)} collective-permute-done((f32[512,512]{1,0:T(8,128)S(1)}, f32[512,512]{1,0:T(8,128)S(1)}, u32[]{:S(2)}, u32[]{:S(2)}) %collective-permute-start.10) | collective-permute-done | bytes 1048608 | tf_op jit(solution)/shard_map/ppermute | solution.py:691
  83.0 10.9 %collective-permute-done.25.refs_2_ = f32[128,512]{1,0:T(8,128)S(1)} collective-permute-done((f32[128,512]{1,0:T(8,128)S(1)}, f32[128,512]{1,0:T(8,128)S(1)}, u32[]{:S(2)}, u32[]{:S(2)}) %collective-permute-start.25) | collective-permute-done | bytes 262176 | tf_op jit(solution)/shard_map/ppermute | solution.py:691
  95.4 2.3 %collective-permute-done.28.refs_1_ = f32[256,512]{1,0:T(8,128)S(1)} collective-permute-done((f32[256,512]{1,0:T(8,128)S(1)}, f32[256,512]{1,0:T(8,128)S(1)}, u32[]{:S(2)}, u32[]{:S(2)}) %collective-permute-start.28) | collective-permute-done | bytes 524320 | tf_op jit(solution)/shard_map/ppermute | solution.py:691
  99.4 4.2 %collective-permute-done.27.refs_2_ = f32[136,512]{1,0:T(8,128)S(1)} collective-permute-done((f32[136,512]{1,0:T(8,128)S(1)}, f32[136,512]{1,0:T(8,128)S(1)}, u32[]{:S(2)}, u32[]{:S(2)}) %collective-permute-start.27) | collective-permute-done | bytes 278560 | tf_op jit(solution)/shard_map/ppermute | solution.py:691
  103.7 2.4 %collective-permute-start.32 = (f32[136,512]{1,0:T(8,128)S(1)}, f32[136,512]{1,0:T(8,128)S(1)}, u32[]{:S(2)}, u32[]{:S(2)}) collective-permute-start(f32[136,512]{1,0:T(8,128)S(1)} %stack.3.refs_7_.refs_0_), channel_id=1, source_target_pairs={{0,16},{4,20},{8,24},{12,28},{16,0},{20,4},{24,8},{28,12},{1,17},{... | collective-permute-start | bytes 835592 | tf_op jit(solution)/shard_map/ppermute | solution.py:691
  108.6 3.5 %collective-permute-done.30.refs_1_ = f32[128,512]{1,0:T(8,128)S(1)} collective-permute-done((f32[128,512]{1,0:T(8,128)S(1)}, f32[128,512]{1,0:T(8,128)S(1)}, u32[]{:S(2)}, u32[]{:S(2)}) %collective-permute-start.30) | collective-permute-done | bytes 262176 | tf_op jit(solution)/shard_map/ppermute | solution.py:691
  115.2 4.0 %collective-permute-done.32.refs_1_ = f32[136,512]{1,0:T(8,128)S(1)} collective-permute-done((f32[136,512]{1,0:T(8,128)S(1)}, f32[136,512]{1,0:T(8,128)S(1)}, u32[]{:S(2)}, u32[]{:S(2)}) %collective-permute-start.32) | collective-permute-done | bytes 278560 | tf_op jit(solution)/shard_map/ppermute | solution.py:691
  120.9 7.8 %collective-permute-done.34.refs_2_ = f32[64,512]{1,0:T(8,128)S(1)} collective-permute-done((f32[64,512]{1,0:T(8,128)S(1)}, f32[64,512]{1,0:T(8,128)S(1)}, u32[]{:S(2)}, u32[]{:S(2)}) %collective-permute-start.34) | collective-permute-done | bytes 131104 | tf_op jit(solution)/shard_map/ppermute | solution.py:691
  135.0 2.5 %collective-permute-done.36.refs_3_ = f32[128,512]{1,0:T(8,128)S(1)} collective-permute-done((f32[128,512]{1,0:T(8,128)S(1)}, f32[128,512]{1,0:T(8,128)S(1)}, u32[]{:S(2)}, u32[]{:S(2)}) %collective-permute-start.36) | collective-permute-done | bytes 262176 | tf_op jit(solution)/shard_map/ppermute | solution.py:691
  (97 shorter events, 52.0 us)
Async XLA Ops:
  2.1 9.5 %collective-permute-start = (f32[520,512]{1,0:T(8,128)S(1)}, f32[520,512]{1,0:T(8,128)S(1)}, u32[]{:S(2)}, u32[]{:S(2)}) collective-permute-start(f32[520,512]{1,0:T(8,128)S(1)} %get-tuple-element.128.refs_1_.refs_0_), channel_id=1, source_target_pairs={{0,1},{1,0},{2,3},{3,2},{4,5},{5,4},{6,7},{7,6},{8,9},{9,8},{10,11... | collective-permute-start | bytes 3194888 | tf_op jit(solution)/shard_map/ppermute | solution.py:691
  2.6 15.2 %collective-permute-start.1 = (f32[2,64,512]{2,1,0:T(8,128)S(1)}, f32[2,64,512]{2,1,0:T(8,128)S(1)}, u32[]{:S(2)}, u32[]{:S(2)}) collective-permute-start(f32[2,64,512]{2,1,0:T(8,128)S(1)} %get-tuple-element.126.refs_7_), channel_id=1, source_target_pairs={{0,4},{2,6},{4,8},{5,1},{6,10},{7,3},{8,12},{9,5},{10,14},{11,7},{... | collective-permute-start | bytes 786440 | tf_op jit(solution)/shard_map/ppermute | solution.py:706
  9.5 9.3 %collective-permute-start.2 = (f32[128,512]{1,0:T(8,128)S(1)}, f32[128,512]{1,0:T(8,128)S(1)}, u32[]{:S(2)}, u32[]{:S(2)}) collective-permute-start(f32[128,512]{1,0:T(8,128)S(1)} %get-tuple-element.139), channel_id=1, source_target_pairs={{0,2},{1,3},{2,0},{3,1},{4,6},{5,7},{6,4},{7,5},{8,10},{9,11},{10,... | collective-permute-start | bytes 786440 | tf_op jit(solution)/shard_map/ppermute | solution.py:691
  11.1 14.2 %collective-permute-start.7 = (f32[512,512]{1,0:T(8,128)S(1)}, f32[512,512]{1,0:T(8,128)S(1)}, u32[]{:S(2)}, u32[]{:S(2)}) collective-permute-start(f32[512,512]{1,0:T(8,128)S(1)} %get-tuple-element.146.refs_13_.refs_2_), channel_id=1, source_target_pairs={{0,1},{1,0},{2,3},{3,2},{4,5},{5,4},{6,7},{7,6},{8,9},{9,8},{10,11... | collective-permute-start | bytes 3145736 | tf_op jit(solution)/shard_map/ppermute | solution.py:691
  11.1 15.8 %collective-permute-start.6 = (f32[512,512]{1,0:T(8,128)S(1)}, f32[512,512]{1,0:T(8,128)S(1)}, u32[]{:S(2)}, u32[]{:S(2)}) collective-permute-start(f32[512,512]{1,0:T(8,128)S(1)} %get-tuple-element.145.refs_11_), channel_id=1, source_target_pairs={{0,1},{1,0},{2,3},{3,2},{4,5},{5,4},{6,7},{7,6},{8,9},{9,8},{10,11... | collective-permute-start | bytes 3145736 | tf_op jit(solution)/shard_map/ppermute | solution.py:691
  22.7 10.1 %collective-permute-start.8 = (f32[128,256]{1,0:T(8,128)S(1)}, f32[128,256]{1,0:T(8,128)S(1)}, u32[]{:S(2)}, u32[]{:S(2)}) collective-permute-start(f32[128,256]{1,0:T(8,128)S(1)} %get-tuple-element.150.refs_0_.refs_5_), channel_id=1, source_target_pairs={{0,2},{1,3},{2,0},{3,1},{4,6},{5,7},{6,4},{7,5},{8,10},{9,11},{10,... | collective-permute-start | bytes 393224 | tf_op jit(solution)/shard_map/ppermute | solution.py:691
  31.2 14.2 %collective-permute-start.11 = (f32[256,512]{1,0:T(8,128)S(1)}, f32[256,512]{1,0:T(8,128)S(1)}, u32[]{:S(2)}, u32[]{:S(2)}) collective-permute-start(f32[256,512]{1,0:T(8,128)S(1)} %get-tuple-element.153.refs_15_.refs_0_), channel_id=1, source_target_pairs={{0,2},{1,3},{2,0},{3,1},{4,6},{5,7},{6,4},{7,5},{8,10},{9,11},{10,... | collective-permute-start | bytes 1572872 | tf_op jit(solution)/shard_map/ppermute | solution.py:691
  41.3 14.8 %collective-permute-start.14 = (f32[256,512]{1,0:T(8,128)S(1)}, f32[256,512]{1,0:T(8,128)S(1)}, u32[]{:S(2)}, u32[]{:S(2)}) collective-permute-start(f32[256,512]{1,0:T(8,128)S(1)} %get-tuple-element.161.refs_4_.refs_0_), channel_id=1, source_target_pairs={{0,2},{1,3},{2,0},{3,1},{4,6},{5,7},{6,4},{7,5},{8,10},{9,11},{10,... | collective-permute-start | bytes 1572872 | tf_op jit(solution)/shard_map/ppermute | solution.py:691
  44.7 33.9 %collective-permute-start.10 = (f32[512,512]{1,0:T(8,128)S(1)}, f32[512,512]{1,0:T(8,128)S(1)}, u32[]{:S(2)}, u32[]{:S(2)}) collective-permute-start(f32[512,512]{1,0:T(8,128)S(1)} %feed_out.1.refs_2_), channel_id=1, source_target_pairs={{0,2},{1,3},{2,0},{3,1},{4,6},{5,7},{6,4},{7,5},{8,10},{9,11},{10,... | collective-permute-start | bytes 3145736 | tf_op jit(solution)/shard_map/ppermute | solution.py:691
  45.9 14.6 %collective-permute-start.15 = (f32[256,512]{1,0:T(8,128)S(1)}, f32[256,512]{1,0:T(8,128)S(1)}, u32[]{:S(2)}, u32[]{:S(2)}) collective-permute-start(f32[256,512]{1,0:T(8,128)S(1)} %get-tuple-element.178), channel_id=1, source_target_pairs={{0,8},{4,12},{8,0},{12,4},{16,24},{20,28},{24,16},{28,20},{1,9},{5... | collective-permute-start | bytes 1572872 | tf_op jit(solution)/shard_map/ppermute | solution.py:691
  47.6 13.1 %collective-permute-start.16 = (f32[256,512]{1,0:T(8,128)S(1)}, f32[256,512]{1,0:T(8,128)S(1)}, u32[]{:S(2)}, u32[]{:S(2)}) collective-permute-start(f32[256,512]{1,0:T(8,128)S(1)} %get-tuple-element.168.refs_12_), channel_id=1, source_target_pairs={{0,4},{4,0},{8,12},{12,8},{16,20},{20,16},{24,28},{28,24},{1,5},{5... | collective-permute-start | bytes 1572872 | tf_op jit(solution)/shard_map/ppermute | solution.py:691
  62.4 8.5 %collective-permute-start.20 = (f32[128,512]{1,0:T(8,128)S(1)}, f32[128,512]{1,0:T(8,128)S(1)}, u32[]{:S(2)}, u32[]{:S(2)}) collective-permute-start(f32[128,512]{1,0:T(8,128)S(1)} %get-tuple-element.180.refs_7_), channel_id=1, source_target_pairs={{0,8},{4,12},{8,0},{12,4},{16,24},{20,28},{24,16},{28,20},{1,9},{5... | collective-permute-start | bytes 786440 | tf_op jit(solution)/shard_map/ppermute | solution.py:691
  69.1 9.9 %collective-permute-start.23 = (f32[264,512]{1,0:T(8,128)S(1)}, f32[264,512]{1,0:T(8,128)S(1)}, u32[]{:S(2)}, u32[]{:S(2)}) collective-permute-start(f32[264,512]{1,0:T(8,128)S(1)} %get-tuple-element.193.refs_4_), channel_id=1, source_target_pairs={{0,1},{1,0},{2,3},{3,2},{4,5},{5,4},{6,7},{7,6},{8,9},{9,8},{10,11... | collective-permute-start | bytes 1622024 | tf_op jit(solution)/shard_map/ppermute | solution.py:691
  71.1 26.6 %collective-permute-start.28 = (f32[256,512]{1,0:T(8,128)S(1)}, f32[256,512]{1,0:T(8,128)S(1)}, u32[]{:S(2)}, u32[]{:S(2)}) collective-permute-start(f32[256,512]{1,0:T(8,128)S(1)} %stack.2.refs_3_.refs_0_), channel_id=1, source_target_pairs={{0,16},{4,20},{8,24},{12,28},{16,0},{20,4},{24,8},{28,12},{1,17},{... | collective-permute-start | bytes 1572872 | tf_op jit(solution)/shard_map/ppermute | solution.py:691
  73.9 32.2 %collective-permute-start.24 = (f32[512,512]{1,0:T(8,128)S(1)}, f32[512,512]{1,0:T(8,128)S(1)}, u32[]{:S(2)}, u32[]{:S(2)}) collective-permute-start(f32[512,512]{1,0:T(8,128)S(1)} %edge_add.1.refs_5_.refs_0_), channel_id=1, source_target_pairs={{0,2},{1,3},{2,0},{3,1},{4,6},{5,7},{6,4},{7,5},{8,10},{9,11},{10,... | collective-permute-start | bytes 3145736 | tf_op jit(solution)/shard_map/ppermute | solution.py:691
  79.2 14.7 %collective-permute-start.26 = (f32[136,512]{1,0:T(8,128)S(1)}, f32[136,512]{1,0:T(8,128)S(1)}, u32[]{:S(2)}, u32[]{:S(2)}) collective-permute-start(f32[136,512]{1,0:T(8,128)S(1)} %get-tuple-element.204), channel_id=1, source_target_pairs={{0,4},{4,0},{8,12},{12,8},{16,20},{20,16},{24,28},{28,24},{1,5},{5... | collective-permute-start | bytes 835592 | tf_op jit(solution)/shard_map/ppermute | solution.py:691
  80.8 13.1 %collective-permute-start.25 = (f32[128,512]{1,0:T(8,128)S(1)}, f32[128,512]{1,0:T(8,128)S(1)}, u32[]{:S(2)}, u32[]{:S(2)}) collective-permute-start(f32[128,512]{1,0:T(8,128)S(1)} %get-tuple-element.203), channel_id=1, source_target_pairs={{0,4},{4,0},{8,12},{12,8},{16,20},{20,16},{24,28},{28,24},{1,5},{5... | collective-permute-start | bytes 786440 | tf_op jit(solution)/shard_map/ppermute | solution.py:691
  94.0 9.6 %collective-permute-start.27 = (f32[136,512]{1,0:T(8,128)S(1)}, f32[136,512]{1,0:T(8,128)S(1)}, u32[]{:S(2)}, u32[]{:S(2)}) collective-permute-start(f32[136,512]{1,0:T(8,128)S(1)} %get-tuple-element.208), channel_id=1, source_target_pairs={{0,8},{4,12},{8,0},{12,4},{16,24},{20,28},{24,16},{28,20},{1,9},{5... | collective-permute-start | bytes 835592 | tf_op jit(solution)/shard_map/ppermute | solution.py:691
  97.8 9.0 %collective-permute-start.31 = (f32[128,512]{1,0:T(8,128)S(1)}, f32[128,512]{1,0:T(8,128)S(1)}, u32[]{:S(2)}, u32[]{:S(2)}) collective-permute-start(f32[128,512]{1,0:T(8,128)S(1)} %get-tuple-element.210.refs_0_), channel_id=1, source_target_pairs={{0,4},{4,0},{8,12},{12,8},{16,20},{20,16},{24,28},{28,24},{1,5},{5... | collective-permute-start | bytes 786440 | tf_op jit(solution)/shard_map/ppermute | solution.py:691
  99.4 12.7 %collective-permute-start.30 = (f32[128,512]{1,0:T(8,128)S(1)}, f32[128,512]{1,0:T(8,128)S(1)}, u32[]{:S(2)}, u32[]{:S(2)}) collective-permute-start(f32[128,512]{1,0:T(8,128)S(1)} %get-tuple-element.209.refs_3_.refs_0_), channel_id=1, source_target_pairs={{0,8},{4,12},{8,0},{12,4},{16,24},{20,28},{24,16},{28,20},{1,9},{5... | collective-permute-start | bytes 786440 | tf_op jit(solution)/shard_map/ppermute | solution.py:691
  103.7 15.6 %collective-permute-start.32 = (f32[136,512]{1,0:T(8,128)S(1)}, f32[136,512]{1,0:T(8,128)S(1)}, u32[]{:S(2)}, u32[]{:S(2)}) collective-permute-start(f32[136,512]{1,0:T(8,128)S(1)} %stack.3.refs_7_.refs_0_), channel_id=1, source_target_pairs={{0,16},{4,20},{8,24},{12,28},{16,0},{20,4},{24,8},{28,12},{1,17},{... | collective-permute-start | bytes 835592 | tf_op jit(solution)/shard_map/ppermute | solution.py:691
  106.8 26.2 %collective-permute-start.39 = (f32[256,512]{1,0:T(8,128)S(1)}, f32[256,512]{1,0:T(8,128)S(1)}, u32[]{:S(2)}, u32[]{:S(2)}) collective-permute-start(f32[256,512]{1,0:T(8,128)S(1)} %join.3.refs_2_.refs_0_), channel_id=1, source_target_pairs={{0,8},{4,12},{8,0},{12,4},{16,24},{20,28},{24,16},{28,20},{1,9},{5... | collective-permute-start | bytes 1572872 | tf_op jit(solution)/shard_map/ppermute | solution.py:691
  112.1 21.8 %collective-permute-start.38 = (f32[256,512]{1,0:T(8,128)S(1)}, f32[256,512]{1,0:T(8,128)S(1)}, u32[]{:S(2)}, u32[]{:S(2)}) collective-permute-start(f32[256,512]{1,0:T(8,128)S(1)} %join.4.refs_2_.refs_0_), channel_id=1, source_target_pairs={{0,4},{4,0},{8,12},{12,8},{16,20},{20,16},{24,28},{28,24},{1,5},{5... | collective-permute-start | bytes 1572872 | tf_op jit(solution)/shard_map/ppermute | solution.py:691
  119.3 9.5 %collective-permute-start.34 = (f32[64,512]{1,0:T(8,128)S(1)}, f32[64,512]{1,0:T(8,128)S(1)}, u32[]{:S(2)}, u32[]{:S(2)}) collective-permute-start(f32[64,512]{1,0:T(8,128)S(1)} %get-tuple-element.214.refs_0_), channel_id=1, source_target_pairs={{0,4},{4,0},{8,12},{12,8},{16,20},{20,16},{24,28},{28,24},{1,5},{5... | collective-permute-start | bytes 393224 | tf_op jit(solution)/shard_map/ppermute | solution.py:691
  (17 other events, 109.1 us)

commit v4 on v2

--- a/solution.py
+++ b/solution.py
@@ -444,7 +444,11 @@
     hidden = own_ref.shape[0]
     for place, outs in enumerate(((own_ref,), pair)):
         at = slice(place * hidden, (place + 1) * hidden)
-        put_rows(mm(h_0[:, at], g_0[...], 0, 0) + mm(h_1[:, at], g_1[...], 0, 0), outs)
+        value = mm(h_0[:, at], g_0[...], 0, 0) + mm(h_1[:, at], g_1[...], 0, 0)
+        for out_ref in outs:
+            out_ref[:hidden] = value
+            if out_ref.shape[0] > hidden:
+                out_ref[hidden:] = jnp.zeros((out_ref.shape[0] - hidden, value.shape[1]), F32)
     vec_ref[...] = column_sums(g_0[...]) + column_sums(g_1[...])
 
 
@@ -498,7 +502,7 @@
 
 def project_weights_kernel(
     normed, normed_edge, dq_0, dq_1, dkv_0, dkv_1, wo_own_0, wo_own_1, wo_pair_0, wo_pair_1, mid_0, mid_1, first, vec_outer, vec_inner,
-    own_0, own_1, rows_ref, pair_0, pair_1, message, sums, row,
+    own_0, own_1, rows_ref, pair_0, pair_1, sums, row,
 ):
     features = normed.shape[2]
     width = wo_own_0.shape[1]
@@ -517,21 +521,20 @@
     rows_ref[3:5] = first[...]
     rows_ref[5:6] = vec_outer[...] * 0.5
     rows_ref[6:] = jnp.zeros((2, features), F32)
-    half = own_0.shape[0]
-    pair_0[half : half + 6] = rows_ref[0:6]
-    pair_0[half + 6 :] = jnp.zeros((2, features), F32)
-    for place, (out_ref, at) in enumerate(((rows_ref, 6), (pair_0, half + 6))):
+    half = pair_0.shape[0]
+    pair_1[half : half + 6] = rows_ref[0:6]
+    pair_1[half + 6 :] = jnp.zeros((2, features), F32)
+    for place, (out_ref, at) in enumerate(((rows_ref, 6), (pair_1, half + 6))):
         for number in range(3):
             lanes = slice(number * width, (number + 1) * width)
             out_ref[at : at + 1, lanes] = row[:, lanes_of(place, width, 2 * number * width)]
         out_ref[at + 1 : at + 2, :hidden] = vec_inner[place : place + 1]
     for place, (outs, wo_0, wo_1) in enumerate((((own_0, own_1), wo_own_0, wo_own_1), ((pair_0, pair_1), wo_pair_0, wo_pair_1))):
-        for number in range(3):
-            lanes = slice(number * width, (number + 1) * width)
-            message[:, lanes] = sums[:, lanes_of(place, width, 2 * number * width)]
-        message[:, 3 * width :] = wo_0[...] + wo_1[...]
-        for number, out_ref in enumerate(outs):
-            out_ref[:half] = message[number * half : (number + 1) * half]
+        for out_ref, rows in zip(outs, (slice(half), slice(half, features)), strict=True):
+            for number in range(3):
+                lanes = slice(number * width, (number + 1) * width)
+                out_ref[:half, lanes] = sums[rows, lanes_of(place, width, 2 * number * width)]
+            out_ref[:half, 3 * width :] = wo_0[rows] + wo_1[rows]
 
 
 def frames_back_kernel(a_ref, b_ref, xhat, rate, dmid_0, dmid_1, params, out):
@@ -568,7 +571,7 @@
         take = min(piece.shape[0], count - at)
         if take:
             out[at : at + take] = a_ref[at : at + take] + piece[:take]
-        if take < piece.shape[0]:
+        if take < piece.shape[0] and new_rows is not None:
             new_rows[...] = rows_ref[...] + piece[take:]
         at += take
 
@@ -638,19 +641,16 @@
 
 
 def join_heads_kernel(bits, *refs):
-    *parts, wq, wk, wv, wo = refs
+    *parts, wq, wk, wv, wo, work = refs
     width = wq.shape[1]
-    at = 0
-    for number, bit in enumerate(bits):
-        mine, theirs = parts[2 * number : 2 * number + 2]
-        half = mine.shape[0]
-        place = place_of(bit)
-        for where, part in ((place, mine), (1 - place, theirs)):
-            rows = pl.ds(pl.multiple_of(at + where * half, half), half)
-            for heads, out in enumerate((wq, wk, wv)):
+    half = parts[0].shape[0]
+    place = place_of(bits[0])
+    for number in range(2):
+        for where, part in zip((place, 1 - place), parts[2 * number : 2 * number + 2], strict=True):
+            rows = pl.ds(pl.multiple_of(2 * number * half + where * half, half), half)
+            for heads, out in enumerate((wq, wk, wv, work)):
                 out[rows, :] = part[:, heads * width : (heads + 1) * width]
-            wo[:, rows] = part[:, 3 * width :].T
-        at += 2 * half
+    wo[...] = work[...].T
 
 
 def small_kernel(rows, far, outs):
@@ -689,12 +689,18 @@
 
 
 class SumsOverTm:
-    def __init__(self, run, a, b, rows=None):
+    def __init__(self, run, a, b, rows=None, joins=None):
         bits = [1 << i for i in range(lax.axis_size("tm").bit_length() - 1)]
         self.run, self.values, self.got, self.ones = run, list(a), [list(v) for v in b], []
         self.rows = [] if rows is None else [rows]
         self.apart = [(bits[1], bits[0]), (bits[0], bits[1])]
         self.together, self.last = bits[2:-1], bits[-1]
+        self.joins = joins
+        if len(a) == 1:
+            self.todo = [("split", (bit,)) for bit in bits[:-1]] + [("last",), ("add",)]
+            self.todo += [("join", (bit,)) for bit in (*reversed(self.together), joins[0])]
+            self.step()
+            return
         self.todo = [("split", pair) for pair in self.apart]
         self.todo.append(("stack",))
         self.todo += [("split", (bit,)) for bit in self.together] + [("last",)] * bool(self.together)
@@ -742,7 +748,7 @@
             self.got = [[swap(value, "tm", self.last)]]
             return
         if kind == "add":
-            parts = [self.count] if self.together else [self.count // 2] * 2
+            parts = [self.count] if self.together or self.joins else [self.count // 2] * 2
             out = run.call(
                 add_whole_kernel, "add", [shape(n) for n in parts] + [v.shape for v in self.rows], (*values, *got)
             )
@@ -754,7 +760,7 @@
             )
         elif kind == "part":
             self.values = [values[0][: count // 2], values[0][count // 2 :]]
-        following = self.todo[0] if self.todo else ("join", self.apart[0])
+        following = self.todo[0] if self.todo else ("join", self.joins[1:] if self.joins else self.apart[0])
         if following[0] == "part":
             return self.step()
         self.got = [[swap(v, "tm", bit)] for v, bit in zip(self.values, following[1], strict=True)]
@@ -786,11 +792,12 @@
 ORDER = (
     ("pack", 8), ("norm", 4.8), ("project", 2.2), ("attend_inner", 11), ("edges", 1), ("hand_on", 0.5),
     ("attend_outer0", 24), ("attend_outer1", 1), ("feed0", 18), ("feed1", 14), ("outer_weights", 6),
-    ("inner_weights", 11), ("feed_out", 0.6), ("grad_sum0", 18), ("ffn", 11), ("back0", 6), ("grad_sum1", 18),
+    ("inner_weights", 11), ("feed_out", 0.6), ("grad_sum0", 18), ("ffn", 11), ("back0", 6), ("grad_sum1", 2),
     ("back1", 0.5), ("ffn", 0.1), ("project_back", 1.8), ("project_weights", 2), ("ffn", 0.1), ("edge_add", 5),
-    ("out_half", 5), ("out_send", 6), ("heads", 20), ("place_out", 1.3), ("heads", 0.1), ("ffn", 0.1), ("heads", 3),
-    ("frames_back", 0.6), ("ffn_last0", 0.1), ("ffn_last1", 20), ("place_frames", 0.1), ("heads", 0.1),
-    ("heads", 0.1), ("join_outer", 0.1), ("join_inner", 0.1), ("finish", 1.3),
+    ("out_half", 5), ("heads0", 20), ("out_send", 20), ("heads1", 20), ("place_out", 1), ("heads0", 0.1),
+    ("heads1", 0.1), ("heads0", 0.1), ("ffn", 0.1), ("frames_back", 0.1), ("heads1", 3), ("ffn_last1", 4),
+    ("heads0", 16), ("heads1", 1), ("ffn_last0", 16), ("heads0", 16), ("place_frames", 0.1), ("heads1", 2),
+    ("join_inner", 0.1), ("join_outer", 3), ("finish", 0.1),
 )
 PIECES = 1
 
@@ -837,6 +844,7 @@
         self.mix_outer, self.far_outer, self.p_outer, self.fed, self.dn2 = (list(pairs) for _ in range(5))
         self.back_of = list(pairs)
         self.sums = {}
+        self.heads_names = ("heads0", "heads1")
 
     def pack(self):
         args = (*self.projections, self.weights[2], self.bq, self.bv, self.bi, self.frames)
@@ -925,7 +933,7 @@
         features, hidden = self.features, self.hidden
         self.outer_own, *pair, self.vec_outer = self.run.call(
             outer_weights_kernel, "outer_weights",
-            [(hidden, features)] + [(hidden // PIECES, features)] * PIECES + [(1, features)],
+            [(hidden, features), (hidden + 8, features), (1, features)],
             (self.fed[0][1], self.fed[1][1], *self.g),
         )
         self.outer_pair = swap_near(pair)
@@ -983,17 +991,18 @@
         features, width = self.features, self.width
         *self.heads_own, self.rows, a, b = self.run.call(
             project_weights_kernel, "project_weights",
-            [(features // 2, 4 * width)] * 2 + [(8, features), (features // 2 + 8, 4 * width), (features // 2, 4 * width)],
+            [(features // 2, 4 * width)] * 2 + [(8, features), (features // 2, 4 * width), (features // 2 + 8, 4 * width)],
             (self.normed, self.normed_edge, *self.pick(1), *self.pick(2), *self.pick(3), *self.pick(4), *self.pick(5),
              self.vec_first, self.vec_outer, self.vec_inner),
-            scratch=[(features, 4 * width), (features, 6 * width), (1, 6 * width)],
+            scratch=[(features, 6 * width), (1, 6 * width)],
         )
         self.heads_pair = swap_near((a, b))
 
     def begin(self, name):
-        if name == "heads":
-            a, b = self.heads_pair
-            return SumsOverTm(self.run, self.heads_own, ((a,), (b,)), self.rows)
+        if name in self.heads_names:
+            number = self.heads_names.index(name)
+            a, b = self.heads_own[number], self.heads_pair[number]
+            return SumsOverTm(self.run, (a,), ((b,),), self.rows if number else None, (2, 1))
         return SumsOverTm(self.run, (self.outer_own, self.inner_own), (self.outer_pair, self.inner_pair))
 
     def sum(self, name):
@@ -1005,14 +1014,11 @@
     def ffn(self):
         self.sum("ffn")
 
-    def heads(self):
-        self.sum("heads")
+    def heads(self, number):
+        self.sum(self.heads_names[number])
 
     def ffn_last(self, number):
         self.sums["ffn"].join_one(number)
-
-    def heads_last(self, number):
-        self.sums["heads"].join_one(number)
 
     def frames_back(self):
         (half,) = self.run.call(
@@ -1046,21 +1052,22 @@
                 self.sum(name)
 
     def join_outer(self):
-        self.settle("ffn", "heads")
+        self.settle("ffn", *self.heads_names)
         self.outer_grad = self.join("join_outer", 0, self.weights[1].shape)
 
     def join_inner(self):
+        self.settle("ffn", *self.heads_names)
         self.inner_grad = self.join("join_inner", 1, self.weights[0].shape)
 
     def finish(self):
         features, width, hidden = self.features, self.width, self.hidden
-        sums = self.sums["heads"]
-        rows = sums.rows[0]
-        bits, parts = zip(*(sums.halves(i) for i in range(2)), strict=True)
+        both = [self.sums[name] for name in self.heads_names]
+        rows = both[1].rows[0]
+        bits, parts = both[0].joins[::-1], [sums.halves(0)[1] for sums in both]
         out = self.run.call(
-            functools.partial(finish_kernel, list(bits)), "finish",
+            functools.partial(finish_kernel, bits), "finish",
             [(1, features)] * 6 + [(1, width)] * 2 + [(1, hidden)] + [(features, width)] * 3 + [(width, features)],
-            (rows, swap(rows, "head", 2), *parts[0], *parts[1]),
+            (rows, swap(rows, "head", 2), *parts[0], *parts[1]), scratch=[(features, width)],
         )
         bo, g2, s2, g1, s1, bu, bq, bv, bi = (v.reshape(v.shape[1]) for v in out[:9])
         wq, wk, wv, wo = out[9:]

time: 139 us -> 139 us (level)
  waiting for transfers between devices: 44.4 us -> 39.6 us
  starting transfers between devices: 43.8 us -> 48 us
    ppermute x39 -> x40, waiting for transfers between devices: 44.4 us -> 39.6 us  [swap(): return lax.ppermute(value, axis, [(i, i ^ bit) for i in range(size)])]
    ppermute x39 -> x40, starting transfers between devices: 38.7 us -> 42.9 us  [swap(): return lax.ppermute(value, axis, [(i, i ^ bit) for i in range(size)])]
    pallas_call x39 -> x44, Pallas kernels: 49.7 us -> 49.7 us  [call(): pl.pallas_call(body, name=name, grid=(1,), in_specs=[in_hbm if i in far e...]
  transfers between devices with their start and end apart: 41 -> 42, of which waited for: 14 -> 14; matrix products, arithmetic and copies ran while one was open for 0% -> 0% of each run, Pallas kernels for 34% -> 34%
where the time goes in v4:
time: 139 us; the launch traced here: 138 us
  Pallas kernels  49.7 us (36%)
  starting transfers between devices  48 us (35%)
  waiting for transfers between devices  39.6 us (28%)
    pallas_call x44, Pallas kernels, call(): pl.pallas_call(body, name=name, grid=(1,), in_specs=[in_hbm if i in far e...  49.7 us
    ppermute x40, starting transfers between devices, swap(): return lax.ppermute(value, axis, [(i, i ^ bit) for i in range(size)])  42.9 us
    ppermute x40, waiting for transfers between devices, swap(): return lax.ppermute(value, axis, [(i, i ^ bit) for i in range(size)])  39.6 us
    ppermute x2, starting transfers between devices, swap_edges(): return lax.ppermute(value, ('tm', 'head'), pairs)  5.1 us
  transfers between devices with their start and end apart: 42, of which 14 were waited for; matrix products, arithmetic and copies ran while one was open for 0% of the time, Pallas kernels for 34%

profile of v4, /device:TPU:0, one launch (start us, length us, event | category | flops | bytes accessed | tf_op | source)
XLA Modules:
  0.0 138.4 jit_solution(8253065686971880578)
XLA Ops:
  2.6 4.4 %collective-permute-start.1 = (f32[2,64,512]{2,1,0:T(8,128)S(1)}, f32[2,64,512]{2,1,0:T(8,128)S(1)}, u32[]{:S(2)}, u32[]{:S(2)}) collective-permute-start(f32[2,64,512]{2,1,0:T(8,128)S(1)} %get-tuple-element.127.refs_7_), channel_id=1, source_target_pairs={{0,4},{2,6},{4,8},{5,1},{6,10},{7,3},{8,12},{9,5},{10,14},{11,7},{... | collective-permute-start | bytes 786440 | tf_op jit(solution)/shard_map/ppermute | solution.py:688
  7.0 2.5 %norm.1 = (f32[2,256,512]{2,1,0:T(8,128)S(1)}, f32[2,256,512]{2,1,0:T(8,128)S(1)}, f32[2,256,128]{2,1,0:T(8,128)S(1)}, f32[2,256,512]{2,1,0:T(8,128)S(1)}, f32[5...) custom-call(f32[2,512,512]{2,1,0:T(8,128)} %refs_0_.6, ...), custom_call_target="tpu_custom_call" | custom-call | flops 2486400000 | tf_op jit(solution)/shard_map/norm/pallas_call | solution.py:118
  11.6 1.9 %project.1 = (f32[2,256,256]{2,1,0:T(8,128)S(1)}, f32[2,256,512]{2,1,0:T(8,128)S(1)}, f32[512,768]{1,0:T(8,128)S(1)}, f32[1,768]{1,0:T(1,128)S(1)}, f32[7,1,512]{2,1,0:T(1,128)S(1)}) custom-call(f32[2,256,512]{2,1,0:T(8,128)S(1)} %get-tuple-element.128.refs_0_, f32[520,512]{1,0:T(8,128)S(1)} %get-tuple-element.129.refs_1_.refs_0_, ...), custom_call_target="tpu_custom_call" | custom-call | flops 1139600000 | tf_op jit(solution)/shard_map/project/pallas_call | solution.py:118
  13.5 3.7 %attend_inner.1 = (f32[128,256]{1,0:T(8,128)S(1)}, f32[128,256]{1,0:T(8,128)S(1)}, f32[2,2,2,128,128]{4,3,2,1,0:T(8,128)S(1)}) custom-call(s32[2,4]{1,0:T(2,128)S(1)} %copy-done, f32[2,256,256]{2,1,0:T(8,128)S(1)} %get-tuple-element.131.refs_1_.refs_7_, f32[2,256,512]{2,1,0:T(8,128)S(1)} %get-tuple-element.132.refs_2_.refs_8_, ...), custom_call_target="tpu_custom_call" | custom-call | flops 5697999872 | tf_op jit(solution)/shard_map/attend_inner/pallas_call | solution.py:118
  19.0 2.1 %attend_outer.2 = (f32[128,256]{1,0:T(8,128)S(1)}, f32[2,2,128,128]{3,2,1,0:T(8,128)S(1)}) custom-call(s32[2,4]{1,0:T(2,128)S(1)} %copy-done, f32[2,256,256]{2,1,0:T(8,128)S(1)} %get-tuple-element.131.refs_1_.refs_7_, f32[2,256,512]{2,1,0:T(8,128)S(1)} %get-tuple-element.132.refs_2_.refs_8_, f32[2,72,512]{2,1,0:T(8,128)S(1)} %get-tuple-element.139.refs_3_.refs_9_, ...), custom_call_target="tpu_custom_call" | custom-call | flops 12432000000 | tf_op jit(solution)/shard_map/attend_outer/pallas_call | solution.py:118
  23.2 2.1 %attend_outer.3 = (f32[128,256]{1,0:T(8,128)S(1)}, f32[2,2,128,128]{3,2,1,0:T(8,128)S(1)}) custom-call(s32[2,4]{1,0:T(2,128)S(1)} %copy-done, f32[2,256,256]{2,1,0:T(8,128)S(1)} %get-tuple-element.131.refs_1_.refs_7_, f32[2,256,512]{2,1,0:T(8,128)S(1)} %get-tuple-element.132.refs_2_.refs_8_, f32[2,72,512]{2,1,0:T(8,128)S(1)} %get-tuple-element.139.refs_3_.refs_9_, ...), custom_call_target="tpu_custom_call" | custom-call | flops 518000000 | tf_op jit(solution)/shard_map/attend_outer/pallas_call | solution.py:118
  27.4 3.9 %feed.2 = (f32[256,512]{1,0:T(8,128)S(1)}, f32[256,1024]{1,0:T(8,128)S(1)}, f32[256,1024]{1,0:T(8,128)S(1)}, f32[256,512]{1,0:T(8,128)S(1)}, f32[256,512]{1,0:T(8,128)S(1)}) custom-call(f32[128,256]{1,0:T(8,128)S(1)} %get-tuple-element.134.refs_0_.refs_5_, f32[128,256]{1,0:T(8,128)S(1)} %get-tuple-element.142.refs_1_.refs_6_, ...), custom_call_target="tpu_custom_call" | custom-call | flops 9324000256 | tf_op jit(solution)/shard_map/feed/pallas_call | solution.py:118
  32.8 4.1 %feed.3 = (f32[256,512]{1,0:T(8,128)S(1)}, f32[256,1024]{1,0:T(8,128)S(1)}, f32[256,1024]{1,0:T(8,128)S(1)}, f32[256,512]{1,0:T(8,128)S(1)}, f32[256,512]{1,0:T(8,128)S(1)}) custom-call(f32[128,256]{1,0:T(8,128)S(1)} %get-tuple-element.151.refs_0_.refs_5_, f32[128,256]{1,0:T(8,128)S(1)} %get-tuple-element.152.refs_1_.refs_6_, ...), custom_call_target="tpu_custom_call" | custom-call | flops 7251999744 | tf_op jit(solution)/shard_map/feed/pallas_call | solution.py:118
  38.9 1.9 %inner_weights.1 = (f32[512,512]{1,0:T(8,128)S(1)}, f32[512,512]{1,0:T(8,128)S(1)}, f32[2,512]{1,0:T(2,128)S(1)}) custom-call(f32[256,512]{1,0:T(8,128)S(1)} %get-tuple-element.158.refs_0_, f32[256,512]{1,0:T(8,128)S(1)} %get-tuple-element.159.refs_1_, f32[256,1024]{1,0:T(8,128)S(1)} %get-tuple-element.160.refs_2_, ...), custom_call_target="tpu_custom_call" | custom-call | flops 5697999872 | tf_op jit(solution)/shard_map/inner_weights/pallas_call | solution.py:118
  42.6 2.1 %feed_out.1.refs_2_ = f32[512,512]{1,0:T(8,128)S(1)} custom-call(f32[256,1024]{1,0:T(8,128)S(1)} %get-tuple-element.156.refs_0_, f32[256,1024]{1,0:T(8,128)S(1)} %get-tuple-element.157.refs_1_, f32[512,512]{1,0:T(8,128)S(1)} %get-tuple-element.147.refs_13_.refs_2_, f32[512,512]{1,0:T(8,128)S(1)} %collective-permute-done.7.refs_14_.refs_3_, ...), custom_call_target="tpu_custom_call" | custom-call | flops 310800000 | tf_op jit(solution)/shard_map/feed_out/pallas_call | solution.py:118
  50.2 4.6 %back.2 = (f32[256,512]{1,0:T(8,128)S(1)}, f32[256,256]{1,0:T(8,128)S(1)}, f32[328,512]{1,0:T(8,128)S(1)}, f32[512,128]{1,0:T(8,128)S(1)}, f32[512,128]{1,0:T(8,128)S(1)}, /*index=5*/f32[3,512]{1,0:T(4,128)S(1)}) custom-call(f32[256,512]{1,0:T(8,128)S(1)} %grad_sum.2.refs_4_.refs_0_, f32[256,512]{1,0:T(8,128)S(1)} %get-tuple-element.150.refs_1_.refs_0_, ...), custom_call_target="tpu_custom_call" | custom-call | flops 3108000000 | tf_op jit(solution)/shard_map/back/pallas_call | solution.py:118
  56.2 4.3 %back.3 = (f32[256,512]{1,0:T(8,128)S(1)}, f32[256,256]{1,0:T(8,128)S(1)}, f32[328,512]{1,0:T(8,128)S(1)}, f32[512,128]{1,0:T(8,128)S(1)}, f32[512,128]{1,0:T(8,128)S(1)}, /*index=5*/f32[3,512]{1,0:T(4,128)S(1)}) custom-call(f32[256,512]{1,0:T(8,128)S(1)} %grad_sum.3.refs_0_.refs_12_, f32[256,512]{1,0:T(8,128)S(1)} %get-tuple-element.155.refs_1_, ...), custom_call_target="tpu_custom_call" | custom-call | flops 259000000 | tf_op jit(solution)/shard_map/back/pallas_call | solution.py:118
  66.5 2.6 %project_weights.1 = (f32[256,512]{1,0:T(8,128)S(1)}, f32[256,512]{1,0:T(8,128)S(1)}, f32[8,512]{1,0:T(8,128)S(1)}, f32[256,512]{1,0:T(8,128)S(1)}, f32[264,512]{1,0:T(8,128)S(1)}) custom-call(f32[2,256,512]{2,1,0:T(8,128)S(1)} %get-tuple-element.128.refs_0_, f32[2,72,512]{2,1,0:T(8,128)S(1)} %get-tuple-element.188.refs_1_, ...), custom_call_target="tpu_custom_call" | custom-call | flops 1036000000 | tf_op jit(solution)/shard_map/project_weights/pallas_call | solution.py:118
  71.1 2.7 %collective-permute-start.25 = (f32[256,512]{1,0:T(8,128)S(1)}, f32[256,512]{1,0:T(8,128)S(1)}, u32[]{:S(2)}, u32[]{:S(2)}) collective-permute-start(f32[256,512]{1,0:T(8,128)S(1)} %stack.3.refs_3_.refs_0_), channel_id=1, source_target_pairs={{0,16},{4,20},{8,24},{12,28},{16,0},{20,4},{24,8},{28,12},{1,17},{... | collective-permute-start | bytes 1572872 | tf_op jit(solution)/shard_map/ppermute | solution.py:673
  75.6 2.9 %collective-permute-done.10.refs_3_ = f32[512,512]{1,0:T(8,128)S(1)} collective-permute-done((f32[512,512]{1,0:T(8,128)S(1)}, f32[512,512]{1,0:T(8,128)S(1)}, u32[]{:S(2)}, u32[]{:S(2)}) %collective-permute-start.10) | collective-permute-done | bytes 1048608 | tf_op jit(solution)/shard_map/ppermute | solution.py:673
  81.3 2.0 %collective-permute-done.22.refs_1_ = f32[512,512]{1,0:T(8,128)S(1)} collective-permute-done((f32[512,512]{1,0:T(8,128)S(1)}, f32[512,512]{1,0:T(8,128)S(1)}, u32[]{:S(2)}, u32[]{:S(2)}) %collective-permute-start.22) | collective-permute-done | bytes 1048608 | tf_op jit(solution)/shard_map/ppermute | solution.py:673
  84.7 3.6 %collective-permute-done.26.refs_1_ = f32[128,512]{1,0:T(8,128)S(1)} collective-permute-done((f32[128,512]{1,0:T(8,128)S(1)}, f32[128,512]{1,0:T(8,128)S(1)}, u32[]{:S(2)}, u32[]{:S(2)}) %collective-permute-start.26) | collective-permute-done | bytes 262176 | tf_op jit(solution)/shard_map/ppermute | solution.py:673
  89.5 3.0 %collective-permute-done.28.refs_2_ = f32[136,512]{1,0:T(8,128)S(1)} collective-permute-done((f32[136,512]{1,0:T(8,128)S(1)}, f32[136,512]{1,0:T(8,128)S(1)}, u32[]{:S(2)}, u32[]{:S(2)}) %collective-permute-start.28) | collective-permute-done | bytes 278560 | tf_op jit(solution)/shard_map/ppermute | solution.py:673
  94.1 6.4 %collective-permute-done.27.refs_1_ = f32[64,512]{1,0:T(8,128)S(1)} collective-permute-done((f32[64,512]{1,0:T(8,128)S(1)}, f32[64,512]{1,0:T(8,128)S(1)}, u32[]{:S(2)}, u32[]{:S(2)}) %collective-permute-start.27) | collective-permute-done | bytes 131104 | tf_op jit(solution)/shard_map/ppermute | solution.py:673
  100.7 4.0 %collective-permute-start.30 = (f32[64,512]{1,0:T(8,128)S(1)}, f32[64,512]{1,0:T(8,128)S(1)}, u32[]{:S(2)}, u32[]{:S(2)}) collective-permute-start(f32[64,512]{1,0:T(8,128)S(1)} %stack.4.refs_2_.refs_0_), channel_id=1, source_target_pairs={{0,16},{4,20},{8,24},{12,28},{16,0},{20,4},{24,8},{28,12},{1,17},{... | collective-permute-start | bytes 393224 | tf_op jit(solution)/shard_map/ppermute | solution.py:673
  106.1 6.6 %collective-permute-done.31.refs_1_ = f32[128,512]{1,0:T(8,128)S(1)} collective-permute-done((f32[128,512]{1,0:T(8,128)S(1)}, f32[128,512]{1,0:T(8,128)S(1)}, u32[]{:S(2)}, u32[]{:S(2)}) %collective-permute-start.31) | collective-permute-done | bytes 262176 | tf_op jit(solution)/shard_map/ppermute | solution.py:673
  114.8 4.3 %collective-permute-done.35.refs_1_ = f32[72,512]{1,0:T(8,128)S(1)} collective-permute-done((f32[72,512]{1,0:T(8,128)S(1)}, f32[72,512]{1,0:T(8,128)S(1)}, u32[]{:S(2)}, u32[]{:S(2)}) %collective-permute-start.35) | collective-permute-done | bytes 147488 | tf_op jit(solution)/shard_map/ppermute | solution.py:673
  119.3 2.1 %collective-permute-start.40 = (f32[256,512]{1,0:T(8,128)S(1)}, f32[256,512]{1,0:T(8,128)S(1)}, u32[]{:S(2)}, u32[]{:S(2)}) collective-permute-start(f32[256,512]{1,0:T(8,128)S(1)} %join.5.refs_2_.refs_0_), channel_id=1, source_target_pairs={{0,8},{4,12},{8,0},{12,4},{16,24},{20,28},{24,16},{28,20},{1,9},{5... | collective-permute-start | bytes 1572872 | tf_op jit(solution)/shard_map/ppermute | solution.py:673
  129.4 6.2 %collective-permute-done.40.refs_1_ = f32[256,512]{1,0:T(8,128)S(1)} collective-permute-done((f32[256,512]{1,0:T(8,128)S(1)}, f32[256,512]{1,0:T(8,128)S(1)}, u32[]{:S(2)}, u32[]{:S(2)}) %collective-permute-start.40) | collective-permute-done | bytes 524320 | tf_op jit(solution)/shard_map/ppermute | solution.py:673
  (106 shorter events, 53.4 us)
Async XLA Ops:
  2.6 15.2 %collective-permute-start.1 = (f32[2,64,512]{2,1,0:T(8,128)S(1)}, f32[2,64,512]{2,1,0:T(8,128)S(1)}, u32[]{:S(2)}, u32[]{:S(2)}) collective-permute-start(f32[2,64,512]{2,1,0:T(8,128)S(1)} %get-tuple-element.127.refs_7_), channel_id=1, source_target_pairs={{0,4},{2,6},{4,8},{5,1},{6,10},{7,3},{8,12},{9,5},{10,14},{11,7},{... | collective-permute-start | bytes 786440 | tf_op jit(solution)/shard_map/ppermute | solution.py:688
  11.1 14.2 %collective-permute-start.7 = (f32[512,512]{1,0:T(8,128)S(1)}, f32[512,512]{1,0:T(8,128)S(1)}, u32[]{:S(2)}, u32[]{:S(2)}) collective-permute-start(f32[512,512]{1,0:T(8,128)S(1)} %get-tuple-element.147.refs_13_.refs_2_), channel_id=1, source_target_pairs={{0,1},{1,0},{2,3},{3,2},{4,5},{5,4},{6,7},{7,6},{8,9},{9,8},{10,11... | collective-permute-start | bytes 3145736 | tf_op jit(solution)/shard_map/ppermute | solution.py:673
  11.1 15.8 %collective-permute-start.6 = (f32[512,512]{1,0:T(8,128)S(1)}, f32[512,512]{1,0:T(8,128)S(1)}, u32[]{:S(2)}, u32[]{:S(2)}) collective-permute-start(f32[512,512]{1,0:T(8,128)S(1)} %get-tuple-element.146.refs_11_), channel_id=1, source_target_pairs={{0,1},{1,0},{2,3},{3,2},{4,5},{5,4},{6,7},{7,6},{8,9},{9,8},{10,11... | collective-permute-start | bytes 3145736 | tf_op jit(solution)/shard_map/ppermute | solution.py:673
  22.7 10.1 %collective-permute-start.8 = (f32[128,256]{1,0:T(8,128)S(1)}, f32[128,256]{1,0:T(8,128)S(1)}, u32[]{:S(2)}, u32[]{:S(2)}) collective-permute-start(f32[128,256]{1,0:T(8,128)S(1)} %get-tuple-element.151.refs_0_.refs_5_), channel_id=1, source_target_pairs={{0,2},{1,3},{2,0},{3,1},{4,6},{5,7},{6,4},{7,5},{8,10},{9,11},{10,... | collective-permute-start | bytes 393224 | tf_op jit(solution)/shard_map/ppermute | solution.py:673
  31.2 13.6 %collective-permute-start.11 = (f32[256,512]{1,0:T(8,128)S(1)}, f32[256,512]{1,0:T(8,128)S(1)}, u32[]{:S(2)}, u32[]{:S(2)}) collective-permute-start(f32[256,512]{1,0:T(8,128)S(1)} %get-tuple-element.154.refs_15_.refs_0_), channel_id=1, source_target_pairs={{0,2},{1,3},{2,0},{3,1},{4,6},{5,7},{6,4},{7,5},{8,10},{9,11},{10,... | collective-permute-start | bytes 1572872 | tf_op jit(solution)/shard_map/ppermute | solution.py:673
  41.3 14.8 %collective-permute-start.14 = (f32[256,512]{1,0:T(8,128)S(1)}, f32[256,512]{1,0:T(8,128)S(1)}, u32[]{:S(2)}, u32[]{:S(2)}) collective-permute-start(f32[256,512]{1,0:T(8,128)S(1)} %get-tuple-element.162.refs_4_.refs_0_), channel_id=1, source_target_pairs={{0,2},{1,3},{2,0},{3,1},{4,6},{5,7},{6,4},{7,5},{8,10},{9,11},{10,... | collective-permute-start | bytes 1572872 | tf_op jit(solution)/shard_map/ppermute | solution.py:673
  45.3 15.3 %collective-permute-start.15 = (f32[256,512]{1,0:T(8,128)S(1)}, f32[256,512]{1,0:T(8,128)S(1)}, u32[]{:S(2)}, u32[]{:S(2)}) collective-permute-start(f32[256,512]{1,0:T(8,128)S(1)} %get-tuple-element.179), channel_id=1, source_target_pairs={{0,8},{4,12},{8,0},{12,4},{16,24},{20,28},{24,16},{28,20},{1,9},{5... | collective-permute-start | bytes 1572872 | tf_op jit(solution)/shard_map/ppermute | solution.py:673
  46.9 13.7 %collective-permute-start.16 = (f32[256,512]{1,0:T(8,128)S(1)}, f32[256,512]{1,0:T(8,128)S(1)}, u32[]{:S(2)}, u32[]{:S(2)}) collective-permute-start(f32[256,512]{1,0:T(8,128)S(1)} %get-tuple-element.169.refs_12_), channel_id=1, source_target_pairs={{0,4},{4,0},{8,12},{12,8},{16,20},{20,16},{24,28},{28,24},{1,5},{5... | collective-permute-start | bytes 1572872 | tf_op jit(solution)/shard_map/ppermute | solution.py:673
  48.4 30.1 %collective-permute-start.10 = (f32[512,512]{1,0:T(8,128)S(1)}, f32[512,512]{1,0:T(8,128)S(1)}, u32[]{:S(2)}, u32[]{:S(2)}) collective-permute-start(f32[512,512]{1,0:T(8,128)S(1)} %feed_out.1.refs_2_), channel_id=1, source_target_pairs={{0,2},{1,3},{2,0},{3,1},{4,6},{5,7},{6,4},{7,5},{8,10},{9,11},{10,... | collective-permute-start | bytes 3145736 | tf_op jit(solution)/shard_map/ppermute | solution.py:673
  71.1 29.4 %collective-permute-start.25 = (f32[256,512]{1,0:T(8,128)S(1)}, f32[256,512]{1,0:T(8,128)S(1)}, u32[]{:S(2)}, u32[]{:S(2)}) collective-permute-start(f32[256,512]{1,0:T(8,128)S(1)} %stack.3.refs_3_.refs_0_), channel_id=1, source_target_pairs={{0,16},{4,20},{8,24},{12,28},{16,0},{20,4},{24,8},{28,12},{1,17},{... | collective-permute-start | bytes 1572872 | tf_op jit(solution)/shard_map/ppermute | solution.py:673
  73.9 31.4 %collective-permute-start.24 = (f32[512,512]{1,0:T(8,128)S(1)}, f32[512,512]{1,0:T(8,128)S(1)}, u32[]{:S(2)}, u32[]{:S(2)}) collective-permute-start(f32[512,512]{1,0:T(8,128)S(1)} %edge_add.1.refs_5_.refs_0_), channel_id=1, source_target_pairs={{0,2},{1,3},{2,0},{3,1},{4,6},{5,7},{6,4},{7,5},{8,10},{9,11},{10,... | collective-permute-start | bytes 3145736 | tf_op jit(solution)/shard_map/ppermute | solution.py:673
  80.8 11.6 %collective-permute-start.28 = (f32[136,512]{1,0:T(8,128)S(1)}, f32[136,512]{1,0:T(8,128)S(1)}, u32[]{:S(2)}, u32[]{:S(2)}) collective-permute-start(f32[136,512]{1,0:T(8,128)S(1)} %get-tuple-element.210), channel_id=1, source_target_pairs={{0,4},{4,0},{8,12},{12,8},{16,20},{20,16},{24,28},{28,24},{1,5},{5... | collective-permute-start | bytes 835592 | tf_op jit(solution)/shard_map/ppermute | solution.py:673
  88.3 12.2 %collective-permute-start.27 = (f32[64,512]{1,0:T(8,128)S(1)}, f32[64,512]{1,0:T(8,128)S(1)}, u32[]{:S(2)}, u32[]{:S(2)}) collective-permute-start(f32[64,512]{1,0:T(8,128)S(1)} %get-tuple-element.208.refs_3_), channel_id=1, source_target_pairs={{0,8},{4,12},{8,0},{12,4},{16,24},{20,28},{24,16},{28,20},{1,9},{5... | collective-permute-start | bytes 393224 | tf_op jit(solution)/shard_map/ppermute | solution.py:673
  92.5 13.5 %collective-permute-start.32 = (f32[72,512]{1,0:T(8,128)S(1)}, f32[72,512]{1,0:T(8,128)S(1)}, u32[]{:S(2)}, u32[]{:S(2)}) collective-permute-start(f32[72,512]{1,0:T(8,128)S(1)} %get-tuple-element.214), channel_id=1, source_target_pairs={{0,8},{4,12},{8,0},{12,4},{16,24},{20,28},{24,16},{28,20},{1,9},{5... | collective-permute-start | bytes 442376 | tf_op jit(solution)/shard_map/ppermute | solution.py:673
  100.6 12.1 %collective-permute-start.31 = (f32[128,512]{1,0:T(8,128)S(1)}, f32[128,512]{1,0:T(8,128)S(1)}, u32[]{:S(2)}, u32[]{:S(2)}) collective-permute-start(f32[128,512]{1,0:T(8,128)S(1)} %get-tuple-element.212.refs_7_.refs_0_), channel_id=1, source_target_pairs={{0,8},{4,12},{8,0},{12,4},{16,24},{20,28},{24,16},{28,20},{1,9},{5... | collective-permute-start | bytes 786440 | tf_op jit(solution)/shard_map/ppermute | solution.py:673
  100.7 13.3 %collective-permute-start.30 = (f32[64,512]{1,0:T(8,128)S(1)}, f32[64,512]{1,0:T(8,128)S(1)}, u32[]{:S(2)}, u32[]{:S(2)}) collective-permute-start(f32[64,512]{1,0:T(8,128)S(1)} %stack.4.refs_2_.refs_0_), channel_id=1, source_target_pairs={{0,16},{4,20},{8,24},{12,28},{16,0},{20,4},{24,8},{28,12},{1,17},{... | collective-permute-start | bytes 393224 | tf_op jit(solution)/shard_map/ppermute | solution.py:673
  104.7 14.5 %collective-permute-start.34 = (f32[128,512]{1,0:T(8,128)S(1)}, f32[128,512]{1,0:T(8,128)S(1)}, u32[]{:S(2)}, u32[]{:S(2)}) collective-permute-start(f32[128,512]{1,0:T(8,128)S(1)} %get-tuple-element.215.refs_0_), channel_id=1, source_target_pairs={{0,4},{4,0},{8,12},{12,8},{16,20},{20,16},{24,28},{28,24},{1,5},{5... | collective-permute-start | bytes 786440 | tf_op jit(solution)/shard_map/ppermute | solution.py:673
  105.9 16.7 %collective-permute-start.29 = (f32[512,512]{1,0:T(8,128)S(1)}, f32[512,512]{1,0:T(8,128)S(1)}, u32[]{:S(2)}, u32[]{:S(2)}) collective-permute-start(f32[512,512]{1,0:T(8,128)S(1)} %frames_back.1.refs_3_.refs_0_), channel_id=1, source_target_pairs={{0,1},{1,0},{2,3},{3,2},{4,5},{5,4},{6,7},{7,6},{8,9},{9,8},{10,11... | collective-permute-start | bytes 3145736 | tf_op jit(solution)/shard_map/ppermute | solution.py:673
  106.0 13.2 %collective-permute-start.35 = (f32[72,512]{1,0:T(8,128)S(1)}, f32[72,512]{1,0:T(8,128)S(1)}, u32[]{:S(2)}, u32[]{:S(2)}) collective-permute-start(f32[72,512]{1,0:T(8,128)S(1)} %stack.5.refs_2_.refs_0_), channel_id=1, source_target_pairs={{0,16},{4,20},{8,24},{12,28},{16,0},{20,4},{24,8},{28,12},{1,17},{... | collective-permute-start | bytes 442376 | tf_op jit(solution)/shard_map/ppermute | solution.py:673
  112.8 15.7 %collective-permute-start.41 = (f32[256,512]{1,0:T(8,128)S(1)}, f32[256,512]{1,0:T(8,128)S(1)}, u32[]{:S(2)}, u32[]{:S(2)}) collective-permute-start(f32[256,512]{1,0:T(8,128)S(1)} %join.4.refs_2_.refs_0_), channel_id=1, source_target_pairs={{0,4},{4,0},{8,12},{12,8},{16,20},{20,16},{24,28},{28,24},{1,5},{5... | collective-permute-start | bytes 1572872 | tf_op jit(solution)/shard_map/ppermute | solution.py:673
  119.3 16.4 %collective-permute-start.40 = (f32[256,512]{1,0:T(8,128)S(1)}, f32[256,512]{1,0:T(8,128)S(1)}, u32[]{:S(2)}, u32[]{:S(2)}) collective-permute-start(f32[256,512]{1,0:T(8,128)S(1)} %join.5.refs_2_.refs_0_), channel_id=1, source_target_pairs={{0,8},{4,12},{8,0},{12,4},{16,24},{20,28},{24,16},{28,20},{1,9},{5... | collective-permute-start | bytes 1572872 | tf_op jit(solution)/shard_map/ppermute | solution.py:673
  121.4 15.2 %collective-permute-start.37 = (f32[128,512]{1,0:T(8,128)S(1)}, f32[128,512]{1,0:T(8,128)S(1)}, u32[]{:S(2)}, u32[]{:S(2)}) collective-permute-start(f32[128,512]{1,0:T(8,128)S(1)} %join.6.refs_2_), channel_id=1, source_target_pairs={{0,4},{4,0},{8,12},{12,8},{16,20},{20,16},{24,28},{28,24},{1,5},{5... | collective-permute-start | bytes 786440 | tf_op jit(solution)/shard_map/ppermute | solution.py:673
  125.7 11.6 %collective-permute-start.39 = (f32[128,512]{1,0:T(8,128)S(1)}, f32[128,512]{1,0:T(8,128)S(1)}, u32[]{:S(2)}, u32[]{:S(2)}) collective-permute-start(f32[128,512]{1,0:T(8,128)S(1)} %join.7.refs_2_.refs_4_), channel_id=1, source_target_pairs={{0,4},{4,0},{8,12},{12,8},{16,20},{20,16},{24,28},{28,24},{1,5},{5... | collective-permute-start | bytes 786440 | tf_op jit(solution)/shard_map/ppermute | solution.py:673
  126.8 9.9 %collective-permute-start.36 = (f32[8,512]{1,0:T(8,128)S(1)}, f32[8,512]{1,0:T(8,128)S(1)}, u32[]{:S(2)}, u32[]{:S(2)}) collective-permute-start(f32[8,512]{1,0:T(8,128)S(1)} %get-tuple-element.216.refs_2_.refs_0_), channel_id=1, source_target_pairs={{0,2},{1,3},{2,0},{3,1},{4,6},{5,7},{6,4},{7,5},{8,10},{9,11},{10,... | collective-permute-start | bytes 49160 | tf_op jit(solution)/shard_map/ppermute | solution.py:673
  (19 other events, 134.4 us)

commit v5 on v4

--- a/solution.py
+++ b/solution.py
@@ -794,10 +794,10 @@
     ("attend_outer0", 24), ("attend_outer1", 1), ("feed0", 18), ("feed1", 14), ("outer_weights", 6),
     ("inner_weights", 11), ("feed_out", 0.6), ("grad_sum0", 18), ("ffn", 11), ("back0", 6), ("grad_sum1", 2),
     ("back1", 0.5), ("ffn", 0.1), ("project_back", 1.8), ("project_weights", 2), ("ffn", 0.1), ("edge_add", 5),
-    ("out_half", 5), ("heads0", 20), ("out_send", 20), ("heads1", 20), ("place_out", 1), ("heads0", 0.1),
-    ("heads1", 0.1), ("heads0", 0.1), ("ffn", 0.1), ("frames_back", 0.1), ("heads1", 3), ("ffn_last1", 4),
-    ("heads0", 16), ("heads1", 1), ("ffn_last0", 16), ("heads0", 16), ("place_frames", 0.1), ("heads1", 2),
-    ("join_inner", 0.1), ("join_outer", 3), ("finish", 0.1),
+    ("out_half", 5), ("heads0", 20), ("out_send", 20), ("heads1", 20), ("place_out", 1), ("heads0", 1),
+    ("heads1", 0.1), ("ffn", 0.1), ("heads0", 0.1), ("heads1", 3), ("frames_back", 0.6), ("ffn_last1", 20),
+    ("heads0", 3), ("heads1", 0.1), ("ffn_last0", 12), ("place_frames", 0.1), ("heads0", 9), ("heads1", 2),
+    ("join_inner", 0.1), ("join_outer", 0.1), ("finish", 1.3),
 )
 PIECES = 1
 

time: 139 us -> 139 us (level)
  waiting for transfers between devices: 39.6 us -> 41.9 us
  starting transfers between devices: 48 us -> 46.1 us
    ppermute x40, waiting for transfers between devices: 39.6 us -> 41.9 us  [swap(): return lax.ppermute(value, axis, [(i, i ^ bit) for i in range(size)])]
    ppermute x40, starting transfers between devices: 42.9 us -> 41 us  [swap(): return lax.ppermute(value, axis, [(i, i ^ bit) for i in range(size)])]
  transfers between devices with their start and end apart: 42 -> 42, of which waited for: 14 -> 17; matrix products, arithmetic and copies ran while one was open for 0% -> 0% of each run, Pallas kernels for 34% -> 34%
where the time goes in v5:
time: 139 us
  Pallas kernels  49.7 us (36%)
  starting transfers between devices  46.1 us (33%)
  waiting for transfers between devices  41.9 us (30%)
    pallas_call x44, Pallas kernels, call(): pl.pallas_call(body, name=name, grid=(1,), in_specs=[in_hbm if i in far e...  49.7 us
    ppermute x40, waiting for transfers between devices, swap(): return lax.ppermute(value, axis, [(i, i ^ bit) for i in range(size)])  41.9 us
    ppermute x40, starting transfers between devices, swap(): return lax.ppermute(value, axis, [(i, i ^ bit) for i in range(size)])  41 us
    ppermute x2, starting transfers between devices, swap_edges(): return lax.ppermute(value, ('tm', 'head'), pairs)  5.1 us
  transfers between devices with their start and end apart: 42, of which 17 were waited for; matrix products, arithmetic and copies ran while one was open for 0% of the time, Pallas kernels for 34%

profile of v5, /device:TPU:0, one launch (start us, length us, event | category | flops | bytes accessed | tf_op | source)
XLA Modules:
  0.0 138.8 jit_solution(171989839176266125)
XLA Ops:
  2.6 4.4 %collective-permute-start.1 = (f32[2,64,512]{2,1,0:T(8,128)S(1)}, f32[2,64,512]{2,1,0:T(8,128)S(1)}, u32[]{:S(2)}, u32[]{:S(2)}) collective-permute-start(f32[2,64,512]{2,1,0:T(8,128)S(1)} %get-tuple-element.127.refs_7_), channel_id=1, source_target_pairs={{0,4},{2,6},{4,8},{5,1},{6,10},{7,3},{8,12},{9,5},{10,14},{11,7},{... | collective-permute-start | bytes 786440 | tf_op jit(solution)/shard_map/ppermute | solution.py:688
  7.0 2.5 %norm.1 = (f32[2,256,512]{2,1,0:T(8,128)S(1)}, f32[2,256,512]{2,1,0:T(8,128)S(1)}, f32[2,256,128]{2,1,0:T(8,128)S(1)}, f32[2,256,512]{2,1,0:T(8,128)S(1)}, f32[5...) custom-call(f32[2,512,512]{2,1,0:T(8,128)} %refs_0_.6, ...), custom_call_target="tpu_custom_call" | custom-call | flops 2486400000 | tf_op jit(solution)/shard_map/norm/pallas_call | solution.py:118
  13.5 3.7 %attend_inner.1 = (f32[128,256]{1,0:T(8,128)S(1)}, f32[128,256]{1,0:T(8,128)S(1)}, f32[2,2,2,128,128]{4,3,2,1,0:T(8,128)S(1)}) custom-call(s32[2,4]{1,0:T(2,128)S(1)} %copy-done, f32[2,256,256]{2,1,0:T(8,128)S(1)} %get-tuple-element.131.refs_1_.refs_7_, f32[2,256,512]{2,1,0:T(8,128)S(1)} %get-tuple-element.132.refs_2_.refs_8_, ...), custom_call_target="tpu_custom_call" | custom-call | flops 5697999872 | tf_op jit(solution)/shard_map/attend_inner/pallas_call | solution.py:118
  19.0 2.1 %attend_outer.2 = (f32[128,256]{1,0:T(8,128)S(1)}, f32[2,2,128,128]{3,2,1,0:T(8,128)S(1)}) custom-call(s32[2,4]{1,0:T(2,128)S(1)} %copy-done, f32[2,256,256]{2,1,0:T(8,128)S(1)} %get-tuple-element.131.refs_1_.refs_7_, f32[2,256,512]{2,1,0:T(8,128)S(1)} %get-tuple-element.132.refs_2_.refs_8_, f32[2,72,512]{2,1,0:T(8,128)S(1)} %get-tuple-element.139.refs_3_.refs_9_, ...), custom_call_target="tpu_custom_call" | custom-call | flops 12432000000 | tf_op jit(solution)/shard_map/attend_outer/pallas_call | solution.py:118
  23.2 2.1 %attend_outer.3 = (f32[128,256]{1,0:T(8,128)S(1)}, f32[2,2,128,128]{3,2,1,0:T(8,128)S(1)}) custom-call(s32[2,4]{1,0:T(2,128)S(1)} %copy-done, f32[2,256,256]{2,1,0:T(8,128)S(1)} %get-tuple-element.131.refs_1_.refs_7_, f32[2,256,512]{2,1,0:T(8,128)S(1)} %get-tuple-element.132.refs_2_.refs_8_, f32[2,72,512]{2,1,0:T(8,128)S(1)} %get-tuple-element.139.refs_3_.refs_9_, ...), custom_call_target="tpu_custom_call" | custom-call | flops 518000000 | tf_op jit(solution)/shard_map/attend_outer/pallas_call | solution.py:118
  27.4 3.9 %feed.2 = (f32[256,512]{1,0:T(8,128)S(1)}, f32[256,1024]{1,0:T(8,128)S(1)}, f32[256,1024]{1,0:T(8,128)S(1)}, f32[256,512]{1,0:T(8,128)S(1)}, f32[256,512]{1,0:T(8,128)S(1)}) custom-call(f32[128,256]{1,0:T(8,128)S(1)} %get-tuple-element.134.refs_0_.refs_5_, f32[128,256]{1,0:T(8,128)S(1)} %get-tuple-element.142.refs_1_.refs_6_, ...), custom_call_target="tpu_custom_call" | custom-call | flops 9324000256 | tf_op jit(solution)/shard_map/feed/pallas_call | solution.py:118
  32.8 4.1 %feed.3 = (f32[256,512]{1,0:T(8,128)S(1)}, f32[256,1024]{1,0:T(8,128)S(1)}, f32[256,1024]{1,0:T(8,128)S(1)}, f32[256,512]{1,0:T(8,128)S(1)}, f32[256,512]{1,0:T(8,128)S(1)}) custom-call(f32[128,256]{1,0:T(8,128)S(1)} %get-tuple-element.151.refs_0_.refs_5_, f32[128,256]{1,0:T(8,128)S(1)} %get-tuple-element.152.refs_1_.refs_6_, ...), custom_call_target="tpu_custom_call" | custom-call | flops 7251999744 | tf_op jit(solution)/shard_map/feed/pallas_call | solution.py:118
  42.6 2.1 %feed_out.1.refs_2_ = f32[512,512]{1,0:T(8,128)S(1)} custom-call(f32[256,1024]{1,0:T(8,128)S(1)} %get-tuple-element.156.refs_0_, f32[256,1024]{1,0:T(8,128)S(1)} %get-tuple-element.157.refs_1_, f32[512,512]{1,0:T(8,128)S(1)} %get-tuple-element.147.refs_13_.refs_2_, f32[512,512]{1,0:T(8,128)S(1)} %collective-permute-done.7.refs_14_.refs_3_, ...), custom_call_target="tpu_custom_call" | custom-call | flops 310800000 | tf_op jit(solution)/shard_map/feed_out/pallas_call | solution.py:118
  50.2 4.6 %back.2 = (f32[256,512]{1,0:T(8,128)S(1)}, f32[256,256]{1,0:T(8,128)S(1)}, f32[328,512]{1,0:T(8,128)S(1)}, f32[512,128]{1,0:T(8,128)S(1)}, f32[512,128]{1,0:T(8,128)S(1)}, /*index=5*/f32[3,512]{1,0:T(4,128)S(1)}) custom-call(f32[256,512]{1,0:T(8,128)S(1)} %grad_sum.2.refs_4_.refs_0_, f32[256,512]{1,0:T(8,128)S(1)} %get-tuple-element.150.refs_1_.refs_0_, ...), custom_call_target="tpu_custom_call" | custom-call | flops 3108000000 | tf_op jit(solution)/shard_map/back/pallas_call | solution.py:118
  56.2 4.3 %back.3 = (f32[256,512]{1,0:T(8,128)S(1)}, f32[256,256]{1,0:T(8,128)S(1)}, f32[328,512]{1,0:T(8,128)S(1)}, f32[512,128]{1,0:T(8,128)S(1)}, f32[512,128]{1,0:T(8,128)S(1)}, /*index=5*/f32[3,512]{1,0:T(4,128)S(1)}) custom-call(f32[256,512]{1,0:T(8,128)S(1)} %grad_sum.3.refs_0_.refs_12_, f32[256,512]{1,0:T(8,128)S(1)} %get-tuple-element.155.refs_1_, ...), custom_call_target="tpu_custom_call" | custom-call | flops 259000000 | tf_op jit(solution)/shard_map/back/pallas_call | solution.py:118
  66.5 2.6 %project_weights.1 = (f32[256,512]{1,0:T(8,128)S(1)}, f32[256,512]{1,0:T(8,128)S(1)}, f32[8,512]{1,0:T(8,128)S(1)}, f32[256,512]{1,0:T(8,128)S(1)}, f32[264,512]{1,0:T(8,128)S(1)}) custom-call(f32[2,256,512]{2,1,0:T(8,128)S(1)} %get-tuple-element.128.refs_0_, f32[2,72,512]{2,1,0:T(8,128)S(1)} %get-tuple-element.188.refs_1_, ...), custom_call_target="tpu_custom_call" | custom-call | flops 1036000000 | tf_op jit(solution)/shard_map/project_weights/pallas_call | solution.py:118
  71.1 2.7 %collective-permute-start.29 = (f32[256,512]{1,0:T(8,128)S(1)}, f32[256,512]{1,0:T(8,128)S(1)}, u32[]{:S(2)}, u32[]{:S(2)}) collective-permute-start(f32[256,512]{1,0:T(8,128)S(1)} %stack.3.refs_3_.refs_0_), channel_id=1, source_target_pairs={{0,16},{4,20},{8,24},{12,28},{16,0},{20,4},{24,8},{28,12},{1,17},{... | collective-permute-start | bytes 1572872 | tf_op jit(solution)/shard_map/ppermute | solution.py:673
  75.6 2.9 %collective-permute-done.10.refs_3_ = f32[512,512]{1,0:T(8,128)S(1)} collective-permute-done((f32[512,512]{1,0:T(8,128)S(1)}, f32[512,512]{1,0:T(8,128)S(1)}, u32[]{:S(2)}, u32[]{:S(2)}) %collective-permute-start.10) | collective-permute-done | bytes 1048608 | tf_op jit(solution)/shard_map/ppermute | solution.py:673
  81.3 2.0 %collective-permute-done.22.refs_1_ = f32[512,512]{1,0:T(8,128)S(1)} collective-permute-done((f32[512,512]{1,0:T(8,128)S(1)}, f32[512,512]{1,0:T(8,128)S(1)}, u32[]{:S(2)}, u32[]{:S(2)}) %collective-permute-start.22) | collective-permute-done | bytes 1048608 | tf_op jit(solution)/shard_map/ppermute | solution.py:673
  84.7 3.6 %collective-permute-done.26.refs_1_ = f32[128,512]{1,0:T(8,128)S(1)} collective-permute-done((f32[128,512]{1,0:T(8,128)S(1)}, f32[128,512]{1,0:T(8,128)S(1)}, u32[]{:S(2)}, u32[]{:S(2)}) %collective-permute-start.26) | collective-permute-done | bytes 262176 | tf_op jit(solution)/shard_map/ppermute | solution.py:673
  88.3 4.1 %collective-permute-done.25.refs_2_ = f32[136,512]{1,0:T(8,128)S(1)} collective-permute-done((f32[136,512]{1,0:T(8,128)S(1)}, f32[136,512]{1,0:T(8,128)S(1)}, u32[]{:S(2)}, u32[]{:S(2)}) %collective-permute-start.25) | collective-permute-done | bytes 278560 | tf_op jit(solution)/shard_map/ppermute | solution.py:673
  94.6 3.1 %collective-permute-done.29.refs_1_ = f32[256,512]{1,0:T(8,128)S(1)} collective-permute-done((f32[256,512]{1,0:T(8,128)S(1)}, f32[256,512]{1,0:T(8,128)S(1)}, u32[]{:S(2)}, u32[]{:S(2)}) %collective-permute-start.29) | collective-permute-done | bytes 524320 | tf_op jit(solution)/shard_map/ppermute | solution.py:673
  99.5 4.1 %collective-permute-done.28.refs_1_ = f32[64,512]{1,0:T(8,128)S(1)} collective-permute-done((f32[64,512]{1,0:T(8,128)S(1)}, f32[64,512]{1,0:T(8,128)S(1)}, u32[]{:S(2)}, u32[]{:S(2)}) %collective-permute-start.28) | collective-permute-done | bytes 131104 | tf_op jit(solution)/shard_map/ppermute | solution.py:673
  107.4 2.7 %collective-permute-done.34.refs_1_ = f32[128,512]{1,0:T(8,128)S(1)} collective-permute-done((f32[128,512]{1,0:T(8,128)S(1)}, f32[128,512]{1,0:T(8,128)S(1)}, u32[]{:S(2)}, u32[]{:S(2)}) %collective-permute-start.34) | collective-permute-done | bytes 262176 | tf_op jit(solution)/shard_map/ppermute | solution.py:673
  111.0 5.9 %collective-permute-done.33.refs_1_ = f32[64,512]{1,0:T(8,128)S(1)} collective-permute-done((f32[64,512]{1,0:T(8,128)S(1)}, f32[64,512]{1,0:T(8,128)S(1)}, u32[]{:S(2)}, u32[]{:S(2)}) %collective-permute-start.33) | collective-permute-done | bytes 131104 | tf_op jit(solution)/shard_map/ppermute | solution.py:673
  117.0 2.2 %collective-permute-done.32.refs_1_ = f32[72,512]{1,0:T(8,128)S(1)} collective-permute-done((f32[72,512]{1,0:T(8,128)S(1)}, f32[72,512]{1,0:T(8,128)S(1)}, u32[]{:S(2)}, u32[]{:S(2)}) %collective-permute-start.32) | collective-permute-done | bytes 147488 | tf_op jit(solution)/shard_map/ppermute | solution.py:673
  119.4 2.1 %collective-permute-start.40 = (f32[256,512]{1,0:T(8,128)S(1)}, f32[256,512]{1,0:T(8,128)S(1)}, u32[]{:S(2)}, u32[]{:S(2)}) collective-permute-start(f32[256,512]{1,0:T(8,128)S(1)} %join.5.refs_2_.refs_0_), channel_id=1, source_target_pairs={{0,8},{4,12},{8,0},{12,4},{16,24},{20,28},{24,16},{28,20},{1,9},{5... | collective-permute-start | bytes 1572872 | tf_op jit(solution)/shard_map/ppermute | solution.py:673
  123.1 2.8 %collective-permute-done.38.refs_1_ = f32[64,512]{1,0:T(8,128)S(1)} collective-permute-done((f32[64,512]{1,0:T(8,128)S(1)}, f32[64,512]{1,0:T(8,128)S(1)}, u32[]{:S(2)}, u32[]{:S(2)}) %collective-permute-start.38) | collective-permute-done | bytes 131104 | tf_op jit(solution)/shard_map/ppermute | solution.py:673
  130.7 5.3 %collective-permute-done.40.refs_1_ = f32[256,512]{1,0:T(8,128)S(1)} collective-permute-done((f32[256,512]{1,0:T(8,128)S(1)}, f32[256,512]{1,0:T(8,128)S(1)}, u32[]{:S(2)}, u32[]{:S(2)}) %collective-permute-start.40) | collective-permute-done | bytes 524320 | tf_op jit(solution)/shard_map/ppermute | solution.py:673
  (106 shorter events, 58.0 us)
Async XLA Ops:
  2.6 15.2 %collective-permute-start.1 = (f32[2,64,512]{2,1,0:T(8,128)S(1)}, f32[2,64,512]{2,1,0:T(8,128)S(1)}, u32[]{:S(2)}, u32[]{:S(2)}) collective-permute-start(f32[2,64,512]{2,1,0:T(8,128)S(1)} %get-tuple-element.127.refs_7_), channel_id=1, source_target_pairs={{0,4},{2,6},{4,8},{5,1},{6,10},{7,3},{8,12},{9,5},{10,14},{11,7},{... | collective-permute-start | bytes 786440 | tf_op jit(solution)/shard_map/ppermute | solution.py:688
  11.1 14.2 %collective-permute-start.7 = (f32[512,512]{1,0:T(8,128)S(1)}, f32[512,512]{1,0:T(8,128)S(1)}, u32[]{:S(2)}, u32[]{:S(2)}) collective-permute-start(f32[512,512]{1,0:T(8,128)S(1)} %get-tuple-element.147.refs_13_.refs_2_), channel_id=1, source_target_pairs={{0,1},{1,0},{2,3},{3,2},{4,5},{5,4},{6,7},{7,6},{8,9},{9,8},{10,11... | collective-permute-start | bytes 3145736 | tf_op jit(solution)/shard_map/ppermute | solution.py:673
  11.1 15.8 %collective-permute-start.6 = (f32[512,512]{1,0:T(8,128)S(1)}, f32[512,512]{1,0:T(8,128)S(1)}, u32[]{:S(2)}, u32[]{:S(2)}) collective-permute-start(f32[512,512]{1,0:T(8,128)S(1)} %get-tuple-element.146.refs_11_), channel_id=1, source_target_pairs={{0,1},{1,0},{2,3},{3,2},{4,5},{5,4},{6,7},{7,6},{8,9},{9,8},{10,11... | collective-permute-start | bytes 3145736 | tf_op jit(solution)/shard_map/ppermute | solution.py:673
  22.7 10.1 %collective-permute-start.8 = (f32[128,256]{1,0:T(8,128)S(1)}, f32[128,256]{1,0:T(8,128)S(1)}, u32[]{:S(2)}, u32[]{:S(2)}) collective-permute-start(f32[128,256]{1,0:T(8,128)S(1)} %get-tuple-element.151.refs_0_.refs_5_), channel_id=1, source_target_pairs={{0,2},{1,3},{2,0},{3,1},{4,6},{5,7},{6,4},{7,5},{8,10},{9,11},{10,... | collective-permute-start | bytes 393224 | tf_op jit(solution)/shard_map/ppermute | solution.py:673
  31.2 13.6 %collective-permute-start.11 = (f32[256,512]{1,0:T(8,128)S(1)}, f32[256,512]{1,0:T(8,128)S(1)}, u32[]{:S(2)}, u32[]{:S(2)}) collective-permute-start(f32[256,512]{1,0:T(8,128)S(1)} %get-tuple-element.154.refs_15_.refs_0_), channel_id=1, source_target_pairs={{0,2},{1,3},{2,0},{3,1},{4,6},{5,7},{6,4},{7,5},{8,10},{9,11},{10,... | collective-permute-start | bytes 1572872 | tf_op jit(solution)/shard_map/ppermute | solution.py:673
  41.3 14.8 %collective-permute-start.14 = (f32[256,512]{1,0:T(8,128)S(1)}, f32[256,512]{1,0:T(8,128)S(1)}, u32[]{:S(2)}, u32[]{:S(2)}) collective-permute-start(f32[256,512]{1,0:T(8,128)S(1)} %get-tuple-element.162.refs_4_.refs_0_), channel_id=1, source_target_pairs={{0,2},{1,3},{2,0},{3,1},{4,6},{5,7},{6,4},{7,5},{8,10},{9,11},{10,... | collective-permute-start | bytes 1572872 | tf_op jit(solution)/shard_map/ppermute | solution.py:673
  45.3 15.3 %collective-permute-start.15 = (f32[256,512]{1,0:T(8,128)S(1)}, f32[256,512]{1,0:T(8,128)S(1)}, u32[]{:S(2)}, u32[]{:S(2)}) collective-permute-start(f32[256,512]{1,0:T(8,128)S(1)} %get-tuple-element.179), channel_id=1, source_target_pairs={{0,8},{4,12},{8,0},{12,4},{16,24},{20,28},{24,16},{28,20},{1,9},{5... | collective-permute-start | bytes 1572872 | tf_op jit(solution)/shard_map/ppermute | solution.py:673
  46.9 13.7 %collective-permute-start.16 = (f32[256,512]{1,0:T(8,128)S(1)}, f32[256,512]{1,0:T(8,128)S(1)}, u32[]{:S(2)}, u32[]{:S(2)}) collective-permute-start(f32[256,512]{1,0:T(8,128)S(1)} %get-tuple-element.169.refs_12_), channel_id=1, source_target_pairs={{0,4},{4,0},{8,12},{12,8},{16,20},{20,16},{24,28},{28,24},{1,5},{5... | collective-permute-start | bytes 1572872 | tf_op jit(solution)/shard_map/ppermute | solution.py:673
  48.4 30.1 %collective-permute-start.10 = (f32[512,512]{1,0:T(8,128)S(1)}, f32[512,512]{1,0:T(8,128)S(1)}, u32[]{:S(2)}, u32[]{:S(2)}) collective-permute-start(f32[512,512]{1,0:T(8,128)S(1)} %feed_out.1.refs_2_), channel_id=1, source_target_pairs={{0,2},{1,3},{2,0},{3,1},{4,6},{5,7},{6,4},{7,5},{8,10},{9,11},{10,... | collective-permute-start | bytes 3145736 | tf_op jit(solution)/shard_map/ppermute | solution.py:673
  69.1 9.7 %collective-permute-start.21 = (f32[256,512]{1,0:T(8,128)S(1)}, f32[256,512]{1,0:T(8,128)S(1)}, u32[]{:S(2)}, u32[]{:S(2)}) collective-permute-start(f32[256,512]{1,0:T(8,128)S(1)} %get-tuple-element.196), channel_id=1, source_target_pairs={{0,1},{1,0},{2,3},{3,2},{4,5},{5,4},{6,7},{7,6},{8,9},{9,8},{10,11... | collective-permute-start | bytes 1572872 | tf_op jit(solution)/shard_map/ppermute | solution.py:673
  71.0 9.7 %collective-permute-start.23 = (f32[264,512]{1,0:T(8,128)S(1)}, f32[264,512]{1,0:T(8,128)S(1)}, u32[]{:S(2)}, u32[]{:S(2)}) collective-permute-start(f32[264,512]{1,0:T(8,128)S(1)} %get-tuple-element.194.refs_4_), channel_id=1, source_target_pairs={{0,1},{1,0},{2,3},{3,2},{4,5},{5,4},{6,7},{7,6},{8,9},{9,8},{10,11... | collective-permute-start | bytes 1622024 | tf_op jit(solution)/shard_map/ppermute | solution.py:673
  71.1 26.6 %collective-permute-start.29 = (f32[256,512]{1,0:T(8,128)S(1)}, f32[256,512]{1,0:T(8,128)S(1)}, u32[]{:S(2)}, u32[]{:S(2)}) collective-permute-start(f32[256,512]{1,0:T(8,128)S(1)} %stack.3.refs_3_.refs_0_), channel_id=1, source_target_pairs={{0,16},{4,20},{8,24},{12,28},{16,0},{20,4},{24,8},{28,12},{1,17},{... | collective-permute-start | bytes 1572872 | tf_op jit(solution)/shard_map/ppermute | solution.py:673
  73.9 32.9 %collective-permute-start.24 = (f32[512,512]{1,0:T(8,128)S(1)}, f32[512,512]{1,0:T(8,128)S(1)}, u32[]{:S(2)}, u32[]{:S(2)}) collective-permute-start(f32[512,512]{1,0:T(8,128)S(1)} %edge_add.1.refs_5_.refs_0_), channel_id=1, source_target_pairs={{0,2},{1,3},{2,0},{3,1},{4,6},{5,7},{6,4},{7,5},{8,10},{9,11},{10,... | collective-permute-start | bytes 3145736 | tf_op jit(solution)/shard_map/ppermute | solution.py:673
  80.8 11.6 %collective-permute-start.25 = (f32[136,512]{1,0:T(8,128)S(1)}, f32[136,512]{1,0:T(8,128)S(1)}, u32[]{:S(2)}, u32[]{:S(2)}) collective-permute-start(f32[136,512]{1,0:T(8,128)S(1)} %get-tuple-element.206), channel_id=1, source_target_pairs={{0,4},{4,0},{8,12},{12,8},{16,20},{20,16},{24,28},{28,24},{1,5},{5... | collective-permute-start | bytes 835592 | tf_op jit(solution)/shard_map/ppermute | solution.py:673
  92.5 12.8 %collective-permute-start.27 = (f32[72,512]{1,0:T(8,128)S(1)}, f32[72,512]{1,0:T(8,128)S(1)}, u32[]{:S(2)}, u32[]{:S(2)}) collective-permute-start(f32[72,512]{1,0:T(8,128)S(1)} %get-tuple-element.212), channel_id=1, source_target_pairs={{0,8},{4,12},{8,0},{12,4},{16,24},{20,28},{24,16},{28,20},{1,9},{5... | collective-permute-start | bytes 442376 | tf_op jit(solution)/shard_map/ppermute | solution.py:673
  97.8 12.4 %collective-permute-start.34 = (f32[128,512]{1,0:T(8,128)S(1)}, f32[128,512]{1,0:T(8,128)S(1)}, u32[]{:S(2)}, u32[]{:S(2)}) collective-permute-start(f32[128,512]{1,0:T(8,128)S(1)} %get-tuple-element.214.refs_2_.refs_0_), channel_id=1, source_target_pairs={{0,8},{4,12},{8,0},{12,4},{16,24},{20,28},{24,16},{28,20},{1,9},{5... | collective-permute-start | bytes 786440 | tf_op jit(solution)/shard_map/ppermute | solution.py:673
  98.4 20.8 %collective-permute-start.31 = (f32[128,512]{1,0:T(8,128)S(1)}, f32[128,512]{1,0:T(8,128)S(1)}, u32[]{:S(2)}, u32[]{:S(2)}) collective-permute-start(f32[128,512]{1,0:T(8,128)S(1)} %get-tuple-element.215.refs_0_), channel_id=1, source_target_pairs={{0,4},{4,0},{8,12},{12,8},{16,20},{20,16},{24,28},{28,24},{1,5},{5... | collective-permute-start | bytes 786440 | tf_op jit(solution)/shard_map/ppermute | solution.py:673
  103.7 13.2 %collective-permute-start.33 = (f32[64,512]{1,0:T(8,128)S(1)}, f32[64,512]{1,0:T(8,128)S(1)}, u32[]{:S(2)}, u32[]{:S(2)}) collective-permute-start(f32[64,512]{1,0:T(8,128)S(1)} %stack.4.refs_3_.refs_0_), channel_id=1, source_target_pairs={{0,16},{4,20},{8,24},{12,28},{16,0},{20,4},{24,8},{28,12},{1,17},{... | collective-permute-start | bytes 393224 | tf_op jit(solution)/shard_map/ppermute | solution.py:673
  105.3 13.9 %collective-permute-start.32 = (f32[72,512]{1,0:T(8,128)S(1)}, f32[72,512]{1,0:T(8,128)S(1)}, u32[]{:S(2)}, u32[]{:S(2)}) collective-permute-start(f32[72,512]{1,0:T(8,128)S(1)} %stack.5.refs_7_.refs_0_), channel_id=1, source_target_pairs={{0,16},{4,20},{8,24},{12,28},{16,0},{20,4},{24,8},{28,12},{1,17},{... | collective-permute-start | bytes 442376 | tf_op jit(solution)/shard_map/ppermute | solution.py:673
  107.3 14.1 %collective-permute-start.30 = (f32[512,512]{1,0:T(8,128)S(1)}, f32[512,512]{1,0:T(8,128)S(1)}, u32[]{:S(2)}, u32[]{:S(2)}) collective-permute-start(f32[512,512]{1,0:T(8,128)S(1)} %frames_back.1.refs_2_.refs_0_), channel_id=1, source_target_pairs={{0,1},{1,0},{2,3},{3,2},{4,5},{5,4},{6,7},{7,6},{8,9},{9,8},{10,11... | collective-permute-start | bytes 3145736 | tf_op jit(solution)/shard_map/ppermute | solution.py:673
  110.2 19.5 %collective-permute-start.41 = (f32[256,512]{1,0:T(8,128)S(1)}, f32[256,512]{1,0:T(8,128)S(1)}, u32[]{:S(2)}, u32[]{:S(2)}) collective-permute-start(f32[256,512]{1,0:T(8,128)S(1)} %join.4.refs_2_.refs_0_), channel_id=1, source_target_pairs={{0,4},{4,0},{8,12},{12,8},{16,20},{20,16},{24,28},{28,24},{1,5},{5... | collective-permute-start | bytes 1572872 | tf_op jit(solution)/shard_map/ppermute | solution.py:673
  119.4 16.6 %collective-permute-start.40 = (f32[256,512]{1,0:T(8,128)S(1)}, f32[256,512]{1,0:T(8,128)S(1)}, u32[]{:S(2)}, u32[]{:S(2)}) collective-permute-start(f32[256,512]{1,0:T(8,128)S(1)} %join.5.refs_2_.refs_0_), channel_id=1, source_target_pairs={{0,8},{4,12},{8,0},{12,4},{16,24},{20,28},{24,16},{28,20},{1,9},{5... | collective-permute-start | bytes 1572872 | tf_op jit(solution)/shard_map/ppermute | solution.py:673
  125.9 11.1 %collective-permute-start.39 = (f32[128,512]{1,0:T(8,128)S(1)}, f32[128,512]{1,0:T(8,128)S(1)}, u32[]{:S(2)}, u32[]{:S(2)}) collective-permute-start(f32[128,512]{1,0:T(8,128)S(1)} %join.7.refs_2_.refs_4_), channel_id=1, source_target_pairs={{0,4},{4,0},{8,12},{12,8},{16,20},{20,16},{24,28},{28,24},{1,5},{5... | collective-permute-start | bytes 786440 | tf_op jit(solution)/shard_map/ppermute | solution.py:673
  127.2 10.5 %collective-permute-start.37 = (f32[128,512]{1,0:T(8,128)S(1)}, f32[128,512]{1,0:T(8,128)S(1)}, u32[]{:S(2)}, u32[]{:S(2)}) collective-permute-start(f32[128,512]{1,0:T(8,128)S(1)} %join.6.refs_2_), channel_id=1, source_target_pairs={{0,4},{4,0},{8,12},{12,8},{16,20},{20,16},{24,28},{28,24},{1,5},{5... | collective-permute-start | bytes 786440 | tf_op jit(solution)/shard_map/ppermute | solution.py:673
  (19 other events, 132.4 us)
